TPU v7x, 32 devices: a whole 2x2x4 slice. The times are simulated.
32 devices in a mesh: depth: 16 (over z, y, core), cols: 2 (over x).
Axes of the slice: x: 2, y: 2, z: 4, core: 2. Of those that a mesh axis runs over, the one named last changes fastest.
Arguments:
- field: float32 [32, 2048, 256], P('depth', None, 'cols'), may hold values from -6 to 6
Outputs:
- picture: float32 [4, 2048, 256], P(None, 'depth', 'cols')
All inputs are finite; a program needn't handle non-finite values.
Results may differ from a plain program's by a relative error of at most 0.00002.
Values sent between devices are 32-bit elements; how exact they have to be, the bound alone decides.
No kernel may reach another device: no remote copies, remote signals or barrier semaphores. Data moves between devices by JAX's collectives and lax.ppermute only.
A program may use at most 128 MiB of HBM per device.

v0:
```python
import math

import jax
import jax.numpy as jnp
from jax import lax
from jax.sharding import PartitionSpec as P


def extended(shard, sides, width):
    for axis, dim in sides:
        size, length = (lax.axis_size(axis), shard.shape[dim])
        up = [(i, (i + 1) % size) for i in range(size - 1)]
        down = [(j, i) for i, j in up]
        last = lax.slice_in_dim(shard, length - width, length, axis=dim)
        initial = lax.slice_in_dim(shard, 0, width, axis=dim)
        before = lax.ppermute(last, axis, up)
        after = lax.ppermute(initial, axis, down)
        shard = jnp.concatenate([before, shard, after], axis=dim)
    return shard


def swapped(block, axis, bit):
    count = lax.axis_size(axis)
    route = []
    for low in range(count):
        high = low | 1 << bit
        if high != low and high < count:
            route += [(low, high), (high, low)]
    return lax.ppermute(block, axis, route)


def apply_taps(array_in, tap_list, which_axis):
    length = array_in.shape[which_axis] - 4
    result = tap_list[0] * lax.slice_in_dim(array_in, 0, length, axis=which_axis)
    for offset in range(1, 5):
        result = result + tap_list[offset] * lax.slice_in_dim(
            array_in, offset, offset + length, axis=which_axis
        )
    return result


def render_slab(padded):
    gauss_taps = [1.0 / 16, 4.0 / 16, 6.0 / 16, 4.0 / 16, 1.0 / 16]
    deriv_taps = [-1.0 / 8, -2.0 / 8, 0.0, 2.0 / 8, 1.0 / 8]
    smooth_x = apply_taps(padded, gauss_taps, 2)
    deriv_x = apply_taps(padded, deriv_taps, 2)
    smooth_xy = apply_taps(smooth_x, gauss_taps, 1)
    deriv_y = apply_taps(smooth_x, deriv_taps, 1)
    deriv_xy = apply_taps(deriv_x, gauss_taps, 1)
    smooth = apply_taps(smooth_xy, gauss_taps, 0)
    grad_z = 8.0 * apply_taps(smooth_xy, deriv_taps, 0)
    grad_y = 8.0 * apply_taps(deriv_y, gauss_taps, 0)
    grad_x = 8.0 * apply_taps(deriv_xy, gauss_taps, 0)
    scaled = 7.0 * smooth
    opacity = 0.6 * jax.nn.sigmoid(6.0 * scaled - 13.2)
    norm_len = jnp.sqrt(grad_x * grad_x + grad_y * grad_y + grad_z * grad_z + 1.0)
    half_len = math.sqrt(0.48 * 0.48 + 0.6 * 0.6 + 1.64 * 1.64)
    dot_light = (0.48 * grad_x + 0.6 * grad_y + 0.64 * grad_z) / norm_len
    dot_half = (0.48 * grad_x + 0.6 * grad_y + 1.64 * grad_z) / (half_len * norm_len)
    shading = 0.25 + 0.6 * jnp.maximum(dot_light, 0.0) + 0.35 * jnp.maximum(dot_half, 0.0) ** 8
    weight = opacity * shading
    colours = jnp.stack(
        [
            jax.nn.sigmoid(2.0 * scaled + 0.5) * weight,
            (0.5 + 0.4 * jnp.tanh(scaled)) * weight,
            jax.nn.sigmoid(-2.0 * scaled) * weight,
        ],
        0,
    )
    return (colours, opacity)


def composite_planes(colours, opacity):

    def step_fn(state_pair, plane):
        colour_sum, opacity_sum = state_pair
        plane_colour, plane_opacity = plane
        remain = 1.0 - opacity_sum
        return (
            (colour_sum + remain[None] * plane_colour, opacity_sum + remain * plane_opacity),
            None,
        )

    start = (
        jnp.zeros(colours.shape[0:1] + colours.shape[2:], jnp.float32),
        jnp.zeros(opacity.shape[1:], jnp.float32),
    )
    final_pair, unused = lax.scan(step_fn, start, (jnp.moveaxis(colours, 1, 0), opacity))
    return jnp.concatenate([final_pair[0], final_pair[1][None]], 0)


def over_op(front_part, back_part):
    return front_part + (1.0 - front_part[3:4]) * back_part


def local(field):
    widened = extended(field, (("depth", 0), ("cols", 2)), 2)
    padded = jnp.pad(widened, ((0, 0), (2, 2), (0, 0)))
    colours, opacity = render_slab(padded)
    partial_image = composite_planes(colours, opacity)
    groups = lax.axis_size("depth")
    position = lax.axis_index("depth")
    section_count = groups.bit_length() - 1
    block_rows = partial_image.shape[1] // groups
    current = partial_image.reshape(4, groups, block_rows, partial_image.shape[2])
    for bit_num in range(section_count):
        lower = current[:, 0::2]
        upper = current[:, 1::2]
        upper_side = position // 2**bit_num % 2 == 1
        kept = jnp.where(upper_side, upper, lower)
        outgoing = jnp.where(upper_side, lower, upper)
        incoming = swapped(outgoing, "depth", bit_num)
        front_part = jnp.where(upper_side, incoming, kept)
        back_part = jnp.where(upper_side, kept, incoming)
        current = over_op(front_part, back_part)
    return current[:, 0]


def solution(mesh):
    return jax.shard_map(
        local,
        mesh=mesh,
        in_specs=(P("depth", None, "cols"),),
        out_specs=P(None, "depth", "cols"),
        check_vma=False,
    )
```

profile of v0, /device:TPU:0, one launch (start us, length us, event | category | flops | bytes accessed | tf_op | source)
XLA Modules:
  0.0 230.2 jit_solution(4208217153971248496)
XLA Ops:
  1.9 2.5 %collective-permute-start = (f32[2,2048,128]{1,2,0:T(8,128)S(1)}, f32[2,2048,128]{1,2,0:T(8,128)S(1)}, u32[]{:S(2)}, u32[]{:S(2)}) collective-permute-start(f32[2,2048,128]{1,2,0:T(8,128)S(1)} %copy.4), channel_id=1, source_target_pairs={{0,2},{2,4},{4,6},{6,8},{8,10},{10,12},{12,14},{14,16},{16,18},{18... | collective-permute-start | bytes 6291464 | tf_op jit(solution)/shard_map/ppermute | solution.py:16
  8.1 4.4 %collective-permute-done.1 = f32[2,2048,128]{1,2,0:T(8,128)S(1)} collective-permute-done((f32[2,2048,128]{1,2,0:T(8,128)S(1)}, f32[2,2048,128]{1,2,0:T(8,128)S(1)}, u32[]{:S(2)}, u32[]{:S(2)}) %collective-permute-start.1) | collective-permute-done | bytes 2097184 | tf_op jit(solution)/shard_map/ppermute | solution.py:17
  13.8 3.4 %collective-permute-start.2 = (f32[6,2048,2]{1,2,0:T(2,128)S(1)}, f32[6,2048,2]{1,2,0:T(2,128)S(1)}, u32[]{:S(2)}, u32[]{:S(2)}) collective-permute-start(f32[6,2048,2]{1,2,0:T(2,128)S(1)} %get-tuple-element.88), channel_id=1, source_target_pairs={{0,1},{2,3},{4,5},{6,7},{8,9},{10,11},{12,13},{14,15},{16,17},{18,... | collective-permute-start | bytes 294920 | tf_op jit(solution)/shard_map/ppermute | solution.py:16
  19.4 4.3 %collective-permute-done.3 = f32[6,2048,2]{1,2,0:T(2,128)S(1)} collective-permute-done((f32[6,2048,2]{1,2,0:T(2,128)S(1)}, f32[6,2048,2]{1,2,0:T(2,128)S(1)}, u32[]{:S(2)}, u32[]{:S(2)}) %collective-permute-start.3) | collective-permute-done | bytes 98336 | tf_op jit(solution)/shard_map/ppermute | solution.py:17
  23.7 8.2 %select_maximum_fusion = f32[6,2052,132]{1,2,0:T(8,128)S(1)} fusion(f32[6,2048,2]{1,2,0:T(2,128)S(1)} %collective-permute-done.3, f32[6,2048,2]{1,2,0:T(2,128)S(1)} %collective-permute-done.2, f32[2,2048,128]{1,2,0:T(8,128)} %copy-done.5, f32[2,2048,128]{1,2,0:T(8,128)S(1)} %copy.4, f32[2,2048,128]{1,2,0:T(8,128)} %copy-done.4), kind=kLoop, calls=%fused_computation.9 | loop fusion | flops 19502208 | bytes 12988800 | tf_op jit(solution)/shard_map/concatenate | solution.py:18
  31.9 6.8 %multiply_add_fusion = (f32[6,2052,128]{1,2,0:T(8,128)S(1)}, f32[6,2052,128]{1,2,0:T(8,128)}) fusion(f32[6,2052,132]{1,2,0:T(8,128)S(1)} %select_maximum_fusion), kind=kLoop, calls=%fused_computation.15 | loop fusion | flops 26790912 | bytes 44126208 | tf_op jit(solution)/shard_map/add | solution.py:36
  38.8 20.1 %multiply_add_fusion.2 = (f32[6,2048,128]{1,2,0:T(8,128)}, f32[6,2048,128]{1,2,0:T(8,128)}) fusion(f32[6,2052,128]{1,2,0:T(8,128)} %get-tuple-element.85), kind=kLoop, calls=%fused_computation.28 | loop fusion | flops 26738688 | bytes 44040192 | tf_op jit(solution)/shard_map/add | solution.py:36
  58.8 6.8 %divide_multiply_fusion = (f32[2,2048,128]{1,2,0:T(8,128)}, f32[2,2048,128]{1,2,0:T(8,128)S(1)}) fusion(f32[6,2048,128]{1,2,0:T(8,128)} %get-tuple-element.87), kind=kLoop, calls=%fused_computation.55 | loop fusion | flops 7864320 | bytes 14680064 | tf_op jit(solution)/shard_map/mul | solution.py:55
  65.6 8.3 %fusion.3 = f32[6,2048,128]{1,2,0:T(8,128)} fusion(f32[6,2052,128]{1,2,0:T(8,128)S(1)} %get-tuple-element.84), kind=kLoop, calls=%fused_computation.18 | loop fusion | flops 14155776 | bytes 37748736 | tf_op jit(solution)/shard_map/add | solution.py:36
  73.9 10.7 %multiply_bitcast_fusion.2 = (f32[1,2,2048,128]{2,3,1,0:T(8,128)S(1)}, f32[2,2048,128]{1,2,0:T(8,128)S(1)}) fusion(f32[2,2048,128]{1,2,0:T(8,128)S(1)} %get-tuple-element.79, f32[6,2048,128]{1,2,0:T(8,128)S(1)} %bitcast.33, f32[6,2048,128]{1,2,0:T(8,128)} %get-tuple-element.86, f32[6,2048,128]{1,2,0:T(8,128)} %fusion.3), kind=kLoop, calls=%fused_computation.53 | loop fusion | flops 35651584 | bytes 37748736 | tf_op jit(solution)/shard_map/stack | solution.py:62
  85.4 3.1 %maximum_bitcast_fusion = f32[2,3,2048,128]{2,3,0,1:T(8,128)} fusion(f32[1,2,2048,128]{2,3,1,0:T(8,128)S(1)} %get-tuple-element.91, f32[1,2,2048,128]{2,3,1,0:T(8,128)S(1)} %get-tuple-element.90, f32[1,2,2048,128]{2,3,1,0:T(8,128)S(1)} %get-tuple-element.80), kind=kLoop, calls=%fused_computation.27 | loop fusion | flops 3145728 | bytes 12582912 | tf_op jit(solution)/shard_map/transpose | solution.py:88
  88.5 27.6 %while.13 = (s32[]{:T(128)}, f32[3,2048,128]{2,1,0:T(8,128)}, f32[2048,128]{1,0:T(8,128)S(1)}, f32[2,3,2048,128]{2,3,0,1:T(8,128)}, f32[2,2048,128]{1,2,0:T(8,128)}, /*index=5*/s32[]{:T(128)}, s32[]{:T(128)}) while((s32[]{:T(128)}, f32[3,2048,128]{2,1,0:T(8,128)}, f32[2048,128]{1,0:T(8,128)S(1)}, f32[2,3,2048,128]{2,3,0,1:T(8,128)}, ...), condition=%wide.region_1.2_spmd.clone, body=%wide.region_0.1_spmd.clone.sunk | while | flops 3407875 | bytes 39846036 | solution.py:88
  95.1 2.4 %copy.13 = f32[1,3,2048,128]{3,2,1,0:T(8,128)} copy(f32[1,3,2048,128]{2,3,0,1:T(8,128)S(1)} %constant_dynamic-slice_fusion.4) | data formatting | bytes 6291456 | tf_op jit(solution)/shard_map/while/body/jit(dynamic_index_in_dim)/dynamic_slice | solution.py:88
  97.5 4.3 %fusion.22 = f32[3,2048,128]{2,1,0:T(8,128)} fusion(f32[1,3,2048,128]{3,2,1,0:T(8,128)} %copy.13, f32[3,2048,128]{2,1,0:T(8,128)} %get-tuple-element.135, f32[2048,128]{1,0:T(8,128)} %get-tuple-element.125, pred[]{:T(512)S(6)} %compare.33), kind=kLoop, calls=%fused_computation.1.clone.1 | loop fusion | flops 2359296 | bytes 10485761 | tf_op jit(solution)/shard_map/while/body/eval_jaxpr/add | solution.py:80
  108.4 2.4 %copy.13 = f32[1,3,2048,128]{3,2,1,0:T(8,128)} copy(f32[1,3,2048,128]{2,3,0,1:T(8,128)S(1)} %constant_dynamic-slice_fusion.4) | data formatting | bytes 6291456 | tf_op jit(solution)/shard_map/while/body/jit(dynamic_index_in_dim)/dynamic_slice | solution.py:88
  110.9 5.2 %fusion.22 = f32[3,2048,128]{2,1,0:T(8,128)} fusion(f32[1,3,2048,128]{3,2,1,0:T(8,128)} %copy.13, f32[3,2048,128]{2,1,0:T(8,128)} %get-tuple-element.135, f32[2048,128]{1,0:T(8,128)} %get-tuple-element.125, pred[]{:T(512)S(6)} %compare.33), kind=kLoop, calls=%fused_computation.1.clone.1 | loop fusion | flops 2359296 | bytes 10485761 | tf_op jit(solution)/shard_map/while/body/eval_jaxpr/add | solution.py:80
  120.9 39.1 %collective-permute-start.4 = (f32[4,8,128,128]{3,2,1,0:T(8,128)}, f32[4,8,128,128]{3,2,1,0:T(8,128)S(1)}, u32[]{:S(2)}, u32[]{:S(2)}) collective-permute-start(f32[4,8,128,128]{3,2,1,0:T(8,128)} %slice_select_fusion.1), channel_id=1, source_target_pairs={{0,2},{2,0},{4,6},{6,4},{8,10},{10,8},{12,14},{14,12},{16,18},{18,... | collective-permute-start | bytes 6291464 | tf_op jit(solution)/shard_map/ppermute | solution.py:29
  160.0 4.0 %collective-permute-done.4 = f32[4,8,128,128]{3,2,1,0:T(8,128)S(1)} collective-permute-done((f32[4,8,128,128]{3,2,1,0:T(8,128)}, f32[4,8,128,128]{3,2,1,0:T(8,128)S(1)}, u32[]{:S(2)}, u32[]{:S(2)}) %collective-permute-start.4) | collective-permute-done | bytes 2097184 | tf_op jit(solution)/shard_map/ppermute | solution.py:29
  164.0 3.6 %broadcast_select_fusion = f32[4,8,128,128]{3,2,1,0:T(8,128)S(1)} fusion(f32[4,8,128,128]{3,2,1,0:T(8,128)S(1)} %collective-permute-done.4, pred[]{:T(512)S(6)} %eq.20, f32[4,16,128,128]{3,2,1,0:T(8,128)} %copy-done), kind=kLoop, calls=%fused_computation.60 | loop fusion | flops 1048576 | bytes 8388609 | tf_op jit(solution)/shard_map/jit(_where)/select_n | solution.py:113
  171.6 4.2 %collective-permute-start.5 = (f32[4,4,128,128]{3,2,1,0:T(8,128)}, f32[4,4,128,128]{3,2,1,0:T(8,128)S(1)}, u32[]{:S(2)}, u32[]{:S(2)}) collective-permute-start(f32[4,4,128,128]{3,2,1,0:T(8,128)} %slice_select_fusion.3), channel_id=1, source_target_pairs={{0,4},{4,0},{2,6},{6,2},{8,12},{12,8},{10,14},{14,10},{16,20},{20,... | collective-permute-start | bytes 3145736 | tf_op jit(solution)/shard_map/ppermute | solution.py:29
  175.8 23.7 %collective-permute-done.5 = f32[4,4,128,128]{3,2,1,0:T(8,128)S(1)} collective-permute-done((f32[4,4,128,128]{3,2,1,0:T(8,128)}, f32[4,4,128,128]{3,2,1,0:T(8,128)S(1)}, u32[]{:S(2)}, u32[]{:S(2)}) %collective-permute-start.5) | collective-permute-done | bytes 1048608 | tf_op jit(solution)/shard_map/ppermute | solution.py:29
  203.7 11.9 %collective-permute-done.6 = f32[4,2,128,128]{3,2,1,0:T(8,128)S(1)} collective-permute-done((f32[4,2,128,128]{3,2,1,0:T(8,128)S(1)}, f32[4,2,128,128]{3,2,1,0:T(8,128)S(1)}, u32[]{:S(2)}, u32[]{:S(2)}) %collective-permute-start.6) | collective-permute-done | bytes 524320 | tf_op jit(solution)/shard_map/ppermute | solution.py:29
  215.8 2.7 %collective-permute-start.7 = (f32[4,1,128,128]{3,2,1,0:T(8,128)S(1)}, f32[4,1,128,128]{3,2,1,0:T(8,128)S(1)}, u32[]{:S(2)}, u32[]{:S(2)}) collective-permute-start(f32[4,1,128,128]{3,2,1,0:T(8,128)S(1)} %slice_select_fusion.7), channel_id=1, source_target_pairs={{0,16},{16,0},{2,18},{18,2},{4,20},{20,4},{6,22},{22,6},{8,24},{24... | collective-permute-start | bytes 786440 | tf_op jit(solution)/shard_map/ppermute | solution.py:29
  218.4 10.9 %collective-permute-done.7 = f32[4,1,128,128]{3,2,1,0:T(8,128)S(1)} collective-permute-done((f32[4,1,128,128]{3,2,1,0:T(8,128)S(1)}, f32[4,1,128,128]{3,2,1,0:T(8,128)S(1)}, u32[]{:S(2)}, u32[]{:S(2)}) %collective-permute-start.7) | collective-permute-done | bytes 262176 | tf_op jit(solution)/shard_map/ppermute | solution.py:29
  (59 shorter events, 37.1 us)
Async XLA Ops:
  1.9 6.1 %collective-permute-start = (f32[2,2048,128]{1,2,0:T(8,128)S(1)}, f32[2,2048,128]{1,2,0:T(8,128)S(1)}, u32[]{:S(2)}, u32[]{:S(2)}) collective-permute-start(f32[2,2048,128]{1,2,0:T(8,128)S(1)} %copy.4), channel_id=1, source_target_pairs={{0,2},{2,4},{4,6},{6,8},{8,10},{10,12},{12,14},{14,16},{16,18},{18... | collective-permute-start | bytes 6291464 | tf_op jit(solution)/shard_map/ppermute | solution.py:16
  4.4 8.1 %collective-permute-start.1 = (f32[2,2048,128]{1,2,0:T(8,128)S(1)}, f32[2,2048,128]{1,2,0:T(8,128)S(1)}, u32[]{:S(2)}, u32[]{:S(2)}) collective-permute-start(f32[2,2048,128]{1,2,0:T(8,128)S(1)} %copy.4), channel_id=1, source_target_pairs={{2,0},{4,2},{6,4},{8,6},{10,8},{12,10},{14,12},{16,14},{18,16},{20... | collective-permute-start | bytes 6291464 | tf_op jit(solution)/shard_map/ppermute | solution.py:17
  8.1 4.5 %copy-start.4 = (f32[2,2048,128]{1,2,0:T(8,128)}, f32[2,2048,128]{1,2,0:T(8,128)S(1)}, u32[]{:S(2)}) copy-start(f32[2,2048,128]{1,2,0:T(8,128)S(1)} %collective-permute-done) | copy-start | bytes 6291460
  12.5 1.3 copy-start.5
  13.8 5.6 %collective-permute-start.2 = (f32[6,2048,2]{1,2,0:T(2,128)S(1)}, f32[6,2048,2]{1,2,0:T(2,128)S(1)}, u32[]{:S(2)}, u32[]{:S(2)}) collective-permute-start(f32[6,2048,2]{1,2,0:T(2,128)S(1)} %get-tuple-element.88), channel_id=1, source_target_pairs={{0,1},{2,3},{4,5},{6,7},{8,9},{10,11},{12,13},{14,15},{16,17},{18,... | collective-permute-start | bytes 294920 | tf_op jit(solution)/shard_map/ppermute | solution.py:16
  17.2 6.5 %collective-permute-start.3 = (f32[6,2048,2]{1,2,0:T(2,128)S(1)}, f32[6,2048,2]{1,2,0:T(2,128)S(1)}, u32[]{:S(2)}, u32[]{:S(2)}) collective-permute-start(f32[6,2048,2]{1,2,0:T(2,128)S(1)} %get-tuple-element.89), channel_id=1, source_target_pairs={{1,0},{3,2},{5,4},{7,6},{9,8},{11,10},{13,12},{15,14},{17,16},{19,... | collective-permute-start | bytes 294920 | tf_op jit(solution)/shard_map/ppermute | solution.py:17
  65.6 8.3 %slice-start = ((s8[6291456]{0:T(1024)(128)(4,1)}), s8[4194304]{0:T(1024)(128)(4,1)S(1)}, s32[]{:S(2)}) async-start(s8[6291456]{0:T(1024)(128)(4,1)} %bitcast.32), calls=%async_computation | async-start | bytes 8388608
  65.6 8.3 %slice-start.1 = ((s8[6291456]{0:T(1024)(128)(4,1)}), s8[2097152]{0:T(1024)(128)(4,1)S(1)}, s32[]{:S(2)}) async-start(s8[6291456]{0:T(1024)(128)(4,1)} %bitcast.32), calls=%async_computation.1 | async-start | bytes 4194304
  92.0 1.0 copy-start.2
  97.5 4.3 %copy-start.3 = (f32[2048,128]{1,0:T(8,128)S(1)}, f32[2048,128]{1,0:T(8,128)}, u32[]{:S(2)}) copy-start(f32[2048,128]{1,0:T(8,128)} %copy-done.2) | copy-start | bytes 3145732 | tf_op jit(solution)/shard_map/while
  105.4 1.0 copy-start.2
  110.9 5.2 %copy-start.3 = (f32[2048,128]{1,0:T(8,128)S(1)}, f32[2048,128]{1,0:T(8,128)}, u32[]{:S(2)}) copy-start(f32[2048,128]{1,0:T(8,128)} %copy-done.2) | copy-start | bytes 3145732 | tf_op jit(solution)/shard_map/while
  118.3 2.6 %copy-start = (f32[4,16,128,128]{3,2,1,0:T(8,128)}, f32[4,16,128,128]{3,2,1,0:T(8,128)S(1)}, u32[]{:S(2)}) copy-start(f32[4,16,128,128]{3,2,1,0:T(8,128)S(1)} %pad_maximum_fusion) | copy-start | bytes 12582916
  120.9 43.1 %collective-permute-start.4 = (f32[4,8,128,128]{3,2,1,0:T(8,128)}, f32[4,8,128,128]{3,2,1,0:T(8,128)S(1)}, u32[]{:S(2)}, u32[]{:S(2)}) collective-permute-start(f32[4,8,128,128]{3,2,1,0:T(8,128)} %slice_select_fusion.1), channel_id=1, source_target_pairs={{0,2},{2,0},{4,6},{6,4},{8,10},{10,8},{12,14},{14,12},{16,18},{18,... | collective-permute-start | bytes 6291464 | tf_op jit(solution)/shard_map/ppermute | solution.py:29
  164.0 3.6 %copy-start.6 = (f32[4,8,128,128]{3,2,1,0:T(8,128)}, f32[4,8,128,128]{3,2,1,0:T(8,128)S(1)}, u32[]{:S(2)}) copy-start(f32[4,8,128,128]{3,2,1,0:T(8,128)S(1)} %collective-permute-done.4) | copy-start | bytes 6291460
  164.0 4.2 %copy-start.1 = (f32[4,16,128,128]{3,2,1,0:T(8,128)S(1)}, f32[4,16,128,128]{3,2,1,0:T(8,128)}, u32[]{:S(2)}) copy-start(f32[4,16,128,128]{3,2,1,0:T(8,128)} %copy-done) | copy-start | bytes 12582916
  171.6 27.8 %collective-permute-start.5 = (f32[4,4,128,128]{3,2,1,0:T(8,128)}, f32[4,4,128,128]{3,2,1,0:T(8,128)S(1)}, u32[]{:S(2)}, u32[]{:S(2)}) collective-permute-start(f32[4,4,128,128]{3,2,1,0:T(8,128)} %slice_select_fusion.3), channel_id=1, source_target_pairs={{0,4},{4,0},{2,6},{6,2},{8,12},{12,8},{10,14},{14,10},{16,20},{20,... | collective-permute-start | bytes 3145736 | tf_op jit(solution)/shard_map/ppermute | solution.py:29
  199.4 1.0 copy-start.7
  202.0 13.5 %collective-permute-start.6 = (f32[4,2,128,128]{3,2,1,0:T(8,128)S(1)}, f32[4,2,128,128]{3,2,1,0:T(8,128)S(1)}, u32[]{:S(2)}, u32[]{:S(2)}) collective-permute-start(f32[4,2,128,128]{3,2,1,0:T(8,128)S(1)} %slice_select_fusion.5), channel_id=1, source_target_pairs={{0,8},{8,0},{2,10},{10,2},{4,12},{12,4},{6,14},{14,6},{16,24},{24,... | collective-permute-start | bytes 1572872 | tf_op jit(solution)/shard_map/ppermute | solution.py:29
  215.8 13.5 %collective-permute-start.7 = (f32[4,1,128,128]{3,2,1,0:T(8,128)S(1)}, f32[4,1,128,128]{3,2,1,0:T(8,128)S(1)}, u32[]{:S(2)}, u32[]{:S(2)}) collective-permute-start(f32[4,1,128,128]{3,2,1,0:T(8,128)S(1)} %slice_select_fusion.7), channel_id=1, source_target_pairs={{0,16},{16,0},{2,18},{18,2},{4,20},{20,4},{6,22},{22,6},{8,24},{24... | collective-permute-start | bytes 786440 | tf_op jit(solution)/shard_map/ppermute | solution.py:29
where the time goes:
time: 231 us; the launch traced here: 230 us
  other arithmetic  91.8 us (40%)
  waiting for transfers between devices  62.3 us (27%)
  starting transfers between devices  56 us (24%)
  local copies, waits for them, and re-layouts  19.7 us (9%)
    ppermute x4, waiting for transfers between devices, swapped(): return lax.ppermute(block, axis, route)  50.4 us
    ppermute x4, starting transfers between devices, swapped(): return lax.ppermute(block, axis, route)  47.6 us
    add x3, other arithmetic, apply_taps(): result + tap_list[offset] * lax.slice_in_dim(array_in, offset, offset + l...  35.2 us
    dynamic_slice x8, local copies, waits for them, and re-layouts, composite_planes(): lax.scan(step_fn, start, (jnp.moveaxis(colours, 1, 0), opacity))  12.2 us
    another operation x2, other arithmetic, render_slab(): jnp.stack([jax.nn.sigmoid(2.0 * scaled + 0.5) * weight, (0.5 + 0.4 * jnp....  11.5 us
    add x2, other arithmetic, step_fn(): colour_sum + remain[None] * plane_colour  9.56 us
    ppermute x2, waiting for transfers between devices, extended(): after = lax.ppermute(initial, axis, down)  8.74 us
    concatenate x1, other arithmetic, extended(): shard = jnp.concatenate([before, shard, after], axis=dim)  8.18 us
  transfers between devices with their start and end apart: 8, of which 8 were waited for; matrix products, arithmetic and copies ran while one was open for 0% of the time, Pallas kernels for 0%

commit v1 on v0

v1 whole, which is shorter than its diff:
```python
import functools
import math

import jax
import jax.numpy as jnp
import numpy as np
from jax import lax
from jax.experimental import pallas as pl
from jax.experimental.pallas import tpu as pltpu
from jax.sharding import PartitionSpec as P

GAUSS = (1.0, 4.0, 6.0, 4.0, 1.0)
DERIV = (-1.0, -2.0, 0.0, 2.0, 1.0)
SCALE = 7.0 / 4096.0
ONE = 49.0 / 256.0
HALF_LEN = math.sqrt(0.48 * 0.48 + 0.6 * 0.6 + 1.64 * 1.64)
SPEC = 0.35 / HALF_LEN**8
LOG2E = 1.0 / math.log(2.0)
LANES = 128
TILE = 16


def column_weights(width):
    body = np.zeros((width, 2 * width), np.float32)
    halo = np.zeros((4, 2 * width), np.float32)
    for out in range(width):
        for k in range(5):
            col = out - 2 + k
            for part, taps in enumerate((GAUSS, DERIV)):
                value = SCALE * taps[k]
                if 0 <= col < width:
                    body[col, part * width + out] = value
                else:
                    halo[col + 2 if col < 0 else col - width + 2, part * width + out] = value
    side = np.zeros((LANES, 2 * width), np.float32)
    for row in range(24):
        side[row] = halo[row % 4]
    return np.concatenate([body, body, body, side], 0).astype(jnp.bfloat16)


def three_parts(x):
    hi = x.astype(jnp.bfloat16)
    rest = x - hi.astype(jnp.float32)
    mid = rest.astype(jnp.bfloat16)
    lo = (rest - mid.astype(jnp.float32)).astype(jnp.bfloat16)
    return hi, mid, lo


def filter_columns(block, plane, rows, weights, sx, dx, slot):
    width = block.shape[2]
    hi, mid, lo = three_parts(block[plane, 0:rows, :])
    sides = [part.astype(jnp.float32) for part in three_parts(block[plane, rows : rows + 8, :])]
    lanes_first = jnp.transpose(jnp.concatenate(sides, 0))
    lane = lax.broadcasted_iota(jnp.int32, lanes_first.shape, 1)
    pieces = []
    for b in range(-(-rows // LANES)):
        mine = jnp.where(lane % 8 // 4 == b, lanes_first, 0.0)
        pieces.append(mine[0 : min(LANES, rows - b * LANES)])
    side = jnp.concatenate(pieces, 0)
    side = jnp.concatenate([side, jnp.zeros((rows, LANES - side.shape[1]), jnp.float32)], 1)
    row = jnp.concatenate([hi, mid, lo, side.astype(jnp.bfloat16)], 1)
    both = jnp.dot(row, weights[...], preferred_element_type=jnp.float32)
    sx[slot] = both[:, :width]
    dx[slot] = both[:, width:]


def gauss_rows(a, b, c, d, e):
    return (a + e) + 4.0 * (b + d) + 6.0 * c


def shade(t, gx, gy, gz, state):
    v_sum, vt_sum, vu_sum, cover = state
    opacity = 0.6 * pl.reciprocal(1.0 + jnp.exp2(jnp.minimum(13.2 * LOG2E - (6.0 * LOG2E) * t, 126.0)))
    tanh_t = jnp.tanh(t)
    tanh_u = jnp.tanh(t + 0.25)
    light = 0.48 * gx + 0.6 * gy + 0.64 * gz
    inv = lax.rsqrt(gx * gx + gy * gy + gz * gz + ONE)
    diffuse = jnp.maximum(light, 0.0) * inv
    half = jnp.maximum(light + gz, 0.0) * inv
    half = half * half
    half = half * half
    shading = 0.25 + 0.6 * diffuse + SPEC * (half * half)
    part = (1.0 - cover) * opacity
    value = part * shading
    return v_sum + value, vt_sum + value * tanh_t, vu_sum + value * tanh_u, cover + part


def render(sx, dx, first, count):
    def rows_of(ref, slot):
        return [ref[slot, pl.ds(first + k, TILE), :] for k in range(5)]

    zero = jnp.zeros((TILE, sx.shape[2]), jnp.float32)
    state = (zero, zero, zero, zero)
    chains = [[None] * 4 for _ in range(3)]
    for index in range(count + 4):
        a, b, c, d, e = rows_of(sx, index)
        inputs = [gauss_rows(a, b, c, d, e), (e - a) + 2.0 * (d - b), gauss_rows(*rows_of(dx, index))]
        totals, diff = [], None
        for which, (chain, x) in enumerate(zip(chains, inputs)):
            for level in range(4):
                before, chain[level] = chain[level], x
                if before is None:
                    x = None
                    break
                if which == 0 and level == 3:
                    diff = x - before
                x = x + before
            totals.append(x)
        if index >= 4:
            state = shade(totals[0], totals[2], totals[1], diff, state)
    return state


def over(front, back):
    rest = 1.0 - front[3]
    return tuple(f + rest * b for f, b in zip(front, back))


def render_kernel(size, last, info, weights, *refs):
    blocks, refs = refs[:size], refs[size:]
    if last:
        boundary, other, image, sx, dx = refs
    else:
        image, sx, dx = refs
    depth, rows = blocks[0].shape[0], sx.shape[1]
    planes = depth * size
    extra = 4 if last else 0
    pos, front = info[0], info[1]
    start = 2 * front + extra * (1 - front)
    empty = (1 - front) * (planes + extra)
    sx[pl.ds(empty, 2)] = jnp.zeros((2,) + sx.shape[1:], jnp.float32)
    dx[pl.ds(empty, 2)] = jnp.zeros((2,) + dx.shape[1:], jnp.float32)
    for step in range(size):
        for plane in range(depth):
            slot = (pos ^ step) * depth + plane + start
            filter_columns(blocks[step], plane, rows, weights, sx, dx, slot)
    for plane in range(extra):
        slot = (planes + 2) * front + plane
        filter_columns(boundary, plane, rows, weights, sx, dx, slot)

    @pl.loop(0, image.shape[1] // TILE)
    def _(tile):
        first = pl.multiple_of(tile * TILE, TILE)
        total = render(sx, dx, first, planes - 2 + extra)
        if last:
            is_front = front == 1
            rest = tuple(other[channel, pl.ds(first, TILE), :] for channel in range(4))
            ahead = tuple(jnp.where(is_front, m, r) for m, r in zip(total, rest))
            behind = tuple(jnp.where(is_front, r, m) for m, r in zip(total, rest))
            v_sum, vt_sum, vu_sum, cover = over(ahead, behind)
            total = (0.5 * (v_sum + vu_sum), 0.5 * v_sum + 0.4 * vt_sum, 0.5 * (v_sum - vt_sum), cover)
        for channel in range(4):
            image[channel, pl.ds(first, TILE), :] = total[channel]


def pack_kernel(size, rows, info, field, sides, *refs):
    outs, padded = refs[:-1], refs[-1]
    depth, height, width = field.shape
    own = rows - 8
    pos, front = info[0], info[1]
    padded[:, 0:8, :] = jnp.zeros((depth, 8, width), jnp.float32)
    padded[:, 8 + height : 16 + height, :] = jnp.zeros((depth, 8, width), jnp.float32)
    padded[:, 8 : 8 + height, :] = field[...]
    for chunk in range(2):
        base = (1 - front) * size if chunk == 0 else front * size
        for step in range(size):
            out = outs[chunk * size + step]
            target = base + (pos ^ step)
            start = pl.multiple_of(target * own, 8)
            for plane in range(depth):
                out[plane, 0:rows, :] = padded[plane, pl.ds(start + 6, rows), :]
                out[plane, rows : rows + 8, :] = sides[target, plane]


def pick_kernel(size, info, *refs):
    blocks, out, sem = refs[:size], refs[size], refs[size + 1]
    depth = blocks[0].shape[0]
    pos, front = info[0], info[1]
    count = 4 // depth
    for part in range(count):
        wanted = pos ^ (front * (size - count) + part)
        for step in range(size):

            @pl.when(wanted == step)
            def _():
                pltpu.make_async_copy(blocks[step], out.at[pl.ds(part * depth, depth)], sem.at[part]).start()

    for part in range(count):
        place = out.at[pl.ds(part * depth, depth)]
        pltpu.make_async_copy(blocks[0], place, sem.at[part]).wait()


SMEM = pl.BlockSpec(memory_space=pltpu.SMEM)
VMEM = pl.BlockSpec(memory_space=pltpu.VMEM)
ANY = pl.BlockSpec(memory_space=pl.ANY)
PARAMS = pltpu.CompilerParams(vmem_limit_bytes=48 * 1024 * 1024)


def cost(flops, size):
    return pl.CostEstimate(flops=flops, bytes_accessed=size, transcendentals=0)


def side_columns(field, own, rows):
    groups = lax.axis_size("cols")
    up = [(i, i + 1) for i in range(groups - 1)]
    down = [(j, i) for i, j in up]
    width = field.shape[2]
    before = lax.ppermute(jnp.transpose(field[:, :, width - 2 :], (2, 0, 1)), "cols", up)
    after = lax.ppermute(jnp.transpose(field[:, :, :2], (2, 0, 1)), "cols", down)
    both = jnp.concatenate([before, after], 0)
    depth, height = both.shape[1:]
    pieces = -(-rows // LANES)
    span = pieces * LANES
    count = height // own
    both = jnp.pad(both, ((0, 0), (0, 0), (2, span)))
    cut = jnp.stack([both[:, :, own * j : own * j + span] for j in range(count)], 0)
    cut = cut.reshape(count, 4, depth, pieces, LANES).transpose(0, 2, 3, 1, 4)
    cut = cut.reshape(count, depth, 4 * pieces, LANES)
    return jnp.pad(cut, ((0, 0), (0, 0), (0, 8 - 4 * pieces), (0, 0)))


def local(field):
    groups = lax.axis_size("depth")
    size = groups // 2
    depth, height, width = field.shape
    own = height // groups
    rows = own + 8
    me = lax.axis_index("depth")
    info = jnp.stack([me % size, 1 - me // size]).astype(jnp.int32)
    weights = jnp.asarray(column_weights(width))
    f32 = jnp.float32
    block = jax.ShapeDtypeStruct((depth, rows + 8, width), f32)
    image = jax.ShapeDtypeStruct((4, own, width), f32)

    sides = side_columns(field, own, rows)
    blocks = pl.pallas_call(
        functools.partial(pack_kernel, size, rows),
        out_shape=(block,) * (2 * size),
        in_specs=[SMEM, VMEM, VMEM],
        out_specs=(VMEM,) * (2 * size),
        scratch_shapes=[pltpu.VMEM((depth, height + 16, width), f32)],
        compiler_params=PARAMS,
        name="pack_blocks",
    )(info, field, sides)

    def render_call(last):
        count = depth * size + (6 if last else 2)
        return pl.pallas_call(
            functools.partial(render_kernel, size, last),
            out_shape=image,
            in_specs=[SMEM] + [VMEM] * (size + (3 if last else 1)),
            out_specs=VMEM,
            scratch_shapes=[pltpu.VMEM((count, rows, width), f32)] * 2,
            compiler_params=PARAMS,
            cost_estimate=cost(5_000_000_000, 2_000_000),
            name="render_last" if last else "render_first",
        )

    pick = pl.pallas_call(
        functools.partial(pick_kernel, size),
        out_shape=jax.ShapeDtypeStruct((4, rows + 8, width), f32),
        in_specs=[SMEM] + [ANY] * size,
        out_specs=ANY,
        scratch_shapes=[pltpu.SemaphoreType.DMA((4 // depth,))],
        name="pick_boundary",
    )

    def swap(x, bits):
        return lax.ppermute(x, "depth", [(i, i ^ bits) for i in range(groups)])

    def gathered(mine):
        return [mine[0]] + [swap(mine[step], step) for step in range(1, size)]

    theirs = gathered(blocks[size:])
    boundary = swap(pick(info, *theirs), size)
    image_part = swap(render_call(False)(info, weights, *theirs), size)
    mine = gathered(blocks[:size])
    return render_call(True)(info, weights, *mine, boundary, image_part)


def solution(mesh):
    return jax.shard_map(
        local,
        mesh=mesh,
        in_specs=(P("depth", None, "cols"),),
        out_specs=P(None, "depth", "cols"),
        check_vma=False,
    )
```

time: 231 us -> 90.1 us (0.39)
  other arithmetic: 91.8 us -> 1.32 us
  waiting for transfers between devices: 62.3 us -> 26.5 us
  starting transfers between devices: 56 us -> 24.5 us
  Pallas kernels: 0 us -> 20.8 us
  local copies, waits for them, and re-layouts: 19.7 us -> 16.5 us
    add x10 -> x0, other arithmetic: 52.3 us -> none  [the longest x3 35.2 us: apply_taps(): result + tap_list[offset] * lax.slice_in_dim(array_in, offset, offset + l...]
    ppermute x8 -> x18, waiting for transfers between devices: 62.3 us -> 26.5 us  [the longest x16 22.1 us: swap(): return lax.ppermute(x, 'depth', [(i, i ^ bits) for i in range(groups)])]
    ppermute x8 -> x18, starting transfers between devices: 56 us -> 24.5 us  [the longest x16 18.2 us: swap(): return lax.ppermute(x, 'depth', [(i, i ^ bits) for i in range(groups)])]
    pallas_call x0 -> x4, Pallas kernels: none -> 20.8 us  [the longest x1 10.7 us: local(): boundary = swap(pick(info, *theirs), size)]
    dynamic_slice x8 -> x0, local copies, waits for them, and re-layouts: 12.2 us -> none  [composite_planes(): lax.scan(step_fn, start, (jnp.moveaxis(colours, 1, 0), opacity))]
    another operation x2 -> x1, other arithmetic: 11.5 us -> 0.08 us  [local(): info = jnp.stack([me % size, 1 - me // size]).astype(jnp.int32)]
    concatenate x2 -> x1, other arithmetic: 10.4 us -> 0.03 us  [side_columns(): both = jnp.concatenate([before, after], 0)]
    mul x5 -> x0, other arithmetic: 6.85 us -> none  [the longest x1 6.77 us: render_slab(): opacity = 0.6 * jax.nn.sigmoid(6.0 * scaled - 13.2)]
  transfers between devices with their start and end apart: 8 -> 18, of which waited for: 8 -> 8; matrix products, arithmetic and copies ran while one was open for 0% -> 3% of each run, Pallas kernels for 0% -> 16%
where the time goes in v1:
time: 90.1 us; the launch traced here: 89.7 us
  waiting for transfers between devices  26.5 us (29%)
  starting transfers between devices  24.5 us (27%)
  Pallas kernels  20.8 us (23%)
  local copies, waits for them, and re-layouts  16.5 us (18%)
  other arithmetic  1.32 us (1%)
    ppermute x16, waiting for transfers between devices, swap(): return lax.ppermute(x, 'depth', [(i, i ^ bits) for i in range(groups)])  22.1 us
    ppermute x16, starting transfers between devices, swap(): return lax.ppermute(x, 'depth', [(i, i ^ bits) for i in range(groups)])  18.2 us
    unnamed x45, local copies, waits for them, and re-layouts  12.1 us
    pallas_call x1, Pallas kernels, local(): boundary = swap(pick(info, *theirs), size)  10.7 us
    pallas_call x1, Pallas kernels, local(): return render_call(True)(info, weights, *mine, boundary, image_part)  5.38 us
    ppermute x1, starting transfers between devices, side_columns(): lax.ppermute(jnp.transpose(field[:, :, width - 2:], (2, 0, 1)), 'cols', up)  4.98 us
    ppermute x1, waiting for transfers between devices, side_columns(): lax.ppermute(jnp.transpose(field[:, :, :2], (2, 0, 1)), 'cols', down)  4.37 us
    slice x1, local copies, waits for them, and re-layouts, side_columns(): field[:, :, width - 2:]  4.24 us
  transfers between devices with their start and end apart: 18, of which 8 were waited for; matrix products, arithmetic and copies ran while one was open for 3% of the time, Pallas kernels for 16%

profile of v1, /device:TPU:0, one launch (start us, length us, event | category | flops | bytes accessed | tf_op | source)
XLA Modules:
  0.0 89.7 jit_solution(5912068337437375356)
XLA Ops:
  0.0 4.2 %fusion.16 = (f32[2,2048,2]{2,1,0:T(8,128)S(1)}, f32[2,2048,2]{2,1,0:T(8,128)}) fusion(f32[2,2048,128]{2,1,0:T(8,128)} %field.1), kind=kLoop, calls=%fused_computation.64 | loop fusion | bytes 131072 | tf_op jit(solution)/shard_map/slice | solution.py:208
  4.9 5.0 %collective-permute-start = (f32[2,2,2048]{2,1,0:T(2,128)S(1)}, f32[2,2,2048]{2,1,0:T(2,128)S(1)}, u32[]{:S(2)}, u32[]{:S(2)}) collective-permute-start(f32[2,2,2048]{2,1,0:T(2,128)S(1)} %bitcast.44), channel_id=1, source_target_pairs={{0,1},{2,3},{4,5},{6,7},{8,9},{10,11},{12,13},{14,15},{16,17},{18,... | collective-permute-start | bytes 98312 | tf_op jit(solution)/shard_map/ppermute | solution.py:208
  9.9 2.2 %copy.40 = f32[2,2048,2]{1,0,2:T(2,128)S(1)} copy(f32[2,2048,2]{2,1,0:T(8,128)} %get-tuple-element.38) | data formatting | bytes 65536
  12.1 1.3 %collective-permute-start.1 = (f32[2,2,2048]{2,1,0:T(2,128)S(1)}, f32[2,2,2048]{2,1,0:T(2,128)S(1)}, u32[]{:S(2)}, u32[]{:S(2)}) collective-permute-start(f32[2,2,2048]{2,1,0:T(2,128)S(1)} %bitcast.45), channel_id=1, source_target_pairs={{1,0},{3,2},{5,4},{7,6},{9,8},{11,10},{13,12},{15,14},{17,16},{19,... | collective-permute-start | bytes 98312 | tf_op jit(solution)/shard_map/ppermute | solution.py:209
  13.5 4.4 %collective-permute-done.1 = f32[2,2,2048]{2,1,0:T(2,128)S(1)} collective-permute-done((f32[2,2,2048]{2,1,0:T(2,128)S(1)}, f32[2,2,2048]{2,1,0:T(2,128)S(1)}, u32[]{:S(2)}, u32[]{:S(2)}) %collective-permute-start.1) | collective-permute-done | bytes 32800 | tf_op jit(solution)/shard_map/ppermute | solution.py:209
  20.8 1.5 %collective-permute-start.10 = (f32[2,144,128]{2,1,0:T(8,128)S(1)}, f32[2,144,128]{2,1,0:T(8,128)S(1)}, u32[]{:S(2)}, u32[]{:S(2)}) collective-permute-start(f32[2,144,128]{2,1,0:T(8,128)S(1)} %get-tuple-element.31), channel_id=1, source_target_pairs={{0,4},{2,6},{4,0},{6,2},{8,12},{10,14},{12,8},{14,10},{16,20},{18,... | collective-permute-start | bytes 442376 | tf_op jit(solution)/shard_map/ppermute | solution.py:269
  22.4 1.6 %collective-permute-start.12 = (f32[2,144,128]{2,1,0:T(8,128)S(1)}, f32[2,144,128]{2,1,0:T(8,128)S(1)}, u32[]{:S(2)}, u32[]{:S(2)}) collective-permute-start(f32[2,144,128]{2,1,0:T(8,128)S(1)} %get-tuple-element.33), channel_id=1, source_target_pairs={{0,8},{2,10},{4,12},{6,14},{8,0},{10,2},{12,4},{14,6},{16,24},{18,... | collective-permute-start | bytes 442376 | tf_op jit(solution)/shard_map/ppermute | solution.py:269
  24.3 2.5 %collective-permute-start.14 = (f32[2,144,128]{2,1,0:T(8,128)S(1)}, f32[2,144,128]{2,1,0:T(8,128)S(1)}, u32[]{:S(2)}, u32[]{:S(2)}) collective-permute-start(f32[2,144,128]{2,1,0:T(8,128)S(1)} %get-tuple-element.35), channel_id=1, source_target_pairs={{0,12},{2,14},{4,8},{6,10},{8,4},{10,6},{12,0},{14,2},{16,28},{18,... | collective-permute-start | bytes 442376 | tf_op jit(solution)/shard_map/ppermute | solution.py:269
  26.9 1.6 %collective-permute-done.11.refs_3_ = f32[2,144,128]{2,1,0:T(8,128)S(1)} collective-permute-done((f32[2,144,128]{2,1,0:T(8,128)S(1)}, f32[2,144,128]{2,1,0:T(8,128)S(1)}, u32[]{:S(2)}, u32[]{:S(2)}) %collective-permute-start.11) | collective-permute-done | bytes 147488 | tf_op jit(solution)/shard_map/ppermute | solution.py:269
  28.5 1.7 %collective-permute-start.9 = (f32[2,144,128]{2,1,0:T(8,128)S(1)}, f32[2,144,128]{2,1,0:T(8,128)S(1)}, u32[]{:S(2)}, u32[]{:S(2)}) collective-permute-start(f32[2,144,128]{2,1,0:T(8,128)S(1)} %get-tuple-element.30), channel_id=1, source_target_pairs={{0,2},{2,0},{4,6},{6,4},{8,10},{10,8},{12,14},{14,12},{16,18},{18,... | collective-permute-start | bytes 442376 | tf_op jit(solution)/shard_map/ppermute | solution.py:269
  30.2 1.4 %collective-permute-done.13.refs_5_ = f32[2,144,128]{2,1,0:T(8,128)S(1)} collective-permute-done((f32[2,144,128]{2,1,0:T(8,128)S(1)}, f32[2,144,128]{2,1,0:T(8,128)S(1)}, u32[]{:S(2)}, u32[]{:S(2)}) %collective-permute-start.13) | collective-permute-done | bytes 147488 | tf_op jit(solution)/shard_map/ppermute | solution.py:269
  31.6 1.7 %collective-permute-start.3 = (f32[2,144,128]{2,1,0:T(8,128)S(1)}, f32[2,144,128]{2,1,0:T(8,128)S(1)}, u32[]{:S(2)}, u32[]{:S(2)}) collective-permute-start(f32[2,144,128]{2,1,0:T(8,128)S(1)} %get-tuple-element.23), channel_id=1, source_target_pairs={{0,4},{2,6},{4,0},{6,2},{8,12},{10,14},{12,8},{14,10},{16,20},{18,... | collective-permute-start | bytes 442376 | tf_op jit(solution)/shard_map/ppermute | solution.py:269
  33.4 1.4 %collective-permute-done.14.refs_6_ = f32[2,144,128]{2,1,0:T(8,128)S(1)} collective-permute-done((f32[2,144,128]{2,1,0:T(8,128)S(1)}, f32[2,144,128]{2,1,0:T(8,128)S(1)}, u32[]{:S(2)}, u32[]{:S(2)}) %collective-permute-start.14) | collective-permute-done | bytes 147488 | tf_op jit(solution)/shard_map/ppermute | solution.py:269
  34.7 1.2 %collective-permute-start.4 = (f32[2,144,128]{2,1,0:T(8,128)S(1)}, f32[2,144,128]{2,1,0:T(8,128)S(1)}, u32[]{:S(2)}, u32[]{:S(2)}) collective-permute-start(f32[2,144,128]{2,1,0:T(8,128)S(1)} %get-tuple-element.24), channel_id=1, source_target_pairs={{0,6},{2,4},{4,2},{6,0},{8,14},{10,12},{12,10},{14,8},{16,22},{18,... | collective-permute-start | bytes 442376 | tf_op jit(solution)/shard_map/ppermute | solution.py:269
  36.0 2.6 %collective-permute-done.15.refs_7_ = f32[2,144,128]{2,1,0:T(8,128)S(1)} collective-permute-done((f32[2,144,128]{2,1,0:T(8,128)S(1)}, f32[2,144,128]{2,1,0:T(8,128)S(1)}, u32[]{:S(2)}, u32[]{:S(2)}) %collective-permute-start.15) | collective-permute-done | bytes 147488 | tf_op jit(solution)/shard_map/ppermute | solution.py:269
  38.6 1.6 %collective-permute-start.5 = (f32[2,144,128]{2,1,0:T(8,128)S(1)}, f32[2,144,128]{2,1,0:T(8,128)S(1)}, u32[]{:S(2)}, u32[]{:S(2)}) collective-permute-start(f32[2,144,128]{2,1,0:T(8,128)S(1)} %get-tuple-element.25), channel_id=1, source_target_pairs={{0,8},{2,10},{4,12},{6,14},{8,0},{10,2},{12,4},{14,6},{16,24},{18,... | collective-permute-start | bytes 442376 | tf_op jit(solution)/shard_map/ppermute | solution.py:269
  40.9 10.7 %pick_boundary.1 = f32[4,144,128]{2,1,0:T(8,128)} custom-call(s32[2]{0:T(128)} %copy-done.17, f32[2,144,128]{2,1,0:T(8,128)} %copy-done.1, f32[2,144,128]{2,1,0:T(8,128)} %copy-done.15, f32[2,144,128]{2,1,0:T(8,128)} %copy-done.3, f32[2,144,128]{2,1,0:T(8,128)} %copy-done.5, f32[2,144,128]{2,1,0:T(8,128)} %copy-done.7, f32[2,144,128]{2,1,0:T(8,128)} %copy-done.9, ...), custom_call_target="tpu_custom_call" | custom-call | tf_op jit(solution)/shard_map/pick_boundary/pallas_call | solution.py:275
  51.6 2.6 %collective-permute-start.16 = (f32[4,144,128]{2,1,0:T(8,128)}, f32[4,144,128]{2,1,0:T(8,128)S(1)}, u32[]{:S(2)}, u32[]{:S(2)}) collective-permute-start(f32[4,144,128]{2,1,0:T(8,128)} %pick_boundary.1), channel_id=1, source_target_pairs={{0,16},{2,18},{4,20},{6,22},{8,24},{10,26},{12,28},{14,30},{16,0},... | collective-permute-start | bytes 884744 | tf_op jit(solution)/shard_map/ppermute | solution.py:269
  62.2 3.9 %render_first.1 = f32[4,128,128]{2,1,0:T(8,128)S(1)} custom-call(s32[2]{0:T(128)S(1)} %copy-done.18, bf16[512,256]{1,0:T(8,128)(2,1)S(1)} %copy-done.20, f32[2,144,128]{2,1,0:T(8,128)S(1)} %copy-done.2, f32[2,144,128]{2,1,0:T(8,128)S(1)} %copy-done.16, f32[2,144,128]{2,1,0:T(8,128)S(1)} %copy-done.4, f32[2,144,128]{2,1,0:T(8,128)S(1)} %copy-done.6, ...), custom_call_target="tpu_custom_call" | custom-call | flops 5000000000 | bytes 2000000 | tf_op jit(solution)/shard_map/render_first/pallas_call | solution.py:276
  67.7 1.6 %collective-permute-start.8 = (f32[2,144,128]{2,1,0:T(8,128)S(1)}, f32[2,144,128]{2,1,0:T(8,128)S(1)}, u32[]{:S(2)}, u32[]{:S(2)}) collective-permute-start(f32[2,144,128]{2,1,0:T(8,128)S(1)} %get-tuple-element.28), channel_id=1, source_target_pairs={{0,14},{2,12},{4,10},{6,8},{8,6},{10,4},{12,2},{14,0},{16,30},{18,... | collective-permute-start | bytes 442376 | tf_op jit(solution)/shard_map/ppermute | solution.py:269
  69.3 7.1 %collective-permute-done.6.refs_5_ = f32[2,144,128]{2,1,0:T(8,128)S(1)} collective-permute-done((f32[2,144,128]{2,1,0:T(8,128)S(1)}, f32[2,144,128]{2,1,0:T(8,128)S(1)}, u32[]{:S(2)}, u32[]{:S(2)}) %collective-permute-start.6) | collective-permute-done | bytes 147488 | tf_op jit(solution)/shard_map/ppermute | solution.py:269
  76.4 4.3 %collective-permute-done.7.refs_6_ = f32[2,144,128]{2,1,0:T(8,128)S(1)} collective-permute-done((f32[2,144,128]{2,1,0:T(8,128)S(1)}, f32[2,144,128]{2,1,0:T(8,128)S(1)}, u32[]{:S(2)}, u32[]{:S(2)}) %collective-permute-start.7) | collective-permute-done | bytes 147488 | tf_op jit(solution)/shard_map/ppermute | solution.py:269
  80.7 3.6 %collective-permute-done.8.refs_7_ = f32[2,144,128]{2,1,0:T(8,128)S(1)} collective-permute-done((f32[2,144,128]{2,1,0:T(8,128)S(1)}, f32[2,144,128]{2,1,0:T(8,128)S(1)}, u32[]{:S(2)}, u32[]{:S(2)}) %collective-permute-start.8) | collective-permute-done | bytes 147488 | tf_op jit(solution)/shard_map/ppermute | solution.py:269
  84.3 5.4 %render_last.1 = f32[4,128,128]{2,1,0:T(8,128)} custom-call(s32[2]{0:T(128)S(1)} %copy-done.19, bf16[512,256]{1,0:T(8,128)(2,1)S(1)} %copy-done.20, f32[2,144,128]{2,1,0:T(8,128)S(1)} %get-tuple-element.21.refs_0_, f32[2,144,128]{2,1,0:T(8,128)S(1)} %collective-permute-done.2.refs_1_, f32[2,144,128]{2,1,0:T(8,128)S(1)} %collective-permute-done.3.refs_2_, ...), custom_call_target="tpu_custom_call" | custom-call | flops 5000000000 | bytes 2000000 | tf_op jit(solution)/shard_map/render_last/pallas_call | solution.py:278
  (81 shorter events, 14.4 us)
Async XLA Ops:
  4.9 14.5 %copy-start = (f32[2,2048,128]{2,1,0:T(8,128)S(1)}, f32[2,2048,128]{2,1,0:T(8,128)}, u32[]{:S(2)}) copy-start(f32[2,2048,128]{2,1,0:T(8,128)} %field.1) | copy-start | bytes 6291460
  4.9 8.6 %collective-permute-start = (f32[2,2,2048]{2,1,0:T(2,128)S(1)}, f32[2,2,2048]{2,1,0:T(2,128)S(1)}, u32[]{:S(2)}, u32[]{:S(2)}) collective-permute-start(f32[2,2,2048]{2,1,0:T(2,128)S(1)} %bitcast.44), channel_id=1, source_target_pairs={{0,1},{2,3},{4,5},{6,7},{8,9},{10,11},{12,13},{14,15},{16,17},{18,... | collective-permute-start | bytes 98312 | tf_op jit(solution)/shard_map/ppermute | solution.py:208
  12.1 5.8 %collective-permute-start.1 = (f32[2,2,2048]{2,1,0:T(2,128)S(1)}, f32[2,2,2048]{2,1,0:T(2,128)S(1)}, u32[]{:S(2)}, u32[]{:S(2)}) collective-permute-start(f32[2,2,2048]{2,1,0:T(2,128)S(1)} %bitcast.45), channel_id=1, source_target_pairs={{1,0},{3,2},{5,4},{7,6},{9,8},{11,10},{13,12},{15,14},{17,16},{19,... | collective-permute-start | bytes 98312 | tf_op jit(solution)/shard_map/ppermute | solution.py:209
  13.5 26.7 %copy-start.17 = (s32[2]{0:T(128)}, s32[2]{0:T(128)S(1)}, u32[]{:S(2)}) copy-start(s32[2]{0:T(128)S(1)} %pad_add_fusion.info) | copy-start | bytes 28
  18.8 35.4 %copy-start.20 = (bf16[512,256]{1,0:T(8,128)(2,1)S(1)}, bf16[512,256]{1,0:T(8,128)(2,1)}, u32[]{:S(2)}) copy-start(bf16[512,256]{1,0:T(8,128)(2,1)} %constant.38.clone.weights) | copy-start | bytes 786436
  20.8 6.0 %collective-permute-start.10 = (f32[2,144,128]{2,1,0:T(8,128)S(1)}, f32[2,144,128]{2,1,0:T(8,128)S(1)}, u32[]{:S(2)}, u32[]{:S(2)}) collective-permute-start(f32[2,144,128]{2,1,0:T(8,128)S(1)} %get-tuple-element.31), channel_id=1, source_target_pairs={{0,4},{2,6},{4,0},{6,2},{8,12},{10,14},{12,8},{14,10},{16,20},{18,... | collective-permute-start | bytes 442376 | tf_op jit(solution)/shard_map/ppermute | solution.py:269
  22.4 6.1 %collective-permute-start.11 = (f32[2,144,128]{2,1,0:T(8,128)S(1)}, f32[2,144,128]{2,1,0:T(8,128)S(1)}, u32[]{:S(2)}, u32[]{:S(2)}) collective-permute-start(f32[2,144,128]{2,1,0:T(8,128)S(1)} %get-tuple-element.32), channel_id=1, source_target_pairs={{0,6},{2,4},{4,2},{6,0},{8,14},{10,12},{12,10},{14,8},{16,22},{18,... | collective-permute-start | bytes 442376 | tf_op jit(solution)/shard_map/ppermute | solution.py:269
  22.4 7.8 %collective-permute-start.12 = (f32[2,144,128]{2,1,0:T(8,128)S(1)}, f32[2,144,128]{2,1,0:T(8,128)S(1)}, u32[]{:S(2)}, u32[]{:S(2)}) collective-permute-start(f32[2,144,128]{2,1,0:T(8,128)S(1)} %get-tuple-element.33), channel_id=1, source_target_pairs={{0,8},{2,10},{4,12},{6,14},{8,0},{10,2},{12,4},{14,6},{16,24},{18,... | collective-permute-start | bytes 442376 | tf_op jit(solution)/shard_map/ppermute | solution.py:269
  23.9 7.7 %collective-permute-start.13 = (f32[2,144,128]{2,1,0:T(8,128)S(1)}, f32[2,144,128]{2,1,0:T(8,128)S(1)}, u32[]{:S(2)}, u32[]{:S(2)}) collective-permute-start(f32[2,144,128]{2,1,0:T(8,128)S(1)} %get-tuple-element.34), channel_id=1, source_target_pairs={{0,10},{2,8},{4,14},{6,12},{8,2},{10,0},{12,6},{14,4},{16,26},{18,... | collective-permute-start | bytes 442376 | tf_op jit(solution)/shard_map/ppermute | solution.py:269
  24.3 10.4 %collective-permute-start.14 = (f32[2,144,128]{2,1,0:T(8,128)S(1)}, f32[2,144,128]{2,1,0:T(8,128)S(1)}, u32[]{:S(2)}, u32[]{:S(2)}) collective-permute-start(f32[2,144,128]{2,1,0:T(8,128)S(1)} %get-tuple-element.35), channel_id=1, source_target_pairs={{0,12},{2,14},{4,8},{6,10},{8,4},{10,6},{12,0},{14,2},{16,28},{18,... | collective-permute-start | bytes 442376 | tf_op jit(solution)/shard_map/ppermute | solution.py:269
  26.9 13.3 %copy-start.3 = (f32[2,144,128]{2,1,0:T(8,128)}, f32[2,144,128]{2,1,0:T(8,128)S(1)}, u32[]{:S(2)}) copy-start(f32[2,144,128]{2,1,0:T(8,128)S(1)} %collective-permute-done.10.refs_2_) | copy-start | bytes 442372
  26.9 11.7 %collective-permute-start.15 = (f32[2,144,128]{2,1,0:T(8,128)S(1)}, f32[2,144,128]{2,1,0:T(8,128)S(1)}, u32[]{:S(2)}, u32[]{:S(2)}) collective-permute-start(f32[2,144,128]{2,1,0:T(8,128)S(1)} %get-tuple-element.36), channel_id=1, source_target_pairs={{0,14},{2,12},{4,10},{6,8},{8,6},{10,4},{12,2},{14,0},{16,30},{18,... | collective-permute-start | bytes 442376 | tf_op jit(solution)/shard_map/ppermute | solution.py:269
  28.5 11.7 %copy-start.5 = (f32[2,144,128]{2,1,0:T(8,128)}, f32[2,144,128]{2,1,0:T(8,128)S(1)}, u32[]{:S(2)}) copy-start(f32[2,144,128]{2,1,0:T(8,128)S(1)} %collective-permute-done.11.refs_3_) | copy-start | bytes 442372
  28.5 11.7 %collective-permute-start.9 = (f32[2,144,128]{2,1,0:T(8,128)S(1)}, f32[2,144,128]{2,1,0:T(8,128)S(1)}, u32[]{:S(2)}, u32[]{:S(2)}) collective-permute-start(f32[2,144,128]{2,1,0:T(8,128)S(1)} %get-tuple-element.30), channel_id=1, source_target_pairs={{0,2},{2,0},{4,6},{6,4},{8,10},{10,8},{12,14},{14,12},{16,18},{18,... | collective-permute-start | bytes 442376 | tf_op jit(solution)/shard_map/ppermute | solution.py:269
  30.2 35.9 %collective-permute-start.2 = (f32[2,144,128]{2,1,0:T(8,128)S(1)}, f32[2,144,128]{2,1,0:T(8,128)S(1)}, u32[]{:S(2)}, u32[]{:S(2)}) collective-permute-start(f32[2,144,128]{2,1,0:T(8,128)S(1)} %get-tuple-element.22), channel_id=1, source_target_pairs={{0,2},{2,0},{4,6},{6,4},{8,10},{10,8},{12,14},{14,12},{16,18},{18,... | collective-permute-start | bytes 442376 | tf_op jit(solution)/shard_map/ppermute | solution.py:269
  31.6 34.8 %collective-permute-start.3 = (f32[2,144,128]{2,1,0:T(8,128)S(1)}, f32[2,144,128]{2,1,0:T(8,128)S(1)}, u32[]{:S(2)}, u32[]{:S(2)}) collective-permute-start(f32[2,144,128]{2,1,0:T(8,128)S(1)} %get-tuple-element.23), channel_id=1, source_target_pairs={{0,4},{2,6},{4,0},{6,2},{8,12},{10,14},{12,8},{14,10},{16,20},{18,... | collective-permute-start | bytes 442376 | tf_op jit(solution)/shard_map/ppermute | solution.py:269
  34.7 31.7 %collective-permute-start.4 = (f32[2,144,128]{2,1,0:T(8,128)S(1)}, f32[2,144,128]{2,1,0:T(8,128)S(1)}, u32[]{:S(2)}, u32[]{:S(2)}) collective-permute-start(f32[2,144,128]{2,1,0:T(8,128)S(1)} %get-tuple-element.24), channel_id=1, source_target_pairs={{0,6},{2,4},{4,2},{6,0},{8,14},{10,12},{12,10},{14,8},{16,22},{18,... | collective-permute-start | bytes 442376 | tf_op jit(solution)/shard_map/ppermute | solution.py:269
  38.6 29.1 %collective-permute-start.5 = (f32[2,144,128]{2,1,0:T(8,128)S(1)}, f32[2,144,128]{2,1,0:T(8,128)S(1)}, u32[]{:S(2)}, u32[]{:S(2)}) collective-permute-start(f32[2,144,128]{2,1,0:T(8,128)S(1)} %get-tuple-element.25), channel_id=1, source_target_pairs={{0,8},{2,10},{4,12},{6,14},{8,0},{10,2},{12,4},{14,6},{16,24},{18,... | collective-permute-start | bytes 442376 | tf_op jit(solution)/shard_map/ppermute | solution.py:269
  51.6 32.7 %collective-permute-start.16 = (f32[4,144,128]{2,1,0:T(8,128)}, f32[4,144,128]{2,1,0:T(8,128)S(1)}, u32[]{:S(2)}, u32[]{:S(2)}) collective-permute-start(f32[4,144,128]{2,1,0:T(8,128)} %pick_boundary.1), channel_id=1, source_target_pairs={{0,16},{2,18},{4,20},{6,22},{8,24},{10,26},{12,28},{14,30},{16,0},... | collective-permute-start | bytes 884744 | tf_op jit(solution)/shard_map/ppermute | solution.py:269
  62.2 22.2 %copy-start.19 = (s32[2]{0:T(128)S(1)}, s32[2]{0:T(128)}, u32[]{:S(2)}) copy-start(s32[2]{0:T(128)} %copy-done.17) | copy-start | bytes 28
  66.0 18.3 %collective-permute-start.17 = (f32[4,128,128]{2,1,0:T(8,128)S(1)}, f32[4,128,128]{2,1,0:T(8,128)S(1)}, u32[]{:S(2)}, u32[]{:S(2)}) collective-permute-start(f32[4,128,128]{2,1,0:T(8,128)S(1)} %render_first.1), channel_id=1, source_target_pairs={{0,16},{2,18},{4,20},{6,22},{8,24},{10,26},{12,28},{14,30},{16,0},... | collective-permute-start | bytes 786440 | tf_op jit(solution)/shard_map/ppermute | solution.py:269
  66.4 9.9 %collective-permute-start.6 = (f32[2,144,128]{2,1,0:T(8,128)S(1)}, f32[2,144,128]{2,1,0:T(8,128)S(1)}, u32[]{:S(2)}, u32[]{:S(2)}) collective-permute-start(f32[2,144,128]{2,1,0:T(8,128)S(1)} %get-tuple-element.26), channel_id=1, source_target_pairs={{0,10},{2,8},{4,14},{6,12},{8,2},{10,0},{12,6},{14,4},{16,26},{18,... | collective-permute-start | bytes 442376 | tf_op jit(solution)/shard_map/ppermute | solution.py:269
  66.5 14.3 %collective-permute-start.7 = (f32[2,144,128]{2,1,0:T(8,128)S(1)}, f32[2,144,128]{2,1,0:T(8,128)S(1)}, u32[]{:S(2)}, u32[]{:S(2)}) collective-permute-start(f32[2,144,128]{2,1,0:T(8,128)S(1)} %get-tuple-element.27), channel_id=1, source_target_pairs={{0,12},{2,14},{4,8},{6,10},{8,4},{10,6},{12,0},{14,2},{16,28},{18,... | collective-permute-start | bytes 442376 | tf_op jit(solution)/shard_map/ppermute | solution.py:269
  67.7 16.6 %collective-permute-start.8 = (f32[2,144,128]{2,1,0:T(8,128)S(1)}, f32[2,144,128]{2,1,0:T(8,128)S(1)}, u32[]{:S(2)}, u32[]{:S(2)}) collective-permute-start(f32[2,144,128]{2,1,0:T(8,128)S(1)} %get-tuple-element.28), channel_id=1, source_target_pairs={{0,14},{2,12},{4,10},{6,8},{8,6},{10,4},{12,2},{14,0},{16,30},{18,... | collective-permute-start | bytes 442376 | tf_op jit(solution)/shard_map/ppermute | solution.py:269
  (15 other events, 35.0 us)

commit v2 on v1

--- a/solution.py
+++ b/solution.py
@@ -46,22 +46,20 @@
     return hi, mid, lo
 
 
-def filter_columns(block, plane, rows, weights, sx, dx, slot):
-    width = block.shape[2]
-    hi, mid, lo = three_parts(block[plane, 0:rows, :])
-    sides = [part.astype(jnp.float32) for part in three_parts(block[plane, rows : rows + 8, :])]
+def filter_columns(block, plane, own, weights, sx, dx, slot):
+    width = block.shape[-1]
+    hi, mid, lo = three_parts(block[plane, 0 : own + 8, :])
+    sides = [part.astype(jnp.float32) for part in three_parts(block[plane, own + 8 : own + 16, :])]
     lanes_first = jnp.transpose(jnp.concatenate(sides, 0))
-    lane = lax.broadcasted_iota(jnp.int32, lanes_first.shape, 1)
-    pieces = []
-    for b in range(-(-rows // LANES)):
-        mine = jnp.where(lane % 8 // 4 == b, lanes_first, 0.0)
-        pieces.append(mine[0 : min(LANES, rows - b * LANES)])
-    side = jnp.concatenate(pieces, 0)
-    side = jnp.concatenate([side, jnp.zeros((rows, LANES - side.shape[1]), jnp.float32)], 1)
+    inner = lax.broadcasted_iota(jnp.int32, lanes_first.shape, 1) % 8 < 4
+    side = jnp.concatenate([jnp.where(inner, lanes_first, 0.0)[0:own], jnp.where(inner, 0.0, lanes_first)[0:8]], 0)
+    side = jnp.concatenate([side, jnp.zeros((own + 8, LANES - side.shape[1]), jnp.float32)], 1)
     row = jnp.concatenate([hi, mid, lo, side.astype(jnp.bfloat16)], 1)
     both = jnp.dot(row, weights[...], preferred_element_type=jnp.float32)
-    sx[slot] = both[:, :width]
-    dx[slot] = both[:, width:]
+    for out, part in ((sx, both[:, :width]), (dx, both[:, width:])):
+        out[slot, 8 : 8 + own] = part[0:own]
+        out[slot, 6:8] = part[own : own + 2]
+        out[slot, 8 + own : 10 + own] = part[own + 2 : own + 4]
 
 
 def gauss_rows(a, b, c, d, e):
@@ -87,7 +85,7 @@
 
 def render(sx, dx, first, count):
     def rows_of(ref, slot):
-        return [ref[slot, pl.ds(first + k, TILE), :] for k in range(5)]
+        return [ref[slot, pl.ds(first + 6 + k, TILE), :] for k in range(5)]
 
     zero = jnp.zeros((TILE, sx.shape[2]), jnp.float32)
     state = (zero, zero, zero, zero)
@@ -122,7 +120,7 @@
         boundary, other, image, sx, dx = refs
     else:
         image, sx, dx = refs
-    depth, rows = blocks[0].shape[0], sx.shape[1]
+    depth, own = blocks[0].shape[0], image.shape[1]
     planes = depth * size
     extra = 4 if last else 0
     pos, front = info[0], info[1]
@@ -133,12 +131,12 @@
     for step in range(size):
         for plane in range(depth):
             slot = (pos ^ step) * depth + plane + start
-            filter_columns(blocks[step], plane, rows, weights, sx, dx, slot)
+            filter_columns(blocks[step], plane, own, weights, sx, dx, slot)
     for plane in range(extra):
         slot = (planes + 2) * front + plane
-        filter_columns(boundary, plane, rows, weights, sx, dx, slot)
-
-    @pl.loop(0, image.shape[1] // TILE)
+        filter_columns(boundary, plane, own, weights, sx, dx, slot)
+
+    @pl.loop(0, own // TILE)
     def _(tile):
         first = pl.multiple_of(tile * TILE, TILE)
         total = render(sx, dx, first, planes - 2 + extra)
@@ -153,27 +151,59 @@
             image[channel, pl.ds(first, TILE), :] = total[channel]
 
 
-def pack_kernel(size, rows, info, field, sides, *refs):
-    outs, padded = refs[:-1], refs[-1]
+def edge_kernel(field, out):
     depth, height, width = field.shape
-    own = rows - 8
+    lane = lax.broadcasted_iota(jnp.int32, (LANES, width), 1)
+    count = depth * height // LANES
+    for base in range(0, count, LANES // 4):
+        packed = jnp.zeros((LANES, width), jnp.float32)
+        for chunk in range(base, min(base + LANES // 4, count)):
+            at = chunk * LANES
+            rows = field[at // height, at % height : at % height + LANES, :]
+            place = 4 * (chunk - base)
+            packed = jnp.where(lane // 4 == chunk - base, pltpu.roll(rows, (place + 2) % width, 1), packed)
+        out[base // (LANES // 4)] = jnp.transpose(packed)
+
+
+def pack_kernel(size, info, field, before, after, *refs):
+    outs, sides = refs[:-1], refs[-1]
+    depth, height, width = field.shape
+    own = outs[0].shape[1] - 16
+    groups = height // own
     pos, front = info[0], info[1]
-    padded[:, 0:8, :] = jnp.zeros((depth, 8, width), jnp.float32)
-    padded[:, 8 + height : 16 + height, :] = jnp.zeros((depth, 8, width), jnp.float32)
-    padded[:, 8 : 8 + height, :] = field[...]
+    row = lax.broadcasted_iota(jnp.int32, before.shape, 1) % 4
+    left = jnp.where(info[2] == 1, before[...], 0.0)
+    right = jnp.where(info[3] == 1, after[...], 0.0)
+    sides[...] = jnp.where(row < 2, left, right).reshape(sides.shape)
+    lane = lax.broadcasted_iota(jnp.int32, (4, LANES), 1)
+    line = lax.broadcasted_iota(jnp.int32, (8, width), 0)
+
+    def side_rows(plane, at, to):
+        chunk = sides[pl.ds(plane * (4 * height // LANES) + at // LANES * 4, 4), :]
+        return pltpu.roll(chunk, (to + LANES - at % LANES) % LANES, 1)
+
     for chunk in range(2):
-        base = (1 - front) * size if chunk == 0 else front * size
+        base = front * size if chunk == 0 else (1 - front) * size
         for step in range(size):
             out = outs[chunk * size + step]
             target = base + (pos ^ step)
             start = pl.multiple_of(target * own, 8)
+            inner_top, inner_end = target > 0, target < groups - 1
+            above = pl.multiple_of(jnp.maximum(start - 8, 0), 8)
+            below = pl.multiple_of(jnp.minimum(start + own, height - 8), 8)
             for plane in range(depth):
-                out[plane, 0:rows, :] = padded[plane, pl.ds(start + 6, rows), :]
-                out[plane, rows : rows + 8, :] = sides[target, plane]
+                out[plane, 0:own, :] = field[plane, pl.ds(start, own), :]
+                top = jnp.where(inner_top, pltpu.roll(field[plane, pl.ds(above, 8), :], 2, 0), 0.0)
+                end = jnp.where(inner_end, pltpu.roll(field[plane, pl.ds(below, 8), :], 2, 0), 0.0)
+                out[plane, own : own + 8, :] = jnp.where(line < 2, top, jnp.where(line < 4, end, 0.0))
+                top = jnp.where(inner_top, side_rows(plane, jnp.maximum(start - 2, 0), 0), 0.0)
+                end = jnp.where(inner_end, side_rows(plane, jnp.minimum(start + own, height - 2), 2), 0.0)
+                out[plane, own + 8 : own + 12, :] = side_rows(plane, start, 0)
+                out[plane, own + 12 : own + 16, :] = jnp.where(lane < 2, top, end)
 
 
 def pick_kernel(size, info, *refs):
-    blocks, out, sem = refs[:size], refs[size], refs[size + 1]
+    blocks, out = refs[:size], refs[size]
     depth = blocks[0].shape[0]
     pos, front = info[0], info[1]
     count = 4 // depth
@@ -183,65 +213,55 @@
 
             @pl.when(wanted == step)
             def _():
-                pltpu.make_async_copy(blocks[step], out.at[pl.ds(part * depth, depth)], sem.at[part]).start()
-
-    for part in range(count):
-        place = out.at[pl.ds(part * depth, depth)]
-        pltpu.make_async_copy(blocks[0], place, sem.at[part]).wait()
+                out[part * depth : (part + 1) * depth] = blocks[step][...]
 
 
 SMEM = pl.BlockSpec(memory_space=pltpu.SMEM)
 VMEM = pl.BlockSpec(memory_space=pltpu.VMEM)
-ANY = pl.BlockSpec(memory_space=pl.ANY)
-PARAMS = pltpu.CompilerParams(vmem_limit_bytes=48 * 1024 * 1024)
+PARAMS = pltpu.CompilerParams(vmem_limit_bytes=20 * 1024 * 1024)
 
 
 def cost(flops, size):
     return pl.CostEstimate(flops=flops, bytes_accessed=size, transcendentals=0)
 
 
-def side_columns(field, own, rows):
-    groups = lax.axis_size("cols")
-    up = [(i, i + 1) for i in range(groups - 1)]
-    down = [(j, i) for i, j in up]
-    width = field.shape[2]
-    before = lax.ppermute(jnp.transpose(field[:, :, width - 2 :], (2, 0, 1)), "cols", up)
-    after = lax.ppermute(jnp.transpose(field[:, :, :2], (2, 0, 1)), "cols", down)
-    both = jnp.concatenate([before, after], 0)
-    depth, height = both.shape[1:]
-    pieces = -(-rows // LANES)
-    span = pieces * LANES
-    count = height // own
-    both = jnp.pad(both, ((0, 0), (0, 0), (2, span)))
-    cut = jnp.stack([both[:, :, own * j : own * j + span] for j in range(count)], 0)
-    cut = cut.reshape(count, 4, depth, pieces, LANES).transpose(0, 2, 3, 1, 4)
-    cut = cut.reshape(count, depth, 4 * pieces, LANES)
-    return jnp.pad(cut, ((0, 0), (0, 0), (0, 8 - 4 * pieces), (0, 0)))
-
-
 def local(field):
     groups = lax.axis_size("depth")
+    columns = lax.axis_size("cols")
     size = groups // 2
     depth, height, width = field.shape
     own = height // groups
-    rows = own + 8
     me = lax.axis_index("depth")
-    info = jnp.stack([me % size, 1 - me // size]).astype(jnp.int32)
+    column = lax.axis_index("cols")
+    has_left, has_right = column > 0, column < columns - 1
+    info = jnp.stack([me % size, 1 - me // size, has_left, has_right]).astype(jnp.int32)
     weights = jnp.asarray(column_weights(width))
     f32 = jnp.float32
-    block = jax.ShapeDtypeStruct((depth, rows + 8, width), f32)
+    block = jax.ShapeDtypeStruct((depth, own + 16, width), f32)
     image = jax.ShapeDtypeStruct((4, own, width), f32)
 
-    sides = side_columns(field, own, rows)
+    edges = pl.pallas_call(
+        edge_kernel,
+        out_shape=jax.ShapeDtypeStruct((-(-depth * height // LANES // (LANES // 4)), LANES, LANES), f32),
+        in_specs=[VMEM],
+        out_specs=VMEM,
+        compiler_params=PARAMS,
+        name="edge_columns",
+    )(field)
+    if columns == 2:
+        before = after = lax.ppermute(edges, "cols", [(0, 1), (1, 0)])
+    else:
+        before = lax.ppermute(edges, "cols", [(i, i + 1) for i in range(columns - 1)])
+        after = lax.ppermute(edges, "cols", [(i + 1, i) for i in range(columns - 1)])
     blocks = pl.pallas_call(
-        functools.partial(pack_kernel, size, rows),
+        functools.partial(pack_kernel, size),
         out_shape=(block,) * (2 * size),
-        in_specs=[SMEM, VMEM, VMEM],
+        in_specs=[SMEM] + [VMEM] * 3,
         out_specs=(VMEM,) * (2 * size),
-        scratch_shapes=[pltpu.VMEM((depth, height + 16, width), f32)],
+        scratch_shapes=[pltpu.VMEM((edges.shape[0] * LANES, LANES), f32)],
         compiler_params=PARAMS,
         name="pack_blocks",
-    )(info, field, sides)
+    )(info, field, before, after)
 
     def render_call(last):
         count = depth * size + (6 if last else 2)
@@ -250,7 +270,7 @@
             out_shape=image,
             in_specs=[SMEM] + [VMEM] * (size + (3 if last else 1)),
             out_specs=VMEM,
-            scratch_shapes=[pltpu.VMEM((count, rows, width), f32)] * 2,
+            scratch_shapes=[pltpu.VMEM((count, own + 16, width), f32)] * 2,
             compiler_params=PARAMS,
             cost_estimate=cost(5_000_000_000, 2_000_000),
             name="render_last" if last else "render_first",
@@ -258,10 +278,10 @@
 
     pick = pl.pallas_call(
         functools.partial(pick_kernel, size),
-        out_shape=jax.ShapeDtypeStruct((4, rows + 8, width), f32),
-        in_specs=[SMEM] + [ANY] * size,
-        out_specs=ANY,
-        scratch_shapes=[pltpu.SemaphoreType.DMA((4 // depth,))],
+        out_shape=jax.ShapeDtypeStruct((4,) + block.shape[1:], f32),
+        in_specs=[SMEM] + [VMEM] * size,
+        out_specs=VMEM,
+        compiler_params=PARAMS,
         name="pick_boundary",
     )
 
@@ -271,10 +291,10 @@
     def gathered(mine):
         return [mine[0]] + [swap(mine[step], step) for step in range(1, size)]
 
-    theirs = gathered(blocks[size:])
+    theirs = gathered(blocks[:size])
     boundary = swap(pick(info, *theirs), size)
     image_part = swap(render_call(False)(info, weights, *theirs), size)
-    mine = gathered(blocks[:size])
+    mine = gathered(blocks[size:])
     return render_call(True)(info, weights, *mine, boundary, image_part)
 
 

time: 90.1 us -> 63.3 us (0.70)
  local copies, waits for them, and re-layouts: 16.5 us -> 1.6 us
  Pallas kernels: 20.8 us -> 11.5 us
  other arithmetic: 1.32 us -> 0.08 us
    unnamed x45 -> x6, local copies, waits for them, and re-layouts: 12.1 us -> 1.6 us
    pallas_call x1, Pallas kernels: 10.7 us -> 0.63 us  [local(): boundary = swap(pick(info, *theirs), size)]
    slice x1 -> x0, local copies, waits for them, and re-layouts: 4.24 us -> none  [side_columns(): field[:, :, width - 2:]]
    ppermute x2 -> x1, starting transfers between devices: 6.27 us -> 3 us  [local(): before = after = lax.ppermute(edges, 'cols', [(0, 1), (1, 0)])]
    ppermute x16, starting transfers between devices: 18.2 us -> 21 us  [swap(): return lax.ppermute(x, 'depth', [(i, i ^ bits) for i in range(groups)])]
    ppermute x2 -> x1, waiting for transfers between devices: 4.38 us -> 2.17 us  [local(): before = after = lax.ppermute(edges, 'cols', [(0, 1), (1, 0)])]
    ppermute x16, waiting for transfers between devices: 22.1 us -> 23.7 us  [swap(): return lax.ppermute(x, 'depth', [(i, i ^ bits) for i in range(groups)])]
    unnamed x14 -> x0, other arithmetic: 1.21 us -> none
  transfers between devices with their start and end apart: 18 -> 17, of which waited for: 8 -> 8; matrix products, arithmetic and copies ran while one was open for 3% -> 0% of each run, Pallas kernels for 16% -> 7%
where the time goes in v2:
time: 63.3 us; the launch traced here: 63.2 us
  waiting for transfers between devices  25.9 us (41%)
  starting transfers between devices  24 us (38%)
  Pallas kernels  11.5 us (18%)
  local copies, waits for them, and re-layouts  1.6 us (3%)
    ppermute x16, waiting for transfers between devices, swap(): return lax.ppermute(x, 'depth', [(i, i ^ bits) for i in range(groups)])  23.7 us
    ppermute x16, starting transfers between devices, swap(): return lax.ppermute(x, 'depth', [(i, i ^ bits) for i in range(groups)])  21 us
    pallas_call x1, Pallas kernels, local(): return render_call(True)(info, weights, *mine, boundary, image_part)  5.35 us
    pallas_call x1, Pallas kernels, local(): image_part = swap(render_call(False)(info, weights, *theirs), size)  3.78 us
    ppermute x1, starting transfers between devices, local(): before = after = lax.ppermute(edges, 'cols', [(0, 1), (1, 0)])  3 us
    ppermute x1, waiting for transfers between devices, local(): before = after = lax.ppermute(edges, 'cols', [(0, 1), (1, 0)])  2.17 us
    unnamed x6, local copies, waits for them, and re-layouts  1.6 us
  transfers between devices with their start and end apart: 17, of which 8 were waited for; matrix products, arithmetic and copies ran while one was open for 0% of the time, Pallas kernels for 7%

profile of v2, /device:TPU:0, one launch (start us, length us, event | category | flops | bytes accessed | tf_op | source)
XLA Modules:
  0.0 63.2 jit_solution(7023170830175187955)
XLA Ops:
  0.0 1.6 %copy-done = f32[2,2048,128]{2,1,0:T(8,128)S(1)} copy-done((f32[2,2048,128]{2,1,0:T(8,128)S(1)}, f32[2,2048,128]{2,1,0:T(8,128)}, u32[]{:S(2)}) %copy-start) | copy-done | bytes 2097176
  1.6 0.7 %edge_columns.1 = f32[1,128,128]{2,1,0:T(8,128)S(1)} custom-call(f32[2,2048,128]{2,1,0:T(8,128)S(1)} %copy-done), custom_call_target="tpu_custom_call" | custom-call | tf_op jit(solution)/shard_map/edge_columns/pallas_call | solution.py:243
  2.3 3.0 %collective-permute-start = (f32[1,128,128]{2,1,0:T(8,128)S(1)}, f32[1,128,128]{2,1,0:T(8,128)S(1)}, u32[]{:S(2)}, u32[]{:S(2)}) collective-permute-start(f32[1,128,128]{2,1,0:T(8,128)S(1)} %edge_columns.1), channel_id=1, source_target_pairs={{0,1},{1,0},{2,3},{3,2},{4,5},{5,4},{6,7},{7,6},{8,9},{9,8},{10,11... | collective-permute-start | bytes 196616 | tf_op jit(solution)/shard_map/ppermute | solution.py:252
  5.4 2.2 %collective-permute-done.before.after = f32[1,128,128]{2,1,0:T(8,128)S(1)} collective-permute-done((f32[1,128,128]{2,1,0:T(8,128)S(1)}, f32[1,128,128]{2,1,0:T(8,128)S(1)}, u32[]{:S(2)}, u32[]{:S(2)}) %collective-permute-start) | collective-permute-done | bytes 65568 | tf_op jit(solution)/shard_map/ppermute | solution.py:252
  7.5 1.1 %pack_blocks.1 = (f32[2,144,128]{2,1,0:T(8,128)S(1)}, f32[2,144,128]{2,1,0:T(8,128)S(1)}, f32[2,144,128]{2,1,0:T(8,128)S(1)}, f32[2,144,128]{2,1,0:T(8,128)S(1)}...) custom-call(s32[4]{0:T(128)S(1)} %pad_add_fusion.info, ...), custom_call_target="tpu_custom_call" | custom-call | tf_op jit(solution)/shard_map/pack_blocks/pallas_call | solution.py:256
  8.7 2.1 %collective-permute-start.9 = (f32[2,144,128]{2,1,0:T(8,128)S(1)}, f32[2,144,128]{2,1,0:T(8,128)S(1)}, u32[]{:S(2)}, u32[]{:S(2)}) collective-permute-start(f32[2,144,128]{2,1,0:T(8,128)S(1)} %get-tuple-element.31), channel_id=1, source_target_pairs={{0,4},{2,6},{4,0},{6,2},{8,12},{10,14},{12,8},{14,10},{16,20},{18,... | collective-permute-start | bytes 442376 | tf_op jit(solution)/shard_map/ppermute | solution.py:289
  10.9 1.8 %collective-permute-start.11 = (f32[2,144,128]{2,1,0:T(8,128)S(1)}, f32[2,144,128]{2,1,0:T(8,128)S(1)}, u32[]{:S(2)}, u32[]{:S(2)}) collective-permute-start(f32[2,144,128]{2,1,0:T(8,128)S(1)} %get-tuple-element.33), channel_id=1, source_target_pairs={{0,8},{2,10},{4,12},{6,14},{8,0},{10,2},{12,4},{14,6},{16,24},{18,... | collective-permute-start | bytes 442376 | tf_op jit(solution)/shard_map/ppermute | solution.py:289
  12.7 2.6 %collective-permute-start.13 = (f32[2,144,128]{2,1,0:T(8,128)S(1)}, f32[2,144,128]{2,1,0:T(8,128)S(1)}, u32[]{:S(2)}, u32[]{:S(2)}) collective-permute-start(f32[2,144,128]{2,1,0:T(8,128)S(1)} %get-tuple-element.35), channel_id=1, source_target_pairs={{0,12},{2,14},{4,8},{6,10},{8,4},{10,6},{12,0},{14,2},{16,28},{18,... | collective-permute-start | bytes 442376 | tf_op jit(solution)/shard_map/ppermute | solution.py:289
  15.5 1.8 %collective-permute-start.14 = (f32[2,144,128]{2,1,0:T(8,128)S(1)}, f32[2,144,128]{2,1,0:T(8,128)S(1)}, u32[]{:S(2)}, u32[]{:S(2)}) collective-permute-start(f32[2,144,128]{2,1,0:T(8,128)S(1)} %get-tuple-element.36), channel_id=1, source_target_pairs={{0,14},{2,12},{4,10},{6,8},{8,6},{10,4},{12,2},{14,0},{16,30},{18,... | collective-permute-start | bytes 442376 | tf_op jit(solution)/shard_map/ppermute | solution.py:289
  17.3 0.9 %collective-permute-done.10.refs_3_ = f32[2,144,128]{2,1,0:T(8,128)S(1)} collective-permute-done((f32[2,144,128]{2,1,0:T(8,128)S(1)}, f32[2,144,128]{2,1,0:T(8,128)S(1)}, u32[]{:S(2)}, u32[]{:S(2)}) %collective-permute-start.10) | collective-permute-done | bytes 147488 | tf_op jit(solution)/shard_map/ppermute | solution.py:289
  18.6 1.7 %collective-permute-start.2 = (f32[2,144,128]{2,1,0:T(8,128)S(1)}, f32[2,144,128]{2,1,0:T(8,128)S(1)}, u32[]{:S(2)}, u32[]{:S(2)}) collective-permute-start(f32[2,144,128]{2,1,0:T(8,128)S(1)} %get-tuple-element.23), channel_id=1, source_target_pairs={{0,4},{2,6},{4,0},{6,2},{8,12},{10,14},{12,8},{14,10},{16,20},{18,... | collective-permute-start | bytes 442376 | tf_op jit(solution)/shard_map/ppermute | solution.py:289
  20.3 1.9 %collective-permute-start.3 = (f32[2,144,128]{2,1,0:T(8,128)S(1)}, f32[2,144,128]{2,1,0:T(8,128)S(1)}, u32[]{:S(2)}, u32[]{:S(2)}) collective-permute-start(f32[2,144,128]{2,1,0:T(8,128)S(1)} %get-tuple-element.24), channel_id=1, source_target_pairs={{0,6},{2,4},{4,2},{6,0},{8,14},{10,12},{12,10},{14,8},{16,22},{18,... | collective-permute-start | bytes 442376 | tf_op jit(solution)/shard_map/ppermute | solution.py:289
  22.2 3.0 %collective-permute-done.13.refs_6_ = f32[2,144,128]{2,1,0:T(8,128)S(1)} collective-permute-done((f32[2,144,128]{2,1,0:T(8,128)S(1)}, f32[2,144,128]{2,1,0:T(8,128)S(1)}, u32[]{:S(2)}, u32[]{:S(2)}) %collective-permute-start.13) | collective-permute-done | bytes 147488 | tf_op jit(solution)/shard_map/ppermute | solution.py:289
  25.1 1.6 %collective-permute-start.4 = (f32[2,144,128]{2,1,0:T(8,128)S(1)}, f32[2,144,128]{2,1,0:T(8,128)S(1)}, u32[]{:S(2)}, u32[]{:S(2)}) collective-permute-start(f32[2,144,128]{2,1,0:T(8,128)S(1)} %get-tuple-element.25), channel_id=1, source_target_pairs={{0,8},{2,10},{4,12},{6,14},{8,0},{10,2},{12,4},{14,6},{16,24},{18,... | collective-permute-start | bytes 442376 | tf_op jit(solution)/shard_map/ppermute | solution.py:289
  26.7 0.4 collective-permute-done.14.refs_7_
  27.2 0.6 %pick_boundary.1 = f32[4,144,128]{2,1,0:T(8,128)S(1)} custom-call(s32[4]{0:T(128)S(1)} %pad_add_fusion.info, f32[2,144,128]{2,1,0:T(8,128)S(1)} %get-tuple-element.29.refs_0_, f32[2,144,128]{2,1,0:T(8,128)S(1)} %collective-permute-done.8.refs_1_, f32[2,144,128]{2,1,0:T(8,128)S(1)} %collective-permute-done.9.refs_2_, ...), custom_call_target="tpu_custom_call" | custom-call | tf_op jit(solution)/shard_map/pick_boundary/pallas_call | solution.py:295
  27.8 2.7 %collective-permute-start.15 = (f32[4,144,128]{2,1,0:T(8,128)S(1)}, f32[4,144,128]{2,1,0:T(8,128)S(1)}, u32[]{:S(2)}, u32[]{:S(2)}) collective-permute-start(f32[4,144,128]{2,1,0:T(8,128)S(1)} %pick_boundary.1), channel_id=1, source_target_pairs={{0,16},{2,18},{4,20},{6,22},{8,24},{10,26},{12,28},{14,30},{16,0},... | collective-permute-start | bytes 884744 | tf_op jit(solution)/shard_map/ppermute | solution.py:289
  30.5 3.8 %render_first.1 = f32[4,128,128]{2,1,0:T(8,128)S(1)} custom-call(s32[4]{0:T(128)S(1)} %pad_add_fusion.info, bf16[512,256]{1,0:T(8,128)(2,1)S(1)} %copy-done.2, f32[2,144,128]{2,1,0:T(8,128)S(1)} %get-tuple-element.29.refs_0_, f32[2,144,128]{2,1,0:T(8,128)S(1)} %collective-permute-done.8.refs_1_, f32[2,144,128]{2,1,0:T(8,128)S(1)} %collective-permute-done.9.refs_2_, ...), custom_call_target="tpu_custom_call" | custom-call | flops 5000000000 | bytes 2000000 | tf_op jit(solution)/shard_map/render_first/pallas_call | solution.py:296
  34.7 1.6 %collective-permute-start.5 = (f32[2,144,128]{2,1,0:T(8,128)S(1)}, f32[2,144,128]{2,1,0:T(8,128)S(1)}, u32[]{:S(2)}, u32[]{:S(2)}) collective-permute-start(f32[2,144,128]{2,1,0:T(8,128)S(1)} %get-tuple-element.26), channel_id=1, source_target_pairs={{0,10},{2,8},{4,14},{6,12},{8,2},{10,0},{12,6},{14,4},{16,26},{18,... | collective-permute-start | bytes 442376 | tf_op jit(solution)/shard_map/ppermute | solution.py:289
  36.2 2.4 %collective-permute-start.7 = (f32[2,144,128]{2,1,0:T(8,128)S(1)}, f32[2,144,128]{2,1,0:T(8,128)S(1)}, u32[]{:S(2)}, u32[]{:S(2)}) collective-permute-start(f32[2,144,128]{2,1,0:T(8,128)S(1)} %get-tuple-element.28), channel_id=1, source_target_pairs={{0,14},{2,12},{4,10},{6,8},{8,6},{10,4},{12,2},{14,0},{16,30},{18,... | collective-permute-start | bytes 442376 | tf_op jit(solution)/shard_map/ppermute | solution.py:289
  38.6 8.1 %collective-permute-done.5.refs_5_ = f32[2,144,128]{2,1,0:T(8,128)S(1)} collective-permute-done((f32[2,144,128]{2,1,0:T(8,128)S(1)}, f32[2,144,128]{2,1,0:T(8,128)S(1)}, u32[]{:S(2)}, u32[]{:S(2)}) %collective-permute-start.5) | collective-permute-done | bytes 147488 | tf_op jit(solution)/shard_map/ppermute | solution.py:289
  46.7 3.2 %collective-permute-done.6.refs_6_ = f32[2,144,128]{2,1,0:T(8,128)S(1)} collective-permute-done((f32[2,144,128]{2,1,0:T(8,128)S(1)}, f32[2,144,128]{2,1,0:T(8,128)S(1)}, u32[]{:S(2)}, u32[]{:S(2)}) %collective-permute-start.6) | collective-permute-done | bytes 147488 | tf_op jit(solution)/shard_map/ppermute | solution.py:289
  49.8 8.0 %collective-permute-done.7.refs_7_ = f32[2,144,128]{2,1,0:T(8,128)S(1)} collective-permute-done((f32[2,144,128]{2,1,0:T(8,128)S(1)}, f32[2,144,128]{2,1,0:T(8,128)S(1)}, u32[]{:S(2)}, u32[]{:S(2)}) %collective-permute-start.7) | collective-permute-done | bytes 147488 | tf_op jit(solution)/shard_map/ppermute | solution.py:289
  57.8 5.4 %render_last.1 = f32[4,128,128]{2,1,0:T(8,128)} custom-call(s32[4]{0:T(128)S(1)} %pad_add_fusion.info, bf16[512,256]{1,0:T(8,128)(2,1)S(1)} %copy-done.2, f32[2,144,128]{2,1,0:T(8,128)S(1)} %get-tuple-element.21.refs_0_, f32[2,144,128]{2,1,0:T(8,128)S(1)} %collective-permute-done.1.refs_1_, f32[2,144,128]{2,1,0:T(8,128)S(1)} %collective-permute-done.2.refs_2_, ...), custom_call_target="tpu_custom_call" | custom-call | flops 5000000000 | bytes 2000000 | tf_op jit(solution)/shard_map/render_last/pallas_call | solution.py:298
  (22 shorter events, 1.3 us)
Async XLA Ops:
  0.0 1.6 %copy-start = (f32[2,2048,128]{2,1,0:T(8,128)S(1)}, f32[2,2048,128]{2,1,0:T(8,128)}, u32[]{:S(2)}) copy-start(f32[2,2048,128]{2,1,0:T(8,128)} %field.3) | copy-start | bytes 6291460
  1.6 5.9 %copy-start.1 = (f32[2,2048,128]{2,1,0:T(8,128)S(1)}, f32[2,2048,128]{2,1,0:T(8,128)}, u32[]{:S(2)}) copy-start(f32[2,2048,128]{2,1,0:T(8,128)} %field.3) | copy-start | bytes 6291460
  2.3 28.2 %copy-start.2 = (bf16[512,256]{1,0:T(8,128)(2,1)S(1)}, bf16[512,256]{1,0:T(8,128)(2,1)}, u32[]{:S(2)}) copy-start(bf16[512,256]{1,0:T(8,128)(2,1)} %constant.38.clone.weights) | copy-start | bytes 786436
  2.3 5.2 %collective-permute-start = (f32[1,128,128]{2,1,0:T(8,128)S(1)}, f32[1,128,128]{2,1,0:T(8,128)S(1)}, u32[]{:S(2)}, u32[]{:S(2)}) collective-permute-start(f32[1,128,128]{2,1,0:T(8,128)S(1)} %edge_columns.1), channel_id=1, source_target_pairs={{0,1},{1,0},{2,3},{3,2},{4,5},{5,4},{6,7},{7,6},{8,9},{9,8},{10,11... | collective-permute-start | bytes 196616 | tf_op jit(solution)/shard_map/ppermute | solution.py:252
  8.6 4.1 %collective-permute-start.8 = (f32[2,144,128]{2,1,0:T(8,128)S(1)}, f32[2,144,128]{2,1,0:T(8,128)S(1)}, u32[]{:S(2)}, u32[]{:S(2)}) collective-permute-start(f32[2,144,128]{2,1,0:T(8,128)S(1)} %get-tuple-element.30), channel_id=1, source_target_pairs={{0,2},{2,0},{4,6},{6,4},{8,10},{10,8},{12,14},{14,12},{16,18},{18,... | collective-permute-start | bytes 442376 | tf_op jit(solution)/shard_map/ppermute | solution.py:289
  8.7 6.8 %collective-permute-start.9 = (f32[2,144,128]{2,1,0:T(8,128)S(1)}, f32[2,144,128]{2,1,0:T(8,128)S(1)}, u32[]{:S(2)}, u32[]{:S(2)}) collective-permute-start(f32[2,144,128]{2,1,0:T(8,128)S(1)} %get-tuple-element.31), channel_id=1, source_target_pairs={{0,4},{2,6},{4,0},{6,2},{8,12},{10,14},{12,8},{14,10},{16,20},{18,... | collective-permute-start | bytes 442376 | tf_op jit(solution)/shard_map/ppermute | solution.py:289
  10.8 7.3 %collective-permute-start.10 = (f32[2,144,128]{2,1,0:T(8,128)S(1)}, f32[2,144,128]{2,1,0:T(8,128)S(1)}, u32[]{:S(2)}, u32[]{:S(2)}) collective-permute-start(f32[2,144,128]{2,1,0:T(8,128)S(1)} %get-tuple-element.32), channel_id=1, source_target_pairs={{0,6},{2,4},{4,2},{6,0},{8,14},{10,12},{12,10},{14,8},{16,22},{18,... | collective-permute-start | bytes 442376 | tf_op jit(solution)/shard_map/ppermute | solution.py:289
  10.9 7.7 %collective-permute-start.11 = (f32[2,144,128]{2,1,0:T(8,128)S(1)}, f32[2,144,128]{2,1,0:T(8,128)S(1)}, u32[]{:S(2)}, u32[]{:S(2)}) collective-permute-start(f32[2,144,128]{2,1,0:T(8,128)S(1)} %get-tuple-element.33), channel_id=1, source_target_pairs={{0,8},{2,10},{4,12},{6,14},{8,0},{10,2},{12,4},{14,6},{16,24},{18,... | collective-permute-start | bytes 442376 | tf_op jit(solution)/shard_map/ppermute | solution.py:289
  12.7 7.6 %collective-permute-start.12 = (f32[2,144,128]{2,1,0:T(8,128)S(1)}, f32[2,144,128]{2,1,0:T(8,128)S(1)}, u32[]{:S(2)}, u32[]{:S(2)}) collective-permute-start(f32[2,144,128]{2,1,0:T(8,128)S(1)} %get-tuple-element.34), channel_id=1, source_target_pairs={{0,10},{2,8},{4,14},{6,12},{8,2},{10,0},{12,6},{14,4},{16,26},{18,... | collective-permute-start | bytes 442376 | tf_op jit(solution)/shard_map/ppermute | solution.py:289
  12.7 12.4 %collective-permute-start.13 = (f32[2,144,128]{2,1,0:T(8,128)S(1)}, f32[2,144,128]{2,1,0:T(8,128)S(1)}, u32[]{:S(2)}, u32[]{:S(2)}) collective-permute-start(f32[2,144,128]{2,1,0:T(8,128)S(1)} %get-tuple-element.35), channel_id=1, source_target_pairs={{0,12},{2,14},{4,8},{6,10},{8,4},{10,6},{12,0},{14,2},{16,28},{18,... | collective-permute-start | bytes 442376 | tf_op jit(solution)/shard_map/ppermute | solution.py:289
  15.5 11.6 %collective-permute-start.14 = (f32[2,144,128]{2,1,0:T(8,128)S(1)}, f32[2,144,128]{2,1,0:T(8,128)S(1)}, u32[]{:S(2)}, u32[]{:S(2)}) collective-permute-start(f32[2,144,128]{2,1,0:T(8,128)S(1)} %get-tuple-element.36), channel_id=1, source_target_pairs={{0,14},{2,12},{4,10},{6,8},{8,6},{10,4},{12,2},{14,0},{16,30},{18,... | collective-permute-start | bytes 442376 | tf_op jit(solution)/shard_map/ppermute | solution.py:289
  18.2 16.1 %collective-permute-start.1 = (f32[2,144,128]{2,1,0:T(8,128)S(1)}, f32[2,144,128]{2,1,0:T(8,128)S(1)}, u32[]{:S(2)}, u32[]{:S(2)}) collective-permute-start(f32[2,144,128]{2,1,0:T(8,128)S(1)} %get-tuple-element.22), channel_id=1, source_target_pairs={{0,2},{2,0},{4,6},{6,4},{8,10},{10,8},{12,14},{14,12},{16,18},{18,... | collective-permute-start | bytes 442376 | tf_op jit(solution)/shard_map/ppermute | solution.py:289
  18.6 16.1 %collective-permute-start.2 = (f32[2,144,128]{2,1,0:T(8,128)S(1)}, f32[2,144,128]{2,1,0:T(8,128)S(1)}, u32[]{:S(2)}, u32[]{:S(2)}) collective-permute-start(f32[2,144,128]{2,1,0:T(8,128)S(1)} %get-tuple-element.23), channel_id=1, source_target_pairs={{0,4},{2,6},{4,0},{6,2},{8,12},{10,14},{12,8},{14,10},{16,20},{18,... | collective-permute-start | bytes 442376 | tf_op jit(solution)/shard_map/ppermute | solution.py:289
  20.3 15.9 %collective-permute-start.3 = (f32[2,144,128]{2,1,0:T(8,128)S(1)}, f32[2,144,128]{2,1,0:T(8,128)S(1)}, u32[]{:S(2)}, u32[]{:S(2)}) collective-permute-start(f32[2,144,128]{2,1,0:T(8,128)S(1)} %get-tuple-element.24), channel_id=1, source_target_pairs={{0,6},{2,4},{4,2},{6,0},{8,14},{10,12},{12,10},{14,8},{16,22},{18,... | collective-permute-start | bytes 442376 | tf_op jit(solution)/shard_map/ppermute | solution.py:289
  25.1 11.1 %collective-permute-start.4 = (f32[2,144,128]{2,1,0:T(8,128)S(1)}, f32[2,144,128]{2,1,0:T(8,128)S(1)}, u32[]{:S(2)}, u32[]{:S(2)}) collective-permute-start(f32[2,144,128]{2,1,0:T(8,128)S(1)} %get-tuple-element.25), channel_id=1, source_target_pairs={{0,8},{2,10},{4,12},{6,14},{8,0},{10,2},{12,4},{14,6},{16,24},{18,... | collective-permute-start | bytes 442376 | tf_op jit(solution)/shard_map/ppermute | solution.py:289
  27.8 30.0 %collective-permute-start.15 = (f32[4,144,128]{2,1,0:T(8,128)S(1)}, f32[4,144,128]{2,1,0:T(8,128)S(1)}, u32[]{:S(2)}, u32[]{:S(2)}) collective-permute-start(f32[4,144,128]{2,1,0:T(8,128)S(1)} %pick_boundary.1), channel_id=1, source_target_pairs={{0,16},{2,18},{4,20},{6,22},{8,24},{10,26},{12,28},{14,30},{16,0},... | collective-permute-start | bytes 884744 | tf_op jit(solution)/shard_map/ppermute | solution.py:289
  34.3 23.6 %collective-permute-start.16 = (f32[4,128,128]{2,1,0:T(8,128)S(1)}, f32[4,128,128]{2,1,0:T(8,128)S(1)}, u32[]{:S(2)}, u32[]{:S(2)}) collective-permute-start(f32[4,128,128]{2,1,0:T(8,128)S(1)} %render_first.1), channel_id=1, source_target_pairs={{0,16},{2,18},{4,20},{6,22},{8,24},{10,26},{12,28},{14,30},{16,0},... | collective-permute-start | bytes 786440 | tf_op jit(solution)/shard_map/ppermute | solution.py:289
  34.7 12.0 %collective-permute-start.5 = (f32[2,144,128]{2,1,0:T(8,128)S(1)}, f32[2,144,128]{2,1,0:T(8,128)S(1)}, u32[]{:S(2)}, u32[]{:S(2)}) collective-permute-start(f32[2,144,128]{2,1,0:T(8,128)S(1)} %get-tuple-element.26), channel_id=1, source_target_pairs={{0,10},{2,8},{4,14},{6,12},{8,2},{10,0},{12,6},{14,4},{16,26},{18,... | collective-permute-start | bytes 442376 | tf_op jit(solution)/shard_map/ppermute | solution.py:289
  36.2 13.6 %collective-permute-start.6 = (f32[2,144,128]{2,1,0:T(8,128)S(1)}, f32[2,144,128]{2,1,0:T(8,128)S(1)}, u32[]{:S(2)}, u32[]{:S(2)}) collective-permute-start(f32[2,144,128]{2,1,0:T(8,128)S(1)} %get-tuple-element.27), channel_id=1, source_target_pairs={{0,12},{2,14},{4,8},{6,10},{8,4},{10,6},{12,0},{14,2},{16,28},{18,... | collective-permute-start | bytes 442376 | tf_op jit(solution)/shard_map/ppermute | solution.py:289
  36.2 21.6 %collective-permute-start.7 = (f32[2,144,128]{2,1,0:T(8,128)S(1)}, f32[2,144,128]{2,1,0:T(8,128)S(1)}, u32[]{:S(2)}, u32[]{:S(2)}) collective-permute-start(f32[2,144,128]{2,1,0:T(8,128)S(1)} %get-tuple-element.28), channel_id=1, source_target_pairs={{0,14},{2,12},{4,10},{6,8},{8,6},{10,4},{12,2},{14,0},{16,30},{18,... | collective-permute-start | bytes 442376 | tf_op jit(solution)/shard_map/ppermute | solution.py:289

commit v3 on v2

--- a/solution.py
+++ b/solution.py
@@ -115,22 +115,22 @@
 
 
 def render_kernel(size, last, info, weights, *refs):
-    blocks, refs = refs[:size], refs[size:]
+    blocks, refs = refs[: size // 2], refs[size // 2 :]
     if last:
         boundary, other, image, sx, dx = refs
     else:
         image, sx, dx = refs
     depth, own = blocks[0].shape[0], image.shape[1]
-    planes = depth * size
+    planes = depth * (size // 2)
     extra = 4 if last else 0
-    pos, front = info[0], info[1]
+    chip, front = info[0], info[2]
     start = 2 * front + extra * (1 - front)
     empty = (1 - front) * (planes + extra)
     sx[pl.ds(empty, 2)] = jnp.zeros((2,) + sx.shape[1:], jnp.float32)
     dx[pl.ds(empty, 2)] = jnp.zeros((2,) + dx.shape[1:], jnp.float32)
-    for step in range(size):
+    for step in range(size // 2):
         for plane in range(depth):
-            slot = (pos ^ step) * depth + plane + start
+            slot = (chip ^ step) * depth + plane + start
             filter_columns(blocks[step], plane, own, weights, sx, dx, slot)
     for plane in range(extra):
         slot = (planes + 2) * front + plane
@@ -151,7 +151,7 @@
             image[channel, pl.ds(first, TILE), :] = total[channel]
 
 
-def edge_kernel(field, out):
+def edge_columns(field, out):
     depth, height, width = field.shape
     lane = lax.broadcasted_iota(jnp.int32, (LANES, width), 1)
     count = depth * height // LANES
@@ -165,51 +165,79 @@
         out[base // (LANES // 4)] = jnp.transpose(packed)
 
 
-def pack_kernel(size, info, field, before, after, *refs):
-    outs, sides = refs[:-1], refs[-1]
+def rows_around(field, plane, target, own):
+    height, width = field.shape[1:]
+    line = lax.broadcasted_iota(jnp.int32, (8, width), 0)
+    start = target * own
+    above = pl.multiple_of(jnp.maximum(start - 8, 0), 8)
+    below = pl.multiple_of(jnp.minimum(start + own, height - 8), 8)
+    top = jnp.where(target > 0, pltpu.roll(field[plane, pl.ds(above, 8), :], 2, 0), 0.0)
+    end = jnp.where(start + own < height, pltpu.roll(field[plane, pl.ds(below, 8), :], 2, 0), 0.0)
+    return jnp.where(line < 2, top, jnp.where(line < 4, end, 0.0))
+
+
+def targets(size, info):
+    chip, core, front = info[0], info[1], info[2]
+    for chunk in range(2):
+        base = front * size if chunk == 0 else (1 - front) * size
+        for step in range(size // 2):
+            yield chunk * (size // 2) + step, base + 2 * (chip ^ step), core
+
+
+def share_kernel(size, info, field, edges, share):
+    own = share.shape[2] - 8
+    edge_columns(field, edges)
+    for index, target, core in targets(size, info):
+        target = target + 1 - core
+        for plane in range(field.shape[0]):
+            start = pl.multiple_of(target * own, 8)
+            share[index, plane, 0:own, :] = field[plane, pl.ds(start, own), :]
+            share[index, plane, own : own + 8, :] = rows_around(field, plane, target, own)
+
+
+def pack_kernel(size, info, field, shared, *refs):
+    edges, outs, sides = refs[:4], refs[4:-1], refs[-1]
     depth, height, width = field.shape
     own = outs[0].shape[1] - 16
-    groups = height // own
-    pos, front = info[0], info[1]
-    row = lax.broadcasted_iota(jnp.int32, before.shape, 1) % 4
-    left = jnp.where(info[2] == 1, before[...], 0.0)
-    right = jnp.where(info[3] == 1, after[...], 0.0)
-    sides[...] = jnp.where(row < 2, left, right).reshape(sides.shape)
+    row = lax.broadcasted_iota(jnp.int32, edges[0].shape, 1) % 4
+    for which in range(2):
+        left = jnp.where(info[3] == 1, edges[2 * which][...], 0.0)
+        right = jnp.where(info[4] == 1, edges[2 * which + 1][...], 0.0)
+        sides[which] = jnp.where(row < 2, left, right).reshape(sides.shape[1:])
     lane = lax.broadcasted_iota(jnp.int32, (4, LANES), 1)
-    line = lax.broadcasted_iota(jnp.int32, (8, width), 0)
-
-    def side_rows(plane, at, to):
-        chunk = sides[pl.ds(plane * (4 * height // LANES) + at // LANES * 4, 4), :]
+
+    def side_rows(which, plane, at, to):
+        chunk = sides[which, pl.ds(plane * (4 * height // LANES) + at // LANES * 4, 4), :]
         return pltpu.roll(chunk, (to + LANES - at % LANES) % LANES, 1)
 
-    for chunk in range(2):
-        base = front * size if chunk == 0 else (1 - front) * size
-        for step in range(size):
-            out = outs[chunk * size + step]
-            target = base + (pos ^ step)
-            start = pl.multiple_of(target * own, 8)
-            inner_top, inner_end = target > 0, target < groups - 1
-            above = pl.multiple_of(jnp.maximum(start - 8, 0), 8)
-            below = pl.multiple_of(jnp.minimum(start + own, height - 8), 8)
+    for index, target, core in targets(size, info):
+        out = outs[index]
+        target = target + core
+        start = pl.multiple_of(target * own, 8)
+        for which in range(2):
             for plane in range(depth):
-                out[plane, 0:own, :] = field[plane, pl.ds(start, own), :]
-                top = jnp.where(inner_top, pltpu.roll(field[plane, pl.ds(above, 8), :], 2, 0), 0.0)
-                end = jnp.where(inner_end, pltpu.roll(field[plane, pl.ds(below, 8), :], 2, 0), 0.0)
-                out[plane, own : own + 8, :] = jnp.where(line < 2, top, jnp.where(line < 4, end, 0.0))
-                top = jnp.where(inner_top, side_rows(plane, jnp.maximum(start - 2, 0), 0), 0.0)
-                end = jnp.where(inner_end, side_rows(plane, jnp.minimum(start + own, height - 2), 2), 0.0)
-                out[plane, own + 8 : own + 12, :] = side_rows(plane, start, 0)
-                out[plane, own + 12 : own + 16, :] = jnp.where(lane < 2, top, end)
+                slot = (core if which == 0 else 1 - core) * depth + plane
+                if which == 0:
+                    out[slot, 0:own, :] = field[plane, pl.ds(start, own), :]
+                    out[slot, own : own + 8, :] = rows_around(field, plane, target, own)
+                else:
+                    out[slot, 0 : own + 8, :] = shared[index, plane]
+                top = side_rows(which, plane, jnp.maximum(start - 2, 0), 0)
+                end = side_rows(which, plane, jnp.minimum(start + own, height - 2), 2)
+                top = jnp.where(target > 0, top, 0.0)
+                end = jnp.where(start + own < height, end, 0.0)
+                out[slot, own + 8 : own + 12, :] = side_rows(which, plane, start, 0)
+                out[slot, own + 12 : own + 16, :] = jnp.where(lane < 2, top, end)
 
 
 def pick_kernel(size, info, *refs):
-    blocks, out = refs[:size], refs[size]
+    blocks, out = refs[:-1], refs[-1]
     depth = blocks[0].shape[0]
-    pos, front = info[0], info[1]
+    chip, front = info[0], info[2]
     count = 4 // depth
     for part in range(count):
-        wanted = pos ^ (front * (size - count) + part)
-        for step in range(size):
+        wanted = chip ^ (front * (size // 2 - count) + part)
+        for step in range(size // 2):
 
             @pl.when(wanted == step)
             def _():
@@ -234,41 +262,57 @@
     me = lax.axis_index("depth")
     column = lax.axis_index("cols")
     has_left, has_right = column > 0, column < columns - 1
-    info = jnp.stack([me % size, 1 - me // size, has_left, has_right]).astype(jnp.int32)
+    info = jnp.stack([me % size // 2, me % 2, 1 - me // size, has_left, has_right]).astype(jnp.int32)
     weights = jnp.asarray(column_weights(width))
     f32 = jnp.float32
-    block = jax.ShapeDtypeStruct((depth, own + 16, width), f32)
+    block = jax.ShapeDtypeStruct((2 * depth, own + 16, width), f32)
     image = jax.ShapeDtypeStruct((4, own, width), f32)
-
-    edges = pl.pallas_call(
-        edge_kernel,
-        out_shape=jax.ShapeDtypeStruct((-(-depth * height // LANES // (LANES // 4)), LANES, LANES), f32),
-        in_specs=[VMEM],
-        out_specs=VMEM,
+    edge_groups = -(-depth * height // LANES // (LANES // 4))
+
+    edges, share = pl.pallas_call(
+        functools.partial(share_kernel, size),
+        out_shape=(
+            jax.ShapeDtypeStruct((edge_groups, LANES, LANES), f32),
+            jax.ShapeDtypeStruct((size, depth, own + 8, width), f32),
+        ),
+        in_specs=[SMEM, VMEM],
+        out_specs=(VMEM, VMEM),
         compiler_params=PARAMS,
-        name="edge_columns",
-    )(field)
-    if columns == 2:
-        before = after = lax.ppermute(edges, "cols", [(0, 1), (1, 0)])
-    else:
-        before = lax.ppermute(edges, "cols", [(i, i + 1) for i in range(columns - 1)])
-        after = lax.ppermute(edges, "cols", [(i + 1, i) for i in range(columns - 1)])
+        name="share_with_core",
+    )(info, field)
+    shared = lax.ppermute(share, "depth", [(i, i ^ 1) for i in range(groups)])
+
+    def from_column(flip, shifts):
+        route = []
+        for i in range(groups):
+            for j in range(columns):
+                for shift in shifts:
+                    if 0 <= j + shift < columns:
+                        route.append((i * columns + j, (i ^ flip) * columns + j + shift))
+        return lax.ppermute(edges, ("depth", "cols"), route)
+
+    sides = []
+    for flip in range(2):
+        if columns == 2:
+            sides += [from_column(flip, (-1, 1))] * 2
+        else:
+            sides += [from_column(flip, (1,)), from_column(flip, (-1,))]
     blocks = pl.pallas_call(
         functools.partial(pack_kernel, size),
-        out_shape=(block,) * (2 * size),
-        in_specs=[SMEM] + [VMEM] * 3,
-        out_specs=(VMEM,) * (2 * size),
-        scratch_shapes=[pltpu.VMEM((edges.shape[0] * LANES, LANES), f32)],
+        out_shape=(block,) * size,
+        in_specs=[SMEM] + [VMEM] * 6,
+        out_specs=(VMEM,) * size,
+        scratch_shapes=[pltpu.VMEM((2, edge_groups * LANES, LANES), f32)],
         compiler_params=PARAMS,
         name="pack_blocks",
-    )(info, field, before, after)
+    )(info, field, shared, *sides)
 
     def render_call(last):
         count = depth * size + (6 if last else 2)
         return pl.pallas_call(
             functools.partial(render_kernel, size, last),
             out_shape=image,
-            in_specs=[SMEM] + [VMEM] * (size + (3 if last else 1)),
+            in_specs=[SMEM] + [VMEM] * (size // 2 + (3 if last else 1)),
             out_specs=VMEM,
             scratch_shapes=[pltpu.VMEM((count, own + 16, width), f32)] * 2,
             compiler_params=PARAMS,
@@ -279,7 +323,7 @@
     pick = pl.pallas_call(
         functools.partial(pick_kernel, size),
         out_shape=jax.ShapeDtypeStruct((4,) + block.shape[1:], f32),
-        in_specs=[SMEM] + [VMEM] * size,
+        in_specs=[SMEM] + [VMEM] * (size // 2),
         out_specs=VMEM,
         compiler_params=PARAMS,
         name="pick_boundary",
@@ -289,12 +333,12 @@
         return lax.ppermute(x, "depth", [(i, i ^ bits) for i in range(groups)])
 
     def gathered(mine):
-        return [mine[0]] + [swap(mine[step], step) for step in range(1, size)]
-
-    theirs = gathered(blocks[:size])
+        return [mine[0]] + [swap(mine[step], 2 * step) for step in range(1, size // 2)]
+
+    theirs = gathered(blocks[: size // 2])
     boundary = swap(pick(info, *theirs), size)
     image_part = swap(render_call(False)(info, weights, *theirs), size)
-    mine = gathered(blocks[size:])
+    mine = gathered(blocks[size // 2 :])
     return render_call(True)(info, weights, *mine, boundary, image_part)
 
 

time: 63.3 us -> 60.5 us (0.956)
  starting transfers between devices: 24 us -> 15.4 us
  waiting for transfers between devices: 25.9 us -> 31.3 us
    ppermute x16 -> x8, starting transfers between devices: 21 us -> 12.2 us  [swap(): return lax.ppermute(x, 'depth', [(i, i ^ bits) for i in range(groups)])]
    ppermute x16 -> x8, waiting for transfers between devices: 23.7 us -> 27.1 us  [swap(): return lax.ppermute(x, 'depth', [(i, i ^ bits) for i in range(groups)])]
    ppermute x1 -> x3, waiting for transfers between devices: 2.17 us -> 4.23 us  [the longest x2 4.22 us: from_column(): return lax.ppermute(edges, ('depth', 'cols'), route)]
    ppermute x1 -> x3, starting transfers between devices: 3 us -> 3.17 us  [the longest x2 2.66 us: from_column(): return lax.ppermute(edges, ('depth', 'cols'), route)]
    unnamed x6 -> x4, local copies, waits for them, and re-layouts: 1.6 us -> 1.6 us
  transfers between devices with their start and end apart: 17 -> 11, of which waited for: 8 -> 7; matrix products, arithmetic and copies ran while one was open for 0% -> 0% of each run, Pallas kernels for 7% -> 7%
where the time goes in v3:
time: 60.5 us; the launch traced here: 60.3 us
  waiting for transfers between devices  31.3 us (52%)
  starting transfers between devices  15.4 us (25%)
  Pallas kernels  11.9 us (20%)
  local copies, waits for them, and re-layouts  1.68 us (3%)
    ppermute x8, waiting for transfers between devices, swap(): return lax.ppermute(x, 'depth', [(i, i ^ bits) for i in range(groups)])  27.1 us
    ppermute x8, starting transfers between devices, swap(): return lax.ppermute(x, 'depth', [(i, i ^ bits) for i in range(groups)])  12.2 us
    pallas_call x1, Pallas kernels, local(): return render_call(True)(info, weights, *mine, boundary, image_part)  5.31 us
    ppermute x2, waiting for transfers between devices, from_column(): return lax.ppermute(edges, ('depth', 'cols'), route)  4.22 us
    pallas_call x1, Pallas kernels, local(): image_part = swap(render_call(False)(info, weights, *theirs), size)  3.77 us
    ppermute x2, starting transfers between devices, from_column(): return lax.ppermute(edges, ('depth', 'cols'), route)  2.66 us
    unnamed x4, local copies, waits for them, and re-layouts  1.6 us
    pallas_call x1, Pallas kernels, local(): pl.pallas_call(functools.partial(share_kernel, size), out_shape=(jax.Shap...  1.29 us
  transfers between devices with their start and end apart: 11, of which 7 were waited for; matrix products, arithmetic and copies ran while one was open for 0% of the time, Pallas kernels for 7%

profile of v3, /device:TPU:0, one launch (start us, length us, event | category | flops | bytes accessed | tf_op | source)
XLA Modules:
  0.0 60.3 jit_solution(17823395248980479007)
XLA Ops:
  0.0 0.1 stack.31.info
  0.1 1.6 %copy-done = f32[2,2048,128]{2,1,0:T(8,128)S(1)} copy-done((f32[2,2048,128]{2,1,0:T(8,128)S(1)}, f32[2,2048,128]{2,1,0:T(8,128)}, u32[]{:S(2)}) %copy-start) | copy-done | bytes 2097176
  1.7 1.3 %share_with_core.1 = (f32[1,128,128]{2,1,0:T(8,128)S(1)}, f32[8,2,136,128]{3,2,1,0:T(8,128)S(1)}) custom-call(s32[5]{0:T(128)S(1)} %stack.31.info, f32[2,2048,128]{2,1,0:T(8,128)S(1)} %copy-done), custom_call_target="tpu_custom_call" | custom-call | tf_op jit(solution)/shard_map/share_with_core/pallas_call | solution.py:272
  3.0 0.5 collective-permute-start
  3.5 2.6 %collective-permute-start.2 = (f32[1,128,128]{2,1,0:T(8,128)S(1)}, f32[1,128,128]{2,1,0:T(8,128)S(1)}, u32[]{:S(2)}, u32[]{:S(2)}) collective-permute-start(f32[1,128,128]{2,1,0:T(8,128)S(1)} %get-tuple-element.16), channel_id=1, source_target_pairs={{0,3},{1,2},{2,1},{3,0},{4,7},{5,6},{6,5},{7,4},{8,11},{9,10},{10,... | collective-permute-start | bytes 196616 | tf_op jit(solution)/shard_map/ppermute | solution.py:292
  6.1 2.4 %collective-permute-done.2.refs_2_.refs_3_ = f32[1,128,128]{2,1,0:T(8,128)S(1)} collective-permute-done((f32[1,128,128]{2,1,0:T(8,128)S(1)}, f32[1,128,128]{2,1,0:T(8,128)S(1)}, u32[]{:S(2)}, u32[]{:S(2)}) %collective-permute-start.2) | collective-permute-done | bytes 65568 | tf_op jit(solution)/shard_map/ppermute | solution.py:292
  8.5 1.8 %collective-permute-done.1.refs_0_.refs_1_ = f32[1,128,128]{2,1,0:T(8,128)S(1)} collective-permute-done((f32[1,128,128]{2,1,0:T(8,128)S(1)}, f32[1,128,128]{2,1,0:T(8,128)S(1)}, u32[]{:S(2)}, u32[]{:S(2)}) %collective-permute-start.1) | collective-permute-done | bytes 65568 | tf_op jit(solution)/shard_map/ppermute | solution.py:292
  10.4 0.9 %pack_blocks.1 = (f32[4,144,128]{2,1,0:T(8,128)S(1)}, f32[4,144,128]{2,1,0:T(8,128)S(1)}, f32[4,144,128]{2,1,0:T(8,128)S(1)}, f32[4,144,128]{2,1,0:T(8,128)S(1)}...) custom-call(s32[5]{0:T(128)S(1)} %stack.31.info, ...), custom_call_target="tpu_custom_call" | custom-call | tf_op jit(solution)/shard_map/pack_blocks/pallas_call | solution.py:300
  11.3 1.6 %collective-permute-start.6 = (f32[4,144,128]{2,1,0:T(8,128)S(1)}, f32[4,144,128]{2,1,0:T(8,128)S(1)}, u32[]{:S(2)}, u32[]{:S(2)}) collective-permute-start(f32[4,144,128]{2,1,0:T(8,128)S(1)} %get-tuple-element.22), channel_id=1, source_target_pairs={{0,4},{2,6},{4,0},{6,2},{8,12},{10,14},{12,8},{14,10},{16,20},{18,... | collective-permute-start | bytes 884744 | tf_op jit(solution)/shard_map/ppermute | solution.py:333
  12.9 1.6 %collective-permute-start.7 = (f32[4,144,128]{2,1,0:T(8,128)S(1)}, f32[4,144,128]{2,1,0:T(8,128)S(1)}, u32[]{:S(2)}, u32[]{:S(2)}) collective-permute-start(f32[4,144,128]{2,1,0:T(8,128)S(1)} %get-tuple-element.23), channel_id=1, source_target_pairs={{0,8},{2,10},{4,12},{6,14},{8,0},{10,2},{12,4},{14,6},{16,24},{18,... | collective-permute-start | bytes 884744 | tf_op jit(solution)/shard_map/ppermute | solution.py:333
  14.5 0.4 collective-permute-start.8
  14.9 1.5 %collective-permute-start.3 = (f32[4,144,128]{2,1,0:T(8,128)S(1)}, f32[4,144,128]{2,1,0:T(8,128)S(1)}, u32[]{:S(2)}, u32[]{:S(2)}) collective-permute-start(f32[4,144,128]{2,1,0:T(8,128)S(1)} %get-tuple-element.18), channel_id=1, source_target_pairs={{0,4},{2,6},{4,0},{6,2},{8,12},{10,14},{12,8},{14,10},{16,20},{18,... | collective-permute-start | bytes 884744 | tf_op jit(solution)/shard_map/ppermute | solution.py:333
  16.4 1.6 %collective-permute-start.4 = (f32[4,144,128]{2,1,0:T(8,128)S(1)}, f32[4,144,128]{2,1,0:T(8,128)S(1)}, u32[]{:S(2)}, u32[]{:S(2)}) collective-permute-start(f32[4,144,128]{2,1,0:T(8,128)S(1)} %get-tuple-element.19), channel_id=1, source_target_pairs={{0,8},{2,10},{4,12},{6,14},{8,0},{10,2},{12,4},{14,6},{16,24},{18,... | collective-permute-start | bytes 884744 | tf_op jit(solution)/shard_map/ppermute | solution.py:333
  18.0 8.2 %collective-permute-done.6.refs_1_ = f32[4,144,128]{2,1,0:T(8,128)S(1)} collective-permute-done((f32[4,144,128]{2,1,0:T(8,128)S(1)}, f32[4,144,128]{2,1,0:T(8,128)S(1)}, u32[]{:S(2)}, u32[]{:S(2)}) %collective-permute-start.6) | collective-permute-done | bytes 294944 | tf_op jit(solution)/shard_map/ppermute | solution.py:333
  26.1 2.5 %collective-permute-start.5 = (f32[4,144,128]{2,1,0:T(8,128)S(1)}, f32[4,144,128]{2,1,0:T(8,128)S(1)}, u32[]{:S(2)}, u32[]{:S(2)}) collective-permute-start(f32[4,144,128]{2,1,0:T(8,128)S(1)} %get-tuple-element.20), channel_id=1, source_target_pairs={{0,12},{2,14},{4,8},{6,10},{8,4},{10,6},{12,0},{14,2},{16,28},{18,... | collective-permute-start | bytes 884744 | tf_op jit(solution)/shard_map/ppermute | solution.py:333
  28.7 0.5 collective-permute-done.8.refs_3_
  29.2 0.6 pick_boundary.1
  29.7 2.7 %collective-permute-start.9 = (f32[4,144,128]{2,1,0:T(8,128)S(1)}, f32[4,144,128]{2,1,0:T(8,128)S(1)}, u32[]{:S(2)}, u32[]{:S(2)}) collective-permute-start(f32[4,144,128]{2,1,0:T(8,128)S(1)} %pick_boundary.1), channel_id=1, source_target_pairs={{0,16},{2,18},{4,20},{6,22},{8,24},{10,26},{12,28},{14,30},{16,0},... | collective-permute-start | bytes 884744 | tf_op jit(solution)/shard_map/ppermute | solution.py:333
  32.4 3.8 %render_first.1 = f32[4,128,128]{2,1,0:T(8,128)S(1)} custom-call(s32[5]{0:T(128)S(1)} %stack.31.info, bf16[512,256]{1,0:T(8,128)(2,1)S(1)} %copy-done.1, f32[4,144,128]{2,1,0:T(8,128)S(1)} %get-tuple-element.21.refs_0_, f32[4,144,128]{2,1,0:T(8,128)S(1)} %collective-permute-done.6.refs_1_, f32[4,144,128]{2,1,0:T(8,128)S(1)} %collective-permute-done.7.refs_2_, ...), custom_call_target="tpu_custom_call" | custom-call | flops 5000000000 | bytes 2000000 | tf_op jit(solution)/shard_map/render_first/pallas_call | solution.py:340
  36.2 0.4 collective-permute-start.10
  36.6 9.6 %collective-permute-done.4.refs_2_ = f32[4,144,128]{2,1,0:T(8,128)S(1)} collective-permute-done((f32[4,144,128]{2,1,0:T(8,128)S(1)}, f32[4,144,128]{2,1,0:T(8,128)S(1)}, u32[]{:S(2)}, u32[]{:S(2)}) %collective-permute-start.4) | collective-permute-done | bytes 294944 | tf_op jit(solution)/shard_map/ppermute | solution.py:333
  46.1 2.0 %collective-permute-done.5.refs_3_ = f32[4,144,128]{2,1,0:T(8,128)S(1)} collective-permute-done((f32[4,144,128]{2,1,0:T(8,128)S(1)}, f32[4,144,128]{2,1,0:T(8,128)S(1)}, u32[]{:S(2)}, u32[]{:S(2)}) %collective-permute-start.5) | collective-permute-done | bytes 294944 | tf_op jit(solution)/shard_map/ppermute | solution.py:333
  48.2 6.9 %collective-permute-done.10.refs_5_ = f32[4,128,128]{2,1,0:T(8,128)S(1)} collective-permute-done((f32[4,128,128]{2,1,0:T(8,128)S(1)}, f32[4,128,128]{2,1,0:T(8,128)S(1)}, u32[]{:S(2)}, u32[]{:S(2)}) %collective-permute-start.10) | collective-permute-done | bytes 262176 | tf_op jit(solution)/shard_map/ppermute | solution.py:333
  55.0 5.3 %render_last.1 = f32[4,128,128]{2,1,0:T(8,128)} custom-call(s32[5]{0:T(128)S(1)} %stack.31.info, bf16[512,256]{1,0:T(8,128)(2,1)S(1)} %copy-done.1, f32[4,144,128]{2,1,0:T(8,128)S(1)} %get-tuple-element.17.refs_0_, f32[4,144,128]{2,1,0:T(8,128)S(1)} %collective-permute-done.3.refs_1_, f32[4,144,128]{2,1,0:T(8,128)S(1)} %collective-permute-done.4.refs_2_, ...), custom_call_target="tpu_custom_call" | custom-call | flops 5000000000 | bytes 2000000 | tf_op jit(solution)/shard_map/render_last/pallas_call | solution.py:342
  (8 shorter events, 0.1 us)
Async XLA Ops:
  0.1 1.6 %copy-start = (f32[2,2048,128]{2,1,0:T(8,128)S(1)}, f32[2,2048,128]{2,1,0:T(8,128)}, u32[]{:S(2)}) copy-start(f32[2,2048,128]{2,1,0:T(8,128)} %field.3) | copy-start | bytes 6291460
  3.0 7.4 %collective-permute-start = (f32[8,2,136,128]{3,2,1,0:T(8,128)S(1)}, f32[8,2,136,128]{3,2,1,0:T(8,128)S(1)}, u32[]{:S(2)}, u32[]{:S(2)}) collective-permute-start(f32[8,2,136,128]{3,2,1,0:T(8,128)S(1)} %get-tuple-element.15), channel_id=1, source_target_pairs={{0,2},{2,0},{4,6},{6,4},{8,10},{10,8},{12,14},{14,12},{16,18},{18,... | collective-permute-start | bytes 3342344 | tf_op jit(solution)/shard_map/ppermute | solution.py:283
  3.5 5.0 %collective-permute-start.2 = (f32[1,128,128]{2,1,0:T(8,128)S(1)}, f32[1,128,128]{2,1,0:T(8,128)S(1)}, u32[]{:S(2)}, u32[]{:S(2)}) collective-permute-start(f32[1,128,128]{2,1,0:T(8,128)S(1)} %get-tuple-element.16), channel_id=1, source_target_pairs={{0,3},{1,2},{2,1},{3,0},{4,7},{5,6},{6,5},{7,4},{8,11},{9,10},{10,... | collective-permute-start | bytes 196616 | tf_op jit(solution)/shard_map/ppermute | solution.py:292
  6.1 4.3 %collective-permute-start.1 = (f32[1,128,128]{2,1,0:T(8,128)S(1)}, f32[1,128,128]{2,1,0:T(8,128)S(1)}, u32[]{:S(2)}, u32[]{:S(2)}) collective-permute-start(f32[1,128,128]{2,1,0:T(8,128)S(1)} %get-tuple-element.16), channel_id=1, source_target_pairs={{0,1},{1,0},{2,3},{3,2},{4,5},{5,4},{6,7},{7,6},{8,9},{9,8},{10,11... | collective-permute-start | bytes 196616 | tf_op jit(solution)/shard_map/ppermute | solution.py:292
  11.3 21.1 %copy-start.1 = (bf16[512,256]{1,0:T(8,128)(2,1)S(1)}, bf16[512,256]{1,0:T(8,128)(2,1)}, u32[]{:S(2)}) copy-start(bf16[512,256]{1,0:T(8,128)(2,1)} %constant.55.clone.weights) | copy-start | bytes 786436
  11.3 14.8 %collective-permute-start.6 = (f32[4,144,128]{2,1,0:T(8,128)S(1)}, f32[4,144,128]{2,1,0:T(8,128)S(1)}, u32[]{:S(2)}, u32[]{:S(2)}) collective-permute-start(f32[4,144,128]{2,1,0:T(8,128)S(1)} %get-tuple-element.22), channel_id=1, source_target_pairs={{0,4},{2,6},{4,0},{6,2},{8,12},{10,14},{12,8},{14,10},{16,20},{18,... | collective-permute-start | bytes 884744 | tf_op jit(solution)/shard_map/ppermute | solution.py:333
  12.9 15.8 %collective-permute-start.7 = (f32[4,144,128]{2,1,0:T(8,128)S(1)}, f32[4,144,128]{2,1,0:T(8,128)S(1)}, u32[]{:S(2)}, u32[]{:S(2)}) collective-permute-start(f32[4,144,128]{2,1,0:T(8,128)S(1)} %get-tuple-element.23), channel_id=1, source_target_pairs={{0,8},{2,10},{4,12},{6,14},{8,0},{10,2},{12,4},{14,6},{16,24},{18,... | collective-permute-start | bytes 884744 | tf_op jit(solution)/shard_map/ppermute | solution.py:333
  14.5 14.7 %collective-permute-start.8 = (f32[4,144,128]{2,1,0:T(8,128)S(1)}, f32[4,144,128]{2,1,0:T(8,128)S(1)}, u32[]{:S(2)}, u32[]{:S(2)}) collective-permute-start(f32[4,144,128]{2,1,0:T(8,128)S(1)} %get-tuple-element.24), channel_id=1, source_target_pairs={{0,12},{2,14},{4,8},{6,10},{8,4},{10,6},{12,0},{14,2},{16,28},{18,... | collective-permute-start | bytes 884744 | tf_op jit(solution)/shard_map/ppermute | solution.py:333
  14.9 21.7 %collective-permute-start.3 = (f32[4,144,128]{2,1,0:T(8,128)S(1)}, f32[4,144,128]{2,1,0:T(8,128)S(1)}, u32[]{:S(2)}, u32[]{:S(2)}) collective-permute-start(f32[4,144,128]{2,1,0:T(8,128)S(1)} %get-tuple-element.18), channel_id=1, source_target_pairs={{0,4},{2,6},{4,0},{6,2},{8,12},{10,14},{12,8},{14,10},{16,20},{18,... | collective-permute-start | bytes 884744 | tf_op jit(solution)/shard_map/ppermute | solution.py:333
  16.4 29.8 %collective-permute-start.4 = (f32[4,144,128]{2,1,0:T(8,128)S(1)}, f32[4,144,128]{2,1,0:T(8,128)S(1)}, u32[]{:S(2)}, u32[]{:S(2)}) collective-permute-start(f32[4,144,128]{2,1,0:T(8,128)S(1)} %get-tuple-element.19), channel_id=1, source_target_pairs={{0,8},{2,10},{4,12},{6,14},{8,0},{10,2},{12,4},{14,6},{16,24},{18,... | collective-permute-start | bytes 884744 | tf_op jit(solution)/shard_map/ppermute | solution.py:333
  26.1 22.0 %collective-permute-start.5 = (f32[4,144,128]{2,1,0:T(8,128)S(1)}, f32[4,144,128]{2,1,0:T(8,128)S(1)}, u32[]{:S(2)}, u32[]{:S(2)}) collective-permute-start(f32[4,144,128]{2,1,0:T(8,128)S(1)} %get-tuple-element.20), channel_id=1, source_target_pairs={{0,12},{2,14},{4,8},{6,10},{8,4},{10,6},{12,0},{14,2},{16,28},{18,... | collective-permute-start | bytes 884744 | tf_op jit(solution)/shard_map/ppermute | solution.py:333
  29.7 25.3 %collective-permute-start.9 = (f32[4,144,128]{2,1,0:T(8,128)S(1)}, f32[4,144,128]{2,1,0:T(8,128)S(1)}, u32[]{:S(2)}, u32[]{:S(2)}) collective-permute-start(f32[4,144,128]{2,1,0:T(8,128)S(1)} %pick_boundary.1), channel_id=1, source_target_pairs={{0,16},{2,18},{4,20},{6,22},{8,24},{10,26},{12,28},{14,30},{16,0},... | collective-permute-start | bytes 884744 | tf_op jit(solution)/shard_map/ppermute | solution.py:333
  36.2 18.9 %collective-permute-start.10 = (f32[4,128,128]{2,1,0:T(8,128)S(1)}, f32[4,128,128]{2,1,0:T(8,128)S(1)}, u32[]{:S(2)}, u32[]{:S(2)}) collective-permute-start(f32[4,128,128]{2,1,0:T(8,128)S(1)} %render_first.1), channel_id=1, source_target_pairs={{0,16},{2,18},{4,20},{6,22},{8,24},{10,26},{12,28},{14,30},{16,0},... | collective-permute-start | bytes 786440 | tf_op jit(solution)/shard_map/ppermute | solution.py:333

commit v4 on v3

--- a/solution.py
+++ b/solution.py
@@ -117,7 +117,7 @@
 def render_kernel(size, last, info, weights, *refs):
     blocks, refs = refs[: size // 2], refs[size // 2 :]
     if last:
-        boundary, other, image, sx, dx = refs
+        boundary, image, sx, dx = refs
     else:
         image, sx, dx = refs
     depth, own = blocks[0].shape[0], image.shape[1]
@@ -132,23 +132,30 @@
         for plane in range(depth):
             slot = (chip ^ step) * depth + plane + start
             filter_columns(blocks[step], plane, own, weights, sx, dx, slot)
-    for plane in range(extra):
-        slot = (planes + 2) * front + plane
-        filter_columns(boundary, plane, own, weights, sx, dx, slot)
+    if last:
+        for plane in range(extra):
+            slot = (planes + 2) * front + plane
+            filter_columns(boundary, plane, own, weights, sx, dx, slot)
 
     @pl.loop(0, own // TILE)
     def _(tile):
         first = pl.multiple_of(tile * TILE, TILE)
         total = render(sx, dx, first, planes - 2 + extra)
-        if last:
-            is_front = front == 1
-            rest = tuple(other[channel, pl.ds(first, TILE), :] for channel in range(4))
-            ahead = tuple(jnp.where(is_front, m, r) for m, r in zip(total, rest))
-            behind = tuple(jnp.where(is_front, r, m) for m, r in zip(total, rest))
-            v_sum, vt_sum, vu_sum, cover = over(ahead, behind)
-            total = (0.5 * (v_sum + vu_sum), 0.5 * v_sum + 0.4 * vt_sum, 0.5 * (v_sum - vt_sum), cover)
         for channel in range(4):
             image[channel, pl.ds(first, TILE), :] = total[channel]
+
+
+def join_kernel(info, mine, other, picture):
+    is_front = info[2] == 1
+    mine = tuple(mine[channel] for channel in range(4))
+    other = tuple(other[channel] for channel in range(4))
+    ahead = tuple(jnp.where(is_front, m, o) for m, o in zip(mine, other))
+    behind = tuple(jnp.where(is_front, o, m) for m, o in zip(mine, other))
+    v_sum, vt_sum, vu_sum, cover = over(ahead, behind)
+    picture[0] = 0.5 * (v_sum + vu_sum)
+    picture[1] = 0.5 * v_sum + 0.4 * vt_sum
+    picture[2] = 0.5 * (v_sum - vt_sum)
+    picture[3] = cover
 
 
 def edge_columns(field, out):
@@ -184,17 +191,6 @@
             yield chunk * (size // 2) + step, base + 2 * (chip ^ step), core
 
 
-def share_kernel(size, info, field, edges, share):
-    own = share.shape[2] - 8
-    edge_columns(field, edges)
-    for index, target, core in targets(size, info):
-        target = target + 1 - core
-        for plane in range(field.shape[0]):
-            start = pl.multiple_of(target * own, 8)
-            share[index, plane, 0:own, :] = field[plane, pl.ds(start, own), :]
-            share[index, plane, own : own + 8, :] = rows_around(field, plane, target, own)
-
-
 def pack_kernel(size, info, field, shared, *refs):
     edges, outs, sides = refs[:4], refs[4:-1], refs[-1]
     depth, height, width = field.shape
@@ -217,11 +213,9 @@
         for which in range(2):
             for plane in range(depth):
                 slot = (core if which == 0 else 1 - core) * depth + plane
-                if which == 0:
-                    out[slot, 0:own, :] = field[plane, pl.ds(start, own), :]
-                    out[slot, own : own + 8, :] = rows_around(field, plane, target, own)
-                else:
-                    out[slot, 0 : own + 8, :] = shared[index, plane]
+                source = (field, shared)[which]
+                out[slot, 0:own, :] = source[plane, pl.ds(start, own), :]
+                out[slot, own : own + 8, :] = rows_around(source, plane, target, own)
                 top = side_rows(which, plane, jnp.maximum(start - 2, 0), 0)
                 end = side_rows(which, plane, jnp.minimum(start + own, height - 2), 2)
                 top = jnp.where(target > 0, top, 0.0)
@@ -269,18 +263,15 @@
     image = jax.ShapeDtypeStruct((4, own, width), f32)
     edge_groups = -(-depth * height // LANES // (LANES // 4))
 
-    edges, share = pl.pallas_call(
-        functools.partial(share_kernel, size),
-        out_shape=(
-            jax.ShapeDtypeStruct((edge_groups, LANES, LANES), f32),
-            jax.ShapeDtypeStruct((size, depth, own + 8, width), f32),
-        ),
-        in_specs=[SMEM, VMEM],
-        out_specs=(VMEM, VMEM),
+    shared = lax.ppermute(field, "depth", [(i, i ^ 1) for i in range(groups)])
+    edges = pl.pallas_call(
+        edge_columns,
+        out_shape=jax.ShapeDtypeStruct((edge_groups, LANES, LANES), f32),
+        in_specs=[VMEM],
+        out_specs=VMEM,
         compiler_params=PARAMS,
-        name="share_with_core",
-    )(info, field)
-    shared = lax.ppermute(share, "depth", [(i, i ^ 1) for i in range(groups)])
+        name="edge_columns",
+    )(field)
 
     def from_column(flip, shifts):
         route = []
@@ -312,7 +303,7 @@
         return pl.pallas_call(
             functools.partial(render_kernel, size, last),
             out_shape=image,
-            in_specs=[SMEM] + [VMEM] * (size // 2 + (3 if last else 1)),
+            in_specs=[SMEM] + [VMEM] * (1 + size // 2 + (1 if last else 0)),
             out_specs=VMEM,
             scratch_shapes=[pltpu.VMEM((count, own + 16, width), f32)] * 2,
             compiler_params=PARAMS,
@@ -338,8 +329,19 @@
     theirs = gathered(blocks[: size // 2])
     boundary = swap(pick(info, *theirs), size)
     image_part = swap(render_call(False)(info, weights, *theirs), size)
-    mine = gathered(blocks[size // 2 :])
-    return render_call(True)(info, weights, *mine, boundary, image_part)
+    mine = [blocks[size // 2]]
+    for step in range(1, size // 2):
+        held, _ = lax.optimization_barrier((blocks[size // 2 + step], theirs[step]))
+        mine.append(swap(held, 2 * step))
+    own_part = render_call(True)(info, weights, *mine, boundary)
+    return pl.pallas_call(
+        join_kernel,
+        out_shape=image,
+        in_specs=[SMEM, VMEM, VMEM],
+        out_specs=VMEM,
+        compiler_params=PARAMS,
+        name="join_halves",
+    )(info, own_part, image_part)
 
 
 def solution(mesh):

time: 60.5 us -> 56.2 us (0.929)
  waiting for transfers between devices: 31.3 us -> 24.5 us
  starting transfers between devices: 15.4 us -> 17 us
  Pallas kernels: 11.9 us -> 12.8 us
    ppermute x8, waiting for transfers between devices: 27.1 us -> 20.3 us  [swap(): return lax.ppermute(x, 'depth', [(i, i ^ bits) for i in range(groups)])]
    ppermute x8, starting transfers between devices: 12.2 us -> 13.8 us  [swap(): return lax.ppermute(x, 'depth', [(i, i ^ bits) for i in range(groups)])]
    pallas_call x1, Pallas kernels: 0.92 us -> 1.96 us  [local(): pl.pallas_call(functools.partial(pack_kernel, size), out_shape=(block,) *...]
    pallas_call x2 -> x3, Pallas kernels: 6.61 us -> 6.55 us  [the longest x1 4.55 us: local(): own_part = render_call(True)(info, weights, *mine, boundary)]
    unnamed x4 -> x6, local copies, waits for them, and re-layouts: 1.6 us -> 1.6 us
  transfers between devices with their start and end apart: 11 -> 11, of which waited for: 7 -> 9; matrix products, arithmetic and copies ran while one was open for 0% -> 0% of each run, Pallas kernels for 7% -> 17%
where the time goes in v4:
time: 56.2 us; the launch traced here: 56 us
  waiting for transfers between devices  24.5 us (44%)
  starting transfers between devices  17 us (30%)
  Pallas kernels  12.8 us (23%)
  local copies, waits for them, and re-layouts  1.68 us (3%)
    ppermute x8, waiting for transfers between devices, swap(): return lax.ppermute(x, 'depth', [(i, i ^ bits) for i in range(groups)])  20.3 us
    ppermute x8, starting transfers between devices, swap(): return lax.ppermute(x, 'depth', [(i, i ^ bits) for i in range(groups)])  13.8 us
    pallas_call x1, Pallas kernels, local(): own_part = render_call(True)(info, weights, *mine, boundary)  4.55 us
    ppermute x2, waiting for transfers between devices, from_column(): return lax.ppermute(edges, ('depth', 'cols'), route)  4.18 us
    pallas_call x1, Pallas kernels, local(): image_part = swap(render_call(False)(info, weights, *theirs), size)  3.76 us
    ppermute x2, starting transfers between devices, from_column(): return lax.ppermute(edges, ('depth', 'cols'), route)  2.68 us
    pallas_call x1, Pallas kernels, local(): pl.pallas_call(functools.partial(pack_kernel, size), out_shape=(block,) *...  1.96 us
    unnamed x6, local copies, waits for them, and re-layouts  1.6 us
  transfers between devices with their start and end apart: 11, of which 9 were waited for; matrix products, arithmetic and copies ran while one was open for 0% of the time, Pallas kernels for 17%

profile of v4, /device:TPU:0, one launch (start us, length us, event | category | flops | bytes accessed | tf_op | source)
XLA Modules:
  0.0 56.0 jit_solution(7993515449723294235)
XLA Ops:
  0.0 0.5 collective-permute-start
  0.5 1.6 %copy-done = f32[2,2048,128]{2,1,0:T(8,128)S(1)} copy-done((f32[2,2048,128]{2,1,0:T(8,128)S(1)}, f32[2,2048,128]{2,1,0:T(8,128)}, u32[]{:S(2)}) %copy-start) | copy-done | bytes 2097176
  2.0 0.7 %edge_columns.1 = f32[1,128,128]{2,1,0:T(8,128)S(1)} custom-call(f32[2,2048,128]{2,1,0:T(8,128)S(1)} %copy-done), custom_call_target="tpu_custom_call" | custom-call | tf_op jit(solution)/shard_map/edge_columns/pallas_call | solution.py:267
  2.7 2.7 %collective-permute-start.2 = (f32[1,128,128]{2,1,0:T(8,128)S(1)}, f32[1,128,128]{2,1,0:T(8,128)S(1)}, u32[]{:S(2)}, u32[]{:S(2)}) collective-permute-start(f32[1,128,128]{2,1,0:T(8,128)S(1)} %edge_columns.1), channel_id=1, source_target_pairs={{0,3},{1,2},{2,1},{3,0},{4,7},{5,6},{6,5},{7,4},{8,11},{9,10},{10,... | collective-permute-start | bytes 196616 | tf_op jit(solution)/shard_map/ppermute | solution.py:283
  5.5 2.4 %collective-permute-done.2.refs_2_.refs_3_ = f32[1,128,128]{2,1,0:T(8,128)S(1)} collective-permute-done((f32[1,128,128]{2,1,0:T(8,128)S(1)}, f32[1,128,128]{2,1,0:T(8,128)S(1)}, u32[]{:S(2)}, u32[]{:S(2)}) %collective-permute-start.2) | collective-permute-done | bytes 65568 | tf_op jit(solution)/shard_map/ppermute | solution.py:283
  7.9 1.8 %collective-permute-done.1.refs_0_.refs_1_ = f32[1,128,128]{2,1,0:T(8,128)S(1)} collective-permute-done((f32[1,128,128]{2,1,0:T(8,128)S(1)}, f32[1,128,128]{2,1,0:T(8,128)S(1)}, u32[]{:S(2)}, u32[]{:S(2)}) %collective-permute-start.1) | collective-permute-done | bytes 65568 | tf_op jit(solution)/shard_map/ppermute | solution.py:283
  9.7 2.0 %pack_blocks.1 = (f32[4,144,128]{2,1,0:T(8,128)S(1)}, f32[4,144,128]{2,1,0:T(8,128)S(1)}, f32[4,144,128]{2,1,0:T(8,128)S(1)}, f32[4,144,128]{2,1,0:T(8,128)S(1)}...) custom-call(s32[5]{0:T(128)S(1)} %stack.31.info, ...), custom_call_target="tpu_custom_call" | custom-call | tf_op jit(solution)/shard_map/pack_blocks/pallas_call | solution.py:291
  11.6 1.6 %collective-permute-start.3 = (f32[4,144,128]{2,1,0:T(8,128)S(1)}, f32[4,144,128]{2,1,0:T(8,128)S(1)}, u32[]{:S(2)}, u32[]{:S(2)}) collective-permute-start(f32[4,144,128]{2,1,0:T(8,128)S(1)} %get-tuple-element.18), channel_id=1, source_target_pairs={{0,4},{2,6},{4,0},{6,2},{8,12},{10,14},{12,8},{14,10},{16,20},{18,... | collective-permute-start | bytes 884744 | tf_op jit(solution)/shard_map/ppermute | solution.py:324
  13.2 1.6 %collective-permute-start.5 = (f32[4,144,128]{2,1,0:T(8,128)S(1)}, f32[4,144,128]{2,1,0:T(8,128)S(1)}, u32[]{:S(2)}, u32[]{:S(2)}) collective-permute-start(f32[4,144,128]{2,1,0:T(8,128)S(1)} %get-tuple-element.21), channel_id=1, source_target_pairs={{0,8},{2,10},{4,12},{6,14},{8,0},{10,2},{12,4},{14,6},{16,24},{18,... | collective-permute-start | bytes 884744 | tf_op jit(solution)/shard_map/ppermute | solution.py:324
  14.8 0.4 collective-permute-start.7
  15.2 6.0 %collective-permute-done.3.refs_1_ = f32[4,144,128]{2,1,0:T(8,128)S(1)} collective-permute-done((f32[4,144,128]{2,1,0:T(8,128)S(1)}, f32[4,144,128]{2,1,0:T(8,128)S(1)}, u32[]{:S(2)}, u32[]{:S(2)}) %collective-permute-start.3) | collective-permute-done | bytes 294944 | tf_op jit(solution)/shard_map/ppermute | solution.py:324
  21.2 1.3 %collective-permute-start.4 = (f32[4,144,128]{2,1,0:T(8,128)S(1)}, f32[4,144,128]{2,1,0:T(8,128)S(1)}, u32[]{:S(2)}, u32[]{:S(2)}) collective-permute-start(f32[4,144,128]{2,1,0:T(8,128)S(1)} %get-tuple-element.19), channel_id=1, source_target_pairs={{0,4},{2,6},{4,0},{6,2},{8,12},{10,14},{12,8},{14,10},{16,20},{18,... | collective-permute-start | bytes 884744 | tf_op jit(solution)/shard_map/ppermute | solution.py:324
  22.5 0.7 %collective-permute-done.5.refs_2_ = f32[4,144,128]{2,1,0:T(8,128)S(1)} collective-permute-done((f32[4,144,128]{2,1,0:T(8,128)S(1)}, f32[4,144,128]{2,1,0:T(8,128)S(1)}, u32[]{:S(2)}, u32[]{:S(2)}) %collective-permute-start.5) | collective-permute-done | bytes 294944 | tf_op jit(solution)/shard_map/ppermute | solution.py:324
  23.2 1.6 %collective-permute-start.6 = (f32[4,144,128]{2,1,0:T(8,128)S(1)}, f32[4,144,128]{2,1,0:T(8,128)S(1)}, u32[]{:S(2)}, u32[]{:S(2)}) collective-permute-start(f32[4,144,128]{2,1,0:T(8,128)S(1)} %get-tuple-element.22), channel_id=1, source_target_pairs={{0,8},{2,10},{4,12},{6,14},{8,0},{10,2},{12,4},{14,6},{16,24},{18,... | collective-permute-start | bytes 884744 | tf_op jit(solution)/shard_map/ppermute | solution.py:324
  24.7 4.7 %collective-permute-done.7.refs_3_ = f32[4,144,128]{2,1,0:T(8,128)S(1)} collective-permute-done((f32[4,144,128]{2,1,0:T(8,128)S(1)}, f32[4,144,128]{2,1,0:T(8,128)S(1)}, u32[]{:S(2)}, u32[]{:S(2)}) %collective-permute-start.7) | collective-permute-done | bytes 294944 | tf_op jit(solution)/shard_map/ppermute | solution.py:324
  29.5 0.6 %pick_boundary.1 = f32[4,144,128]{2,1,0:T(8,128)S(1)} custom-call(s32[5]{0:T(128)S(1)} %stack.31.info, f32[4,144,128]{2,1,0:T(8,128)S(1)} %get-tuple-element.26.refs_0_, f32[4,144,128]{2,1,0:T(8,128)S(1)} %collective-permute-done.3.refs_1_, f32[4,144,128]{2,1,0:T(8,128)S(1)} %collective-permute-done.5.refs_2_, f32[4,144,128]{2,1,0:T(8,128)S(1)} %collective-permute-done.7.refs_3_), custom_call_target="tpu_custom_call" | custom-call | tf_op jit(solution)/shard_map/pick_boundary/pallas_call | solution.py:330
  30.1 2.6 %collective-permute-start.9 = (f32[4,144,128]{2,1,0:T(8,128)S(1)}, f32[4,144,128]{2,1,0:T(8,128)S(1)}, u32[]{:S(2)}, u32[]{:S(2)}) collective-permute-start(f32[4,144,128]{2,1,0:T(8,128)S(1)} %pick_boundary.1), channel_id=1, source_target_pairs={{0,16},{2,18},{4,20},{6,22},{8,24},{10,26},{12,28},{14,30},{16,0},... | collective-permute-start | bytes 884744 | tf_op jit(solution)/shard_map/ppermute | solution.py:324
  32.7 4.7 %collective-permute-start.8 = (f32[4,144,128]{2,1,0:T(8,128)S(1)}, f32[4,144,128]{2,1,0:T(8,128)S(1)}, u32[]{:S(2)}, u32[]{:S(2)}) collective-permute-start(f32[4,144,128]{2,1,0:T(8,128)S(1)} %get-tuple-element.25), channel_id=1, source_target_pairs={{0,12},{2,14},{4,8},{6,10},{8,4},{10,6},{12,0},{14,2},{16,28},{18,... | collective-permute-start | bytes 884744 | tf_op jit(solution)/shard_map/ppermute | solution.py:324
  37.4 3.8 %render_first.1 = f32[4,128,128]{2,1,0:T(8,128)S(1)} custom-call(s32[5]{0:T(128)S(1)} %stack.31.info, bf16[512,256]{1,0:T(8,128)(2,1)S(1)} %copy-done.2, f32[4,144,128]{2,1,0:T(8,128)S(1)} %get-tuple-element.26.refs_0_, f32[4,144,128]{2,1,0:T(8,128)S(1)} %collective-permute-done.3.refs_1_, f32[4,144,128]{2,1,0:T(8,128)S(1)} %collective-permute-done.5.refs_2_, ...), custom_call_target="tpu_custom_call" | custom-call | flops 5000000000 | bytes 2000000 | tf_op jit(solution)/shard_map/render_first/pallas_call | solution.py:331
  41.7 3.5 %collective-permute-done.9.refs_4_ = f32[4,144,128]{2,1,0:T(8,128)S(1)} collective-permute-done((f32[4,144,128]{2,1,0:T(8,128)S(1)}, f32[4,144,128]{2,1,0:T(8,128)S(1)}, u32[]{:S(2)}, u32[]{:S(2)}) %collective-permute-start.9) | collective-permute-done | bytes 294944 | tf_op jit(solution)/shard_map/ppermute | solution.py:324
  45.1 2.5 %collective-permute-done.8.refs_3_ = f32[4,144,128]{2,1,0:T(8,128)S(1)} collective-permute-done((f32[4,144,128]{2,1,0:T(8,128)S(1)}, f32[4,144,128]{2,1,0:T(8,128)S(1)}, u32[]{:S(2)}, u32[]{:S(2)}) %collective-permute-start.8) | collective-permute-done | bytes 294944 | tf_op jit(solution)/shard_map/ppermute | solution.py:324
  47.6 4.6 %render_last.1.mine = f32[4,128,128]{2,1,0:T(8,128)S(1)} custom-call(s32[5]{0:T(128)S(1)} %stack.31.info, bf16[512,256]{1,0:T(8,128)(2,1)S(1)} %copy-done.2, f32[4,144,128]{2,1,0:T(8,128)S(1)} %get-tuple-element.16.refs_0_, f32[4,144,128]{2,1,0:T(8,128)S(1)} %collective-permute-done.4.refs_1_, f32[4,144,128]{2,1,0:T(8,128)S(1)} %collective-permute-done.6.refs_2_, ...), custom_call_target="tpu_custom_call" | custom-call | flops 5000000000 | bytes 2000000 | tf_op jit(solution)/shard_map/render_last/pallas_call | solution.py:336
  52.2 2.5 %collective-permute-done.10.other = f32[4,128,128]{2,1,0:T(8,128)S(1)} collective-permute-done((f32[4,128,128]{2,1,0:T(8,128)S(1)}, f32[4,128,128]{2,1,0:T(8,128)S(1)}, u32[]{:S(2)}, u32[]{:S(2)}) %collective-permute-start.10) | collective-permute-done | bytes 262176 | tf_op jit(solution)/shard_map/ppermute | solution.py:324
  54.7 1.3 %join_halves.1 = f32[4,128,128]{2,1,0:T(8,128)} custom-call(s32[5]{0:T(128)S(1)} %stack.31.info, f32[4,128,128]{2,1,0:T(8,128)S(1)} %render_last.1.mine, f32[4,128,128]{2,1,0:T(8,128)S(1)} %collective-permute-done.10.other), custom_call_target="tpu_custom_call" | custom-call | tf_op jit(solution)/shard_map/join_halves/pallas_call | solution.py:337
  (11 shorter events, 0.6 us)
Async XLA Ops:
  0.0 9.7 %collective-permute-start = (f32[2,2048,128]{2,1,0:T(8,128)}, f32[2,2048,128]{2,1,0:T(8,128)}, u32[]{:S(2)}, u32[]{:S(2)}) collective-permute-start(f32[2,2048,128]{2,1,0:T(8,128)} %field.3), channel_id=1, source_target_pairs={{0,2},{2,0},{4,6},{6,4},{8,10},{10,8},{12,14},{14,12},{16,18},{18,... | collective-permute-start | bytes 6291464 | tf_op jit(solution)/shard_map/ppermute | solution.py:266
  0.5 1.6 %copy-start = (f32[2,2048,128]{2,1,0:T(8,128)S(1)}, f32[2,2048,128]{2,1,0:T(8,128)}, u32[]{:S(2)}) copy-start(f32[2,2048,128]{2,1,0:T(8,128)} %field.3) | copy-start | bytes 6291460
  2.0 7.6 %copy-start.1 = (f32[2,2048,128]{2,1,0:T(8,128)S(1)}, f32[2,2048,128]{2,1,0:T(8,128)}, u32[]{:S(2)}) copy-start(f32[2,2048,128]{2,1,0:T(8,128)} %field.3) | copy-start | bytes 6291460
  2.7 5.1 %collective-permute-start.2 = (f32[1,128,128]{2,1,0:T(8,128)S(1)}, f32[1,128,128]{2,1,0:T(8,128)S(1)}, u32[]{:S(2)}, u32[]{:S(2)}) collective-permute-start(f32[1,128,128]{2,1,0:T(8,128)S(1)} %edge_columns.1), channel_id=1, source_target_pairs={{0,3},{1,2},{2,1},{3,0},{4,7},{5,6},{6,5},{7,4},{8,11},{9,10},{10,... | collective-permute-start | bytes 196616 | tf_op jit(solution)/shard_map/ppermute | solution.py:283
  5.4 4.3 %collective-permute-start.1 = (f32[1,128,128]{2,1,0:T(8,128)S(1)}, f32[1,128,128]{2,1,0:T(8,128)S(1)}, u32[]{:S(2)}, u32[]{:S(2)}) collective-permute-start(f32[1,128,128]{2,1,0:T(8,128)S(1)} %edge_columns.1), channel_id=1, source_target_pairs={{0,1},{1,0},{2,3},{3,2},{4,5},{5,4},{6,7},{7,6},{8,9},{9,8},{10,11... | collective-permute-start | bytes 196616 | tf_op jit(solution)/shard_map/ppermute | solution.py:283
  5.5 31.9 %copy-start.2 = (bf16[512,256]{1,0:T(8,128)(2,1)S(1)}, bf16[512,256]{1,0:T(8,128)(2,1)}, u32[]{:S(2)}) copy-start(bf16[512,256]{1,0:T(8,128)(2,1)} %constant.55.clone.weights) | copy-start | bytes 786436
  11.6 9.6 %collective-permute-start.3 = (f32[4,144,128]{2,1,0:T(8,128)S(1)}, f32[4,144,128]{2,1,0:T(8,128)S(1)}, u32[]{:S(2)}, u32[]{:S(2)}) collective-permute-start(f32[4,144,128]{2,1,0:T(8,128)S(1)} %get-tuple-element.18), channel_id=1, source_target_pairs={{0,4},{2,6},{4,0},{6,2},{8,12},{10,14},{12,8},{14,10},{16,20},{18,... | collective-permute-start | bytes 884744 | tf_op jit(solution)/shard_map/ppermute | solution.py:324
  13.2 9.9 %collective-permute-start.5 = (f32[4,144,128]{2,1,0:T(8,128)S(1)}, f32[4,144,128]{2,1,0:T(8,128)S(1)}, u32[]{:S(2)}, u32[]{:S(2)}) collective-permute-start(f32[4,144,128]{2,1,0:T(8,128)S(1)} %get-tuple-element.21), channel_id=1, source_target_pairs={{0,8},{2,10},{4,12},{6,14},{8,0},{10,2},{12,4},{14,6},{16,24},{18,... | collective-permute-start | bytes 884744 | tf_op jit(solution)/shard_map/ppermute | solution.py:324
  14.8 14.7 %collective-permute-start.7 = (f32[4,144,128]{2,1,0:T(8,128)S(1)}, f32[4,144,128]{2,1,0:T(8,128)S(1)}, u32[]{:S(2)}, u32[]{:S(2)}) collective-permute-start(f32[4,144,128]{2,1,0:T(8,128)S(1)} %get-tuple-element.24), channel_id=1, source_target_pairs={{0,12},{2,14},{4,8},{6,10},{8,4},{10,6},{12,0},{14,2},{16,28},{18,... | collective-permute-start | bytes 884744 | tf_op jit(solution)/shard_map/ppermute | solution.py:324
  21.2 20.1 %collective-permute-start.4 = (f32[4,144,128]{2,1,0:T(8,128)S(1)}, f32[4,144,128]{2,1,0:T(8,128)S(1)}, u32[]{:S(2)}, u32[]{:S(2)}) collective-permute-start(f32[4,144,128]{2,1,0:T(8,128)S(1)} %get-tuple-element.19), channel_id=1, source_target_pairs={{0,4},{2,6},{4,0},{6,2},{8,12},{10,14},{12,8},{14,10},{16,20},{18,... | collective-permute-start | bytes 884744 | tf_op jit(solution)/shard_map/ppermute | solution.py:324
  23.2 18.5 %collective-permute-start.6 = (f32[4,144,128]{2,1,0:T(8,128)S(1)}, f32[4,144,128]{2,1,0:T(8,128)S(1)}, u32[]{:S(2)}, u32[]{:S(2)}) collective-permute-start(f32[4,144,128]{2,1,0:T(8,128)S(1)} %get-tuple-element.22), channel_id=1, source_target_pairs={{0,8},{2,10},{4,12},{6,14},{8,0},{10,2},{12,4},{14,6},{16,24},{18,... | collective-permute-start | bytes 884744 | tf_op jit(solution)/shard_map/ppermute | solution.py:324
  30.1 15.1 %collective-permute-start.9 = (f32[4,144,128]{2,1,0:T(8,128)S(1)}, f32[4,144,128]{2,1,0:T(8,128)S(1)}, u32[]{:S(2)}, u32[]{:S(2)}) collective-permute-start(f32[4,144,128]{2,1,0:T(8,128)S(1)} %pick_boundary.1), channel_id=1, source_target_pairs={{0,16},{2,18},{4,20},{6,22},{8,24},{10,26},{12,28},{14,30},{16,0},... | collective-permute-start | bytes 884744 | tf_op jit(solution)/shard_map/ppermute | solution.py:324
  32.7 14.9 %collective-permute-start.8 = (f32[4,144,128]{2,1,0:T(8,128)S(1)}, f32[4,144,128]{2,1,0:T(8,128)S(1)}, u32[]{:S(2)}, u32[]{:S(2)}) collective-permute-start(f32[4,144,128]{2,1,0:T(8,128)S(1)} %get-tuple-element.25), channel_id=1, source_target_pairs={{0,12},{2,14},{4,8},{6,10},{8,4},{10,6},{12,0},{14,2},{16,28},{18,... | collective-permute-start | bytes 884744 | tf_op jit(solution)/shard_map/ppermute | solution.py:324
  41.1 13.6 %collective-permute-start.10 = (f32[4,128,128]{2,1,0:T(8,128)S(1)}, f32[4,128,128]{2,1,0:T(8,128)S(1)}, u32[]{:S(2)}, u32[]{:S(2)}) collective-permute-start(f32[4,128,128]{2,1,0:T(8,128)S(1)} %render_first.1), channel_id=1, source_target_pairs={{0,16},{2,18},{4,20},{6,22},{8,24},{10,26},{12,28},{14,30},{16,0},... | collective-permute-start | bytes 786440 | tf_op jit(solution)/shard_map/ppermute | solution.py:324

commit v5 on v4

--- a/solution.py
+++ b/solution.py
@@ -46,15 +46,15 @@
     return hi, mid, lo
 
 
-def filter_columns(block, plane, own, weights, sx, dx, slot):
+def filter_columns(block, plane, side, own, weights, sx, dx, slot):
     width = block.shape[-1]
-    hi, mid, lo = three_parts(block[plane, 0 : own + 8, :])
-    sides = [part.astype(jnp.float32) for part in three_parts(block[plane, own + 8 : own + 16, :])]
+    hi, mid, lo = three_parts(block[plane])
+    sides = [part.astype(jnp.float32) for part in three_parts(side)]
     lanes_first = jnp.transpose(jnp.concatenate(sides, 0))
     inner = lax.broadcasted_iota(jnp.int32, lanes_first.shape, 1) % 8 < 4
-    side = jnp.concatenate([jnp.where(inner, lanes_first, 0.0)[0:own], jnp.where(inner, 0.0, lanes_first)[0:8]], 0)
-    side = jnp.concatenate([side, jnp.zeros((own + 8, LANES - side.shape[1]), jnp.float32)], 1)
-    row = jnp.concatenate([hi, mid, lo, side.astype(jnp.bfloat16)], 1)
+    halo = jnp.concatenate([jnp.where(inner, lanes_first, 0.0)[0:own], jnp.where(inner, 0.0, lanes_first)[0:8]], 0)
+    halo = jnp.concatenate([halo, jnp.zeros((own + 8, LANES - halo.shape[1]), jnp.float32)], 1)
+    row = jnp.concatenate([hi, mid, lo, halo.astype(jnp.bfloat16)], 1)
     both = jnp.dot(row, weights[...], preferred_element_type=jnp.float32)
     for out, part in ((sx, both[:, :width]), (dx, both[:, width:])):
         out[slot, 8 : 8 + own] = part[0:own]
@@ -114,28 +114,35 @@
     return tuple(f + rest * b for f, b in zip(front, back))
 
 
-def render_kernel(size, last, info, weights, *refs):
-    blocks, refs = refs[: size // 2], refs[size // 2 :]
-    if last:
-        boundary, image, sx, dx = refs
-    else:
-        image, sx, dx = refs
+def render_kernel(size, last, info, weights, before, after, *refs):
+    steps = size // 2
+    blocks, (image, sx, dx) = refs[:-3], refs[-3:]
     depth, own = blocks[0].shape[0], image.shape[1]
-    planes = depth * (size // 2)
+    planes = depth * steps
     extra = 4 if last else 0
     chip, front = info[0], info[2]
     start = 2 * front + extra * (1 - front)
     empty = (1 - front) * (planes + extra)
     sx[pl.ds(empty, 2)] = jnp.zeros((2,) + sx.shape[1:], jnp.float32)
     dx[pl.ds(empty, 2)] = jnp.zeros((2,) + dx.shape[1:], jnp.float32)
-    for step in range(size // 2):
+    line = lax.broadcasted_iota(jnp.int32, (8, LANES), 0) % 4
+    from_left = (line < 2) & (info[3] == 1)
+    from_right = (line >= 2) & (info[4] == 1)
+
+    def side(index):
+        left, right = (
+            jnp.concatenate([ref[0, 4 * index : 4 * index + 4], ref[1, 4 * index : 4 * index + 4]], 0)
+            for ref in (before, after)
+        )
+        return jnp.where(from_left, left, jnp.where(from_right, right, 0.0))
+
+    for step in range(steps):
         for plane in range(depth):
             slot = (chip ^ step) * depth + plane + start
-            filter_columns(blocks[step], plane, own, weights, sx, dx, slot)
-    if last:
-        for plane in range(extra):
-            slot = (planes + 2) * front + plane
-            filter_columns(boundary, plane, own, weights, sx, dx, slot)
+            filter_columns(blocks[step], plane, side(step * depth + plane), own, weights, sx, dx, slot)
+    for plane in range(extra):
+        slot = (planes + 2) * front + plane
+        filter_columns(blocks[steps], plane, side(planes + plane), own, weights, sx, dx, slot)
 
     @pl.loop(0, own // TILE)
     def _(tile):
@@ -158,18 +165,21 @@
     picture[3] = cover
 
 
-def edge_columns(field, out):
-    depth, height, width = field.shape
-    lane = lax.broadcasted_iota(jnp.int32, (LANES, width), 1)
-    count = depth * height // LANES
-    for base in range(0, count, LANES // 4):
-        packed = jnp.zeros((LANES, width), jnp.float32)
-        for chunk in range(base, min(base + LANES // 4, count)):
-            at = chunk * LANES
-            rows = field[at // height, at % height : at % height + LANES, :]
-            place = 4 * (chunk - base)
-            packed = jnp.where(lane // 4 == chunk - base, pltpu.roll(rows, (place + 2) % width, 1), packed)
-        out[base // (LANES // 4)] = jnp.transpose(packed)
+def edge_kernel(*refs):
+    blocks, out = refs[:-1], refs[-1]
+    own, width = blocks[0].shape[1] - 8, blocks[0].shape[2]
+    places = [(block, plane) for block in blocks for plane in range(block.shape[0])]
+    group = LANES // 4
+    lane = lax.broadcasted_iota(jnp.int32, (own + 8, width), 1) // 4
+    for base in range(0, len(places), group):
+        packed = jnp.zeros((own + 8, width), jnp.float32)
+        for at, (block, plane) in enumerate(places[base : base + group]):
+            packed = jnp.where(lane == at, pltpu.roll(block[plane], (4 * at + 2) % width, 1), packed)
+        for part, rows in enumerate((packed[0:own], packed[own:])):
+            missing = LANES - rows.shape[0]
+            if missing:
+                rows = jnp.concatenate([rows, jnp.zeros((missing, width), jnp.float32)], 0)
+            out[part, 4 * base : 4 * base + LANES] = jnp.transpose(rows)
 
 
 def rows_around(field, plane, target, own):
@@ -191,37 +201,16 @@
             yield chunk * (size // 2) + step, base + 2 * (chip ^ step), core
 
 
-def pack_kernel(size, info, field, shared, *refs):
-    edges, outs, sides = refs[:4], refs[4:-1], refs[-1]
-    depth, height, width = field.shape
-    own = outs[0].shape[1] - 16
-    row = lax.broadcasted_iota(jnp.int32, edges[0].shape, 1) % 4
-    for which in range(2):
-        left = jnp.where(info[3] == 1, edges[2 * which][...], 0.0)
-        right = jnp.where(info[4] == 1, edges[2 * which + 1][...], 0.0)
-        sides[which] = jnp.where(row < 2, left, right).reshape(sides.shape[1:])
-    lane = lax.broadcasted_iota(jnp.int32, (4, LANES), 1)
-
-    def side_rows(which, plane, at, to):
-        chunk = sides[which, pl.ds(plane * (4 * height // LANES) + at // LANES * 4, 4), :]
-        return pltpu.roll(chunk, (to + LANES - at % LANES) % LANES, 1)
-
+def pack_kernel(size, shared, info, source, *refs):
+    outs = refs[-size:]
+    depth, own = source.shape[0], outs[0].shape[1] - 8
     for index, target, core in targets(size, info):
-        out = outs[index]
         target = target + core
         start = pl.multiple_of(target * own, 8)
-        for which in range(2):
-            for plane in range(depth):
-                slot = (core if which == 0 else 1 - core) * depth + plane
-                source = (field, shared)[which]
-                out[slot, 0:own, :] = source[plane, pl.ds(start, own), :]
-                out[slot, own : own + 8, :] = rows_around(source, plane, target, own)
-                top = side_rows(which, plane, jnp.maximum(start - 2, 0), 0)
-                end = side_rows(which, plane, jnp.minimum(start + own, height - 2), 2)
-                top = jnp.where(target > 0, top, 0.0)
-                end = jnp.where(start + own < height, end, 0.0)
-                out[slot, own + 8 : own + 12, :] = side_rows(which, plane, start, 0)
-                out[slot, own + 12 : own + 16, :] = jnp.where(lane < 2, top, end)
+        for plane in range(depth):
+            slot = (1 - core if shared else core) * depth + plane
+            outs[index][slot, 0:own, :] = source[plane, pl.ds(start, own), :]
+            outs[index][slot, own : own + 8, :] = rows_around(source, plane, target, own)
 
 
 def pick_kernel(size, info, *refs):
@@ -259,57 +248,53 @@
     info = jnp.stack([me % size // 2, me % 2, 1 - me // size, has_left, has_right]).astype(jnp.int32)
     weights = jnp.asarray(column_weights(width))
     f32 = jnp.float32
-    block = jax.ShapeDtypeStruct((2 * depth, own + 16, width), f32)
+    steps = size // 2
+    block = jax.ShapeDtypeStruct((2 * depth, own + 8, width), f32)
     image = jax.ShapeDtypeStruct((4, own, width), f32)
-    edge_groups = -(-depth * height // LANES // (LANES // 4))
 
     shared = lax.ppermute(field, "depth", [(i, i ^ 1) for i in range(groups)])
-    edges = pl.pallas_call(
-        edge_columns,
-        out_shape=jax.ShapeDtypeStruct((edge_groups, LANES, LANES), f32),
-        in_specs=[VMEM],
-        out_specs=VMEM,
-        compiler_params=PARAMS,
-        name="edge_columns",
-    )(field)
-
-    def from_column(flip, shifts):
-        route = []
-        for i in range(groups):
-            for j in range(columns):
-                for shift in shifts:
-                    if 0 <= j + shift < columns:
-                        route.append((i * columns + j, (i ^ flip) * columns + j + shift))
-        return lax.ppermute(edges, ("depth", "cols"), route)
-
-    sides = []
-    for flip in range(2):
+    blocks = ()
+    for source in (field, shared):
+        blocks = pl.pallas_call(
+            functools.partial(pack_kernel, size, source is shared),
+            out_shape=(block,) * size,
+            in_specs=[SMEM, VMEM] + [VMEM] * len(blocks),
+            out_specs=(VMEM,) * size,
+            input_output_aliases={2 + i: i for i in range(len(blocks))},
+            compiler_params=PARAMS,
+            name="pack_shared" if source is shared else "pack_own",
+        )(info, source, *blocks)
+
+    def columns_near(parts):
+        count = sum(part.shape[0] for part in parts)
+        edges = pl.pallas_call(
+            edge_kernel,
+            out_shape=jax.ShapeDtypeStruct((2, -(-count // (LANES // 4)) * LANES, LANES), f32),
+            in_specs=[VMEM] * len(parts),
+            out_specs=VMEM,
+            compiler_params=PARAMS,
+            cost_estimate=cost(1000, 1000),
+            name="edge_columns",
+        )(*parts)
         if columns == 2:
-            sides += [from_column(flip, (-1, 1))] * 2
-        else:
-            sides += [from_column(flip, (1,)), from_column(flip, (-1,))]
-    blocks = pl.pallas_call(
-        functools.partial(pack_kernel, size),
-        out_shape=(block,) * size,
-        in_specs=[SMEM] + [VMEM] * 6,
-        out_specs=(VMEM,) * size,
-        scratch_shapes=[pltpu.VMEM((2, edge_groups * LANES, LANES), f32)],
-        compiler_params=PARAMS,
-        name="pack_blocks",
-    )(info, field, shared, *sides)
-
-    def render_call(last):
+            return (lax.ppermute(edges, "cols", [(0, 1), (1, 0)]),) * 2
+        return tuple(
+            lax.ppermute(edges, "cols", [(i, i + shift) for i in range(columns) if 0 <= i + shift < columns])
+            for shift in (1, -1)
+        )
+
+    def render_call(last, parts):
         count = depth * size + (6 if last else 2)
         return pl.pallas_call(
             functools.partial(render_kernel, size, last),
             out_shape=image,
-            in_specs=[SMEM] + [VMEM] * (1 + size // 2 + (1 if last else 0)),
+            in_specs=[SMEM] + [VMEM] * (3 + len(parts)),
             out_specs=VMEM,
             scratch_shapes=[pltpu.VMEM((count, own + 16, width), f32)] * 2,
             compiler_params=PARAMS,
-            cost_estimate=cost(5_000_000_000, 2_000_000),
+            cost_estimate=cost(1000, 1000),
             name="render_last" if last else "render_first",
-        )
+        )(info, weights, *columns_near(parts), *parts)
 
     pick = pl.pallas_call(
         functools.partial(pick_kernel, size),
@@ -317,29 +302,33 @@
         in_specs=[SMEM] + [VMEM] * (size // 2),
         out_specs=VMEM,
         compiler_params=PARAMS,
+        cost_estimate=cost(1000, 1000),
         name="pick_boundary",
     )
 
     def swap(x, bits):
         return lax.ppermute(x, "depth", [(i, i ^ bits) for i in range(groups)])
 
-    def gathered(mine):
-        return [mine[0]] + [swap(mine[step], 2 * step) for step in range(1, size // 2)]
-
-    theirs = gathered(blocks[: size // 2])
+    def gathered(parts):
+        return [parts[0]] + [swap(parts[step], 2 * step) for step in range(1, steps)]
+
+    theirs = gathered(blocks[:steps])
     boundary = swap(pick(info, *theirs), size)
-    image_part = swap(render_call(False)(info, weights, *theirs), size)
-    mine = [blocks[size // 2]]
-    for step in range(1, size // 2):
-        held, _ = lax.optimization_barrier((blocks[size // 2 + step], theirs[step]))
+    first_image = render_call(False, theirs)
+    image_part = swap(first_image, size)
+    mine = [blocks[steps]]
+    for step in range(1, steps):
+        held, _ = lax.optimization_barrier((blocks[steps + step], theirs[step]))
         mine.append(swap(held, 2 * step))
-    own_part = render_call(True)(info, weights, *mine, boundary)
+    parts, _ = lax.optimization_barrier((mine + [boundary], first_image))
+    own_part = render_call(True, parts)
     return pl.pallas_call(
         join_kernel,
         out_shape=image,
         in_specs=[SMEM, VMEM, VMEM],
         out_specs=VMEM,
         compiler_params=PARAMS,
+        cost_estimate=cost(1000, 1000),
         name="join_halves",
     )(info, own_part, image_part)
 

time: 56.2 us -> 55.1 us (0.980)
  waiting for transfers between devices: 24.5 us -> 22.5 us
  starting transfers between devices: 17 us -> 17.7 us
    ppermute x8, waiting for transfers between devices: 20.3 us -> 14.1 us  [swap(): return lax.ppermute(x, 'depth', [(i, i ^ bits) for i in range(groups)])]
    ppermute x2, waiting for transfers between devices: 4.18 us -> 6.74 us  [columns_near(): return (lax.ppermute(edges, 'cols', [(0, 1), (1, 0)]),) * 2]
    ppermute x1, waiting for transfers between devices: 0.01 us -> 1.69 us  [local(): shared = lax.ppermute(field, 'depth', [(i, i ^ 1) for i in range(groups)])]
    ppermute x2, starting transfers between devices: 2.68 us -> 3.33 us  [columns_near(): return (lax.ppermute(edges, 'cols', [(0, 1), (1, 0)]),) * 2]
    pallas_call x4 -> x6, Pallas kernels: 11 us -> 10.6 us  [the longest x2 8.36 us: render_call(): pl.pallas_call(functools.partial(render_kernel, size, last), out_shape=im...]
    unnamed x6 -> x4, local copies, waits for them, and re-layouts: 1.6 us -> 1.6 us
  transfers between devices with their start and end apart: 11 -> 11, of which waited for: 9 -> 7; matrix products, arithmetic and copies ran while one was open for 0% -> 0% of each run, Pallas kernels for 17% -> 19%
where the time goes in v5:
time: 55.1 us; the launch traced here: 54.4 us
  waiting for transfers between devices  22.5 us (41%)
  starting transfers between devices  17.7 us (32%)
  Pallas kernels  12.5 us (23%)
  local copies, waits for them, and re-layouts  1.68 us (3%)
    ppermute x8, waiting for transfers between devices, swap(): return lax.ppermute(x, 'depth', [(i, i ^ bits) for i in range(groups)])  14.1 us
    ppermute x8, starting transfers between devices, swap(): return lax.ppermute(x, 'depth', [(i, i ^ bits) for i in range(groups)])  13.9 us
    pallas_call x2, Pallas kernels, render_call(): pl.pallas_call(functools.partial(render_kernel, size, last), out_shape=im...  8.36 us
    ppermute x2, waiting for transfers between devices, columns_near(): return (lax.ppermute(edges, 'cols', [(0, 1), (1, 0)]),) * 2  6.74 us
    ppermute x2, starting transfers between devices, columns_near(): return (lax.ppermute(edges, 'cols', [(0, 1), (1, 0)]),) * 2  3.33 us
    ppermute x1, waiting for transfers between devices, local(): shared = lax.ppermute(field, 'depth', [(i, i ^ 1) for i in range(groups)])  1.69 us
    unnamed x4, local copies, waits for them, and re-layouts  1.6 us
    pallas_call x1, Pallas kernels, local(): pl.pallas_call(join_kernel, out_shape=image, in_specs=[SMEM, VMEM, VMEM],...  1.31 us
  transfers between devices with their start and end apart: 11, of which 7 were waited for; matrix products, arithmetic and copies ran while one was open for 0% of the time, Pallas kernels for 19%

profile of v5, /device:TPU:0, one launch (start us, length us, event | category | flops | bytes accessed | tf_op | source)
XLA Modules:
  0.0 54.4 jit_solution(13917320254444954672)
XLA Ops:
  0.0 0.5 collective-permute-start
  0.5 1.6 %copy-done = f32[2,2048,128]{2,1,0:T(8,128)S(1)} copy-done((f32[2,2048,128]{2,1,0:T(8,128)S(1)}, f32[2,2048,128]{2,1,0:T(8,128)}, u32[]{:S(2)}) %copy-start) | copy-done | bytes 2097176
  2.1 0.6 %pack_own.1 = (f32[4,136,128]{2,1,0:T(8,128)S(1)}, f32[4,136,128]{2,1,0:T(8,128)S(1)}, f32[4,136,128]{2,1,0:T(8,128)S(1)}, f32[4,136,128]{2,1,0:T(8,128)S(1)}, f...) custom-call(s32[5]{0:T(128)S(1)} %stack.31.info, ...), custom_call_target="tpu_custom_call" | custom-call | tf_op jit(solution)/shard_map/pack_own/pallas_call | solution.py:258
  2.8 1.7 %collective-permute-done.source = f32[2,2048,128]{2,1,0:T(8,128)S(1)} collective-permute-done((f32[2,2048,128]{2,1,0:T(8,128)}, f32[2,2048,128]{2,1,0:T(8,128)S(1)}, u32[]{:S(2)}, u32[]{:S(2)}) %collective-permute-start) | collective-permute-done | bytes 2097184 | tf_op jit(solution)/shard_map/ppermute | solution.py:255
  4.5 0.6 %pack_shared.1 = (f32[4,136,128]{2,1,0:T(8,128)S(1)}, f32[4,136,128]{2,1,0:T(8,128)S(1)}, f32[4,136,128]{2,1,0:T(8,128)S(1)}, f32[4,136,128]{2,1,0:T(8,128)S(1)}...) custom-call(s32[5]{0:T(128)S(1)} %stack.31.info, ...), custom_call_target="tpu_custom_call", output_to_operand_aliasing={{0}: (2, {}), {1}: (3, {}), {2}: (4, {}), {3}: (5, {}), {4}... | custom-call | tf_op jit(solution)/shard_map/pack_shared/pallas_call | solution.py:258
  5.1 3.0 %collective-permute-start.1 = (f32[4,136,128]{2,1,0:T(8,128)S(1)}, f32[4,136,128]{2,1,0:T(8,128)S(1)}, u32[]{:S(2)}, u32[]{:S(2)}) collective-permute-start(f32[4,136,128]{2,1,0:T(8,128)S(1)} %get-tuple-element.39), channel_id=1, source_target_pairs={{0,4},{2,6},{4,0},{6,2},{8,12},{10,14},{12,8},{14,10},{16,20},{18,... | collective-permute-start | bytes 835592 | tf_op jit(solution)/shard_map/ppermute | solution.py:310
  8.1 1.6 %collective-permute-start.3 = (f32[4,136,128]{2,1,0:T(8,128)S(1)}, f32[4,136,128]{2,1,0:T(8,128)S(1)}, u32[]{:S(2)}, u32[]{:S(2)}) collective-permute-start(f32[4,136,128]{2,1,0:T(8,128)S(1)} %get-tuple-element.42), channel_id=1, source_target_pairs={{0,8},{2,10},{4,12},{6,14},{8,0},{10,2},{12,4},{14,6},{16,24},{18,... | collective-permute-start | bytes 835592 | tf_op jit(solution)/shard_map/ppermute | solution.py:310
  9.6 5.4 %collective-permute-done.1.refs_1_ = f32[4,136,128]{2,1,0:T(8,128)S(1)} collective-permute-done((f32[4,136,128]{2,1,0:T(8,128)S(1)}, f32[4,136,128]{2,1,0:T(8,128)S(1)}, u32[]{:S(2)}, u32[]{:S(2)}) %collective-permute-start.1) | collective-permute-done | bytes 278560 | tf_op jit(solution)/shard_map/ppermute | solution.py:310
  15.0 1.7 %collective-permute-start.2 = (f32[4,136,128]{2,1,0:T(8,128)S(1)}, f32[4,136,128]{2,1,0:T(8,128)S(1)}, u32[]{:S(2)}, u32[]{:S(2)}) collective-permute-start(f32[4,136,128]{2,1,0:T(8,128)S(1)} %get-tuple-element.40), channel_id=1, source_target_pairs={{0,4},{2,6},{4,0},{6,2},{8,12},{10,14},{12,8},{14,10},{16,20},{18,... | collective-permute-start | bytes 835592 | tf_op jit(solution)/shard_map/ppermute | solution.py:310
  16.8 0.8 %collective-permute-done.3.refs_2_ = f32[4,136,128]{2,1,0:T(8,128)S(1)} collective-permute-done((f32[4,136,128]{2,1,0:T(8,128)S(1)}, f32[4,136,128]{2,1,0:T(8,128)S(1)}, u32[]{:S(2)}, u32[]{:S(2)}) %collective-permute-start.3) | collective-permute-done | bytes 278560 | tf_op jit(solution)/shard_map/ppermute | solution.py:310
  17.6 1.6 %collective-permute-start.4 = (f32[4,136,128]{2,1,0:T(8,128)S(1)}, f32[4,136,128]{2,1,0:T(8,128)S(1)}, u32[]{:S(2)}, u32[]{:S(2)}) collective-permute-start(f32[4,136,128]{2,1,0:T(8,128)S(1)} %get-tuple-element.43), channel_id=1, source_target_pairs={{0,8},{2,10},{4,12},{6,14},{8,0},{10,2},{12,4},{14,6},{16,24},{18,... | collective-permute-start | bytes 835592 | tf_op jit(solution)/shard_map/ppermute | solution.py:310
  19.2 3.9 %collective-permute-done.5.refs_3_ = f32[4,136,128]{2,1,0:T(8,128)S(1)} collective-permute-done((f32[4,136,128]{2,1,0:T(8,128)S(1)}, f32[4,136,128]{2,1,0:T(8,128)S(1)}, u32[]{:S(2)}, u32[]{:S(2)}) %collective-permute-start.5) | collective-permute-done | bytes 278560 | tf_op jit(solution)/shard_map/ppermute | solution.py:310
  23.1 0.6 %pick_boundary.1 = f32[4,136,128]{2,1,0:T(8,128)S(1)} custom-call(s32[5]{0:T(128)S(1)} %stack.31.info, f32[4,136,128]{2,1,0:T(8,128)S(1)} %get-tuple-element.47.refs_0_, f32[4,136,128]{2,1,0:T(8,128)S(1)} %collective-permute-done.1.refs_1_, f32[4,136,128]{2,1,0:T(8,128)S(1)} %collective-permute-done.3.refs_2_, f32[4,136,128]{2,1,0:T(8,128)S(1)} %collective-permute-done.5.refs_3_), custom_call_target="tpu_custom_call" | custom-call | flops 1000 | bytes 1000 | tf_op jit(solution)/shard_map/pick_boundary/pallas_call | solution.py:316
  23.7 3.1 %collective-permute-start.7 = (f32[4,136,128]{2,1,0:T(8,128)S(1)}, f32[4,136,128]{2,1,0:T(8,128)S(1)}, u32[]{:S(2)}, u32[]{:S(2)}) collective-permute-start(f32[4,136,128]{2,1,0:T(8,128)S(1)} %pick_boundary.1), channel_id=1, source_target_pairs={{0,16},{2,18},{4,20},{6,22},{8,24},{10,26},{12,28},{14,30},{16,0},... | collective-permute-start | bytes 835592 | tf_op jit(solution)/shard_map/ppermute | solution.py:310
  26.8 2.5 %collective-permute-start.6 = (f32[4,136,128]{2,1,0:T(8,128)S(1)}, f32[4,136,128]{2,1,0:T(8,128)S(1)}, u32[]{:S(2)}, u32[]{:S(2)}) collective-permute-start(f32[4,136,128]{2,1,0:T(8,128)S(1)} %get-tuple-element.46), channel_id=1, source_target_pairs={{0,12},{2,14},{4,8},{6,10},{8,4},{10,6},{12,0},{14,2},{16,28},{18,... | collective-permute-start | bytes 835592 | tf_op jit(solution)/shard_map/ppermute | solution.py:310
  29.8 1.6 %collective-permute-start.8 = (f32[2,128,128]{2,1,0:T(8,128)S(1)}, f32[2,128,128]{2,1,0:T(8,128)S(1)}, u32[]{:S(2)}, u32[]{:S(2)}) collective-permute-start(f32[2,128,128]{2,1,0:T(8,128)S(1)} %edge_columns.2), channel_id=1, source_target_pairs={{0,1},{1,0},{2,3},{3,2},{4,5},{5,4},{6,7},{7,6},{8,9},{9,8},{10,11... | collective-permute-start | bytes 393224 | tf_op jit(solution)/shard_map/ppermute | solution.py:280
  31.3 3.5 %collective-permute-done.8.before.after = f32[2,128,128]{2,1,0:T(8,128)S(1)} collective-permute-done((f32[2,128,128]{2,1,0:T(8,128)S(1)}, f32[2,128,128]{2,1,0:T(8,128)S(1)}, u32[]{:S(2)}, u32[]{:S(2)}) %collective-permute-start.8) | collective-permute-done | bytes 131104 | tf_op jit(solution)/shard_map/ppermute | solution.py:280
  34.8 3.8 %render_first.1 = f32[4,128,128]{2,1,0:T(8,128)S(1)} custom-call(s32[5]{0:T(128)S(1)} %stack.31.info, bf16[512,256]{1,0:T(8,128)(2,1)S(1)} %copy-done.1, f32[2,128,128]{2,1,0:T(8,128)S(1)} %collective-permute-done.8.before.after, f32[2,128,128]{2,1,0:T(8,128)S(1)} %collective-permute-done.8.before.after, f32[4,136,128]{2,1,0:T(8,128)S(1)} %get-tuple-element.47.refs_0_, ...), custom_call_target="tpu_custom_call" | custom-call | flops 1000 | bytes 1000 | tf_op jit(solution)/shard_map/render_first/pallas_call | solution.py:288
  39.0 4.0 %collective-permute-done.6.refs_3_ = f32[4,136,128]{2,1,0:T(8,128)S(1)} collective-permute-done((f32[4,136,128]{2,1,0:T(8,128)S(1)}, f32[4,136,128]{2,1,0:T(8,128)S(1)}, u32[]{:S(2)}, u32[]{:S(2)}) %collective-permute-start.6) | collective-permute-done | bytes 278560 | tf_op jit(solution)/shard_map/ppermute | solution.py:310
  43.0 0.5 edge_columns.3
  43.5 1.8 %collective-permute-start.9 = (f32[2,128,128]{2,1,0:T(8,128)S(1)}, f32[2,128,128]{2,1,0:T(8,128)S(1)}, u32[]{:S(2)}, u32[]{:S(2)}) collective-permute-start(f32[2,128,128]{2,1,0:T(8,128)S(1)} %edge_columns.3), channel_id=1, source_target_pairs={{0,1},{1,0},{2,3},{3,2},{4,5},{5,4},{6,7},{7,6},{8,9},{9,8},{10,11... | collective-permute-start | bytes 393224 | tf_op jit(solution)/shard_map/ppermute | solution.py:280
  45.3 3.3 %collective-permute-done.9.before.after = f32[2,128,128]{2,1,0:T(8,128)S(1)} collective-permute-done((f32[2,128,128]{2,1,0:T(8,128)S(1)}, f32[2,128,128]{2,1,0:T(8,128)S(1)}, u32[]{:S(2)}, u32[]{:S(2)}) %collective-permute-start.9) | collective-permute-done | bytes 131104 | tf_op jit(solution)/shard_map/ppermute | solution.py:280
  48.5 4.6 %render_last.1.mine = f32[4,128,128]{2,1,0:T(8,128)S(1)} custom-call(s32[5]{0:T(128)S(1)} %stack.31.info, bf16[512,256]{1,0:T(8,128)(2,1)S(1)} %copy-done.1, f32[2,128,128]{2,1,0:T(8,128)S(1)} %collective-permute-done.9.before.after, f32[2,128,128]{2,1,0:T(8,128)S(1)} %collective-permute-done.9.before.after, f32[4,136,128]{2,1,0:T(8,128)S(1)} %get-tuple-element.48.refs_0_, ...), custom_call_target="tpu_custom_call" | custom-call | flops 1000 | bytes 1000 | tf_op jit(solution)/shard_map/render_last/pallas_call | solution.py:288
  53.1 1.3 %join_halves.1 = f32[4,128,128]{2,1,0:T(8,128)} custom-call(s32[5]{0:T(128)S(1)} %stack.31.info, f32[4,128,128]{2,1,0:T(8,128)S(1)} %render_last.1.mine, f32[4,128,128]{2,1,0:T(8,128)S(1)} %collective-permute-done.10.other), custom_call_target="tpu_custom_call" | custom-call | flops 1000 | bytes 1000 | tf_op jit(solution)/shard_map/join_halves/pallas_call | solution.py:325
  (11 shorter events, 1.0 us)
Async XLA Ops:
  0.0 4.5 %collective-permute-start = (f32[2,2048,128]{2,1,0:T(8,128)}, f32[2,2048,128]{2,1,0:T(8,128)S(1)}, u32[]{:S(2)}, u32[]{:S(2)}) collective-permute-start(f32[2,2048,128]{2,1,0:T(8,128)} %source.1), channel_id=1, source_target_pairs={{0,2},{2,0},{4,6},{6,4},{8,10},{10,8},{12,14},{14,12},{16,18},{18,... | collective-permute-start | bytes 6291464 | tf_op jit(solution)/shard_map/ppermute | solution.py:255
  0.5 1.6 %copy-start = (f32[2,2048,128]{2,1,0:T(8,128)S(1)}, f32[2,2048,128]{2,1,0:T(8,128)}, u32[]{:S(2)}) copy-start(f32[2,2048,128]{2,1,0:T(8,128)} %source.1) | copy-start | bytes 6291460
  5.1 29.7 %copy-start.1 = (bf16[512,256]{1,0:T(8,128)(2,1)S(1)}, bf16[512,256]{1,0:T(8,128)(2,1)}, u32[]{:S(2)}) copy-start(bf16[512,256]{1,0:T(8,128)(2,1)} %constant.55.clone.weights) | copy-start | bytes 786436
  5.1 9.9 %collective-permute-start.1 = (f32[4,136,128]{2,1,0:T(8,128)S(1)}, f32[4,136,128]{2,1,0:T(8,128)S(1)}, u32[]{:S(2)}, u32[]{:S(2)}) collective-permute-start(f32[4,136,128]{2,1,0:T(8,128)S(1)} %get-tuple-element.39), channel_id=1, source_target_pairs={{0,4},{2,6},{4,0},{6,2},{8,12},{10,14},{12,8},{14,10},{16,20},{18,... | collective-permute-start | bytes 835592 | tf_op jit(solution)/shard_map/ppermute | solution.py:310
  8.1 9.5 %collective-permute-start.3 = (f32[4,136,128]{2,1,0:T(8,128)S(1)}, f32[4,136,128]{2,1,0:T(8,128)S(1)}, u32[]{:S(2)}, u32[]{:S(2)}) collective-permute-start(f32[4,136,128]{2,1,0:T(8,128)S(1)} %get-tuple-element.42), channel_id=1, source_target_pairs={{0,8},{2,10},{4,12},{6,14},{8,0},{10,2},{12,4},{14,6},{16,24},{18,... | collective-permute-start | bytes 835592 | tf_op jit(solution)/shard_map/ppermute | solution.py:310
  9.6 13.4 %collective-permute-start.5 = (f32[4,136,128]{2,1,0:T(8,128)S(1)}, f32[4,136,128]{2,1,0:T(8,128)S(1)}, u32[]{:S(2)}, u32[]{:S(2)}) collective-permute-start(f32[4,136,128]{2,1,0:T(8,128)S(1)} %get-tuple-element.45), channel_id=1, source_target_pairs={{0,12},{2,14},{4,8},{6,10},{8,4},{10,6},{12,0},{14,2},{16,28},{18,... | collective-permute-start | bytes 835592 | tf_op jit(solution)/shard_map/ppermute | solution.py:310
  15.0 24.0 %collective-permute-start.2 = (f32[4,136,128]{2,1,0:T(8,128)S(1)}, f32[4,136,128]{2,1,0:T(8,128)S(1)}, u32[]{:S(2)}, u32[]{:S(2)}) collective-permute-start(f32[4,136,128]{2,1,0:T(8,128)S(1)} %get-tuple-element.40), channel_id=1, source_target_pairs={{0,4},{2,6},{4,0},{6,2},{8,12},{10,14},{12,8},{14,10},{16,20},{18,... | collective-permute-start | bytes 835592 | tf_op jit(solution)/shard_map/ppermute | solution.py:310
  17.6 21.4 %collective-permute-start.4 = (f32[4,136,128]{2,1,0:T(8,128)S(1)}, f32[4,136,128]{2,1,0:T(8,128)S(1)}, u32[]{:S(2)}, u32[]{:S(2)}) collective-permute-start(f32[4,136,128]{2,1,0:T(8,128)S(1)} %get-tuple-element.43), channel_id=1, source_target_pairs={{0,8},{2,10},{4,12},{6,14},{8,0},{10,2},{12,4},{14,6},{16,24},{18,... | collective-permute-start | bytes 835592 | tf_op jit(solution)/shard_map/ppermute | solution.py:310
  23.7 15.3 %collective-permute-start.7 = (f32[4,136,128]{2,1,0:T(8,128)S(1)}, f32[4,136,128]{2,1,0:T(8,128)S(1)}, u32[]{:S(2)}, u32[]{:S(2)}) collective-permute-start(f32[4,136,128]{2,1,0:T(8,128)S(1)} %pick_boundary.1), channel_id=1, source_target_pairs={{0,16},{2,18},{4,20},{6,22},{8,24},{10,26},{12,28},{14,30},{16,0},... | collective-permute-start | bytes 835592 | tf_op jit(solution)/shard_map/ppermute | solution.py:310
  26.8 16.2 %collective-permute-start.6 = (f32[4,136,128]{2,1,0:T(8,128)S(1)}, f32[4,136,128]{2,1,0:T(8,128)S(1)}, u32[]{:S(2)}, u32[]{:S(2)}) collective-permute-start(f32[4,136,128]{2,1,0:T(8,128)S(1)} %get-tuple-element.46), channel_id=1, source_target_pairs={{0,12},{2,14},{4,8},{6,10},{8,4},{10,6},{12,0},{14,2},{16,28},{18,... | collective-permute-start | bytes 835592 | tf_op jit(solution)/shard_map/ppermute | solution.py:310
  29.8 5.0 %collective-permute-start.8 = (f32[2,128,128]{2,1,0:T(8,128)S(1)}, f32[2,128,128]{2,1,0:T(8,128)S(1)}, u32[]{:S(2)}, u32[]{:S(2)}) collective-permute-start(f32[2,128,128]{2,1,0:T(8,128)S(1)} %edge_columns.2), channel_id=1, source_target_pairs={{0,1},{1,0},{2,3},{3,2},{4,5},{5,4},{6,7},{7,6},{8,9},{9,8},{10,11... | collective-permute-start | bytes 393224 | tf_op jit(solution)/shard_map/ppermute | solution.py:280
  38.6 14.5 %collective-permute-start.10 = (f32[4,128,128]{2,1,0:T(8,128)S(1)}, f32[4,128,128]{2,1,0:T(8,128)S(1)}, u32[]{:S(2)}, u32[]{:S(2)}) collective-permute-start(f32[4,128,128]{2,1,0:T(8,128)S(1)} %render_first.1), channel_id=1, source_target_pairs={{0,16},{2,18},{4,20},{6,22},{8,24},{10,26},{12,28},{14,30},{16,0},... | collective-permute-start | bytes 786440 | tf_op jit(solution)/shard_map/ppermute | solution.py:310
  43.5 5.0 %collective-permute-start.9 = (f32[2,128,128]{2,1,0:T(8,128)S(1)}, f32[2,128,128]{2,1,0:T(8,128)S(1)}, u32[]{:S(2)}, u32[]{:S(2)}) collective-permute-start(f32[2,128,128]{2,1,0:T(8,128)S(1)} %edge_columns.3), channel_id=1, source_target_pairs={{0,1},{1,0},{2,3},{3,2},{4,5},{5,4},{6,7},{7,6},{8,9},{9,8},{10,11... | collective-permute-start | bytes 393224 | tf_op jit(solution)/shard_map/ppermute | solution.py:280

commit v6 on v5

--- a/solution.py
+++ b/solution.py
@@ -22,20 +22,12 @@
 
 def column_weights(width):
     body = np.zeros((width, 2 * width), np.float32)
-    halo = np.zeros((4, 2 * width), np.float32)
     for out in range(width):
         for k in range(5):
-            col = out - 2 + k
-            for part, taps in enumerate((GAUSS, DERIV)):
-                value = SCALE * taps[k]
-                if 0 <= col < width:
-                    body[col, part * width + out] = value
-                else:
-                    halo[col + 2 if col < 0 else col - width + 2, part * width + out] = value
-    side = np.zeros((LANES, 2 * width), np.float32)
-    for row in range(24):
-        side[row] = halo[row % 4]
-    return np.concatenate([body, body, body, side], 0).astype(jnp.bfloat16)
+            if 0 <= out - 2 + k < width:
+                body[out - 2 + k, out] = SCALE * GAUSS[k]
+                body[out - 2 + k, width + out] = SCALE * DERIV[k]
+    return np.concatenate([body, body, body], 0).astype(jnp.bfloat16)
 
 
 def three_parts(x):
@@ -46,15 +38,9 @@
     return hi, mid, lo
 
 
-def filter_columns(block, plane, side, own, weights, sx, dx, slot):
+def filter_columns(block, plane, own, weights, sx, dx, slot):
     width = block.shape[-1]
-    hi, mid, lo = three_parts(block[plane])
-    sides = [part.astype(jnp.float32) for part in three_parts(side)]
-    lanes_first = jnp.transpose(jnp.concatenate(sides, 0))
-    inner = lax.broadcasted_iota(jnp.int32, lanes_first.shape, 1) % 8 < 4
-    halo = jnp.concatenate([jnp.where(inner, lanes_first, 0.0)[0:own], jnp.where(inner, 0.0, lanes_first)[0:8]], 0)
-    halo = jnp.concatenate([halo, jnp.zeros((own + 8, LANES - halo.shape[1]), jnp.float32)], 1)
-    row = jnp.concatenate([hi, mid, lo, halo.astype(jnp.bfloat16)], 1)
+    row = jnp.concatenate(three_parts(block[plane]), 1)
     both = jnp.dot(row, weights[...], preferred_element_type=jnp.float32)
     for out, part in ((sx, both[:, :width]), (dx, both[:, width:])):
         out[slot, 8 : 8 + own] = part[0:own]
@@ -83,16 +69,13 @@
     return v_sum + value, vt_sum + value * tanh_t, vu_sum + value * tanh_u, cover + part
 
 
-def render(sx, dx, first, count):
-    def rows_of(ref, slot):
-        return [ref[slot, pl.ds(first + 6 + k, TILE), :] for k in range(5)]
-
-    zero = jnp.zeros((TILE, sx.shape[2]), jnp.float32)
+def render(smooth_rows, slope_rows, shape, count):
+    zero = jnp.zeros(shape, jnp.float32)
     state = (zero, zero, zero, zero)
     chains = [[None] * 4 for _ in range(3)]
     for index in range(count + 4):
-        a, b, c, d, e = rows_of(sx, index)
-        inputs = [gauss_rows(a, b, c, d, e), (e - a) + 2.0 * (d - b), gauss_rows(*rows_of(dx, index))]
+        a, b, c, d, e = smooth_rows(index)
+        inputs = [gauss_rows(a, b, c, d, e), (e - a) + 2.0 * (d - b), gauss_rows(*slope_rows(index))]
         totals, diff = [], None
         for which, (chain, x) in enumerate(zip(chains, inputs)):
             for level in range(4):
@@ -114,47 +97,112 @@
     return tuple(f + rest * b for f, b in zip(front, back))
 
 
-def render_kernel(size, last, info, weights, before, after, *refs):
-    steps = size // 2
-    blocks, (image, sx, dx) = refs[:-3], refs[-3:]
-    depth, own = blocks[0].shape[0], image.shape[1]
-    planes = depth * steps
+def plane_slots(size, depth, last, info):
+    planes = depth * (size // 2)
     extra = 4 if last else 0
     chip, front = info[0], info[2]
     start = 2 * front + extra * (1 - front)
-    empty = (1 - front) * (planes + extra)
-    sx[pl.ds(empty, 2)] = jnp.zeros((2,) + sx.shape[1:], jnp.float32)
-    dx[pl.ds(empty, 2)] = jnp.zeros((2,) + dx.shape[1:], jnp.float32)
-    line = lax.broadcasted_iota(jnp.int32, (8, LANES), 0) % 4
-    from_left = (line < 2) & (info[3] == 1)
-    from_right = (line >= 2) & (info[4] == 1)
-
-    def side(index):
-        left, right = (
-            jnp.concatenate([ref[0, 4 * index : 4 * index + 4], ref[1, 4 * index : 4 * index + 4]], 0)
-            for ref in (before, after)
-        )
-        return jnp.where(from_left, left, jnp.where(from_right, right, 0.0))
-
-    for step in range(steps):
-        for plane in range(depth):
-            slot = (chip ^ step) * depth + plane + start
-            filter_columns(blocks[step], plane, side(step * depth + plane), own, weights, sx, dx, slot)
-    for plane in range(extra):
-        slot = (planes + 2) * front + plane
-        filter_columns(blocks[steps], plane, side(planes + plane), own, weights, sx, dx, slot)
+    slots = [(chip ^ step) * depth + plane + start for step in range(size // 2) for plane in range(depth)]
+    return slots + [(planes + 2) * front + plane for plane in range(extra)], (1 - front) * (planes + extra)
+
+
+def render_kernel(size, last, info, weights, *refs):
+    blocks, (image, sx, dx) = refs[:-3], refs[-3:]
+    depth, own = blocks[0].shape[0], image.shape[1]
+    slots, empty = plane_slots(size, depth, last, info)
+    for out in (sx, dx):
+        out[pl.ds(empty, 2)] = jnp.zeros((2,) + out.shape[1:], jnp.float32)
+    for index, slot in enumerate(slots):
+        filter_columns(blocks[index // depth], index % depth, own, weights, sx, dx, slot)
 
     @pl.loop(0, own // TILE)
     def _(tile):
         first = pl.multiple_of(tile * TILE, TILE)
-        total = render(sx, dx, first, planes - 2 + extra)
+
+        def rows_of(ref):
+            return lambda index: [ref[index, pl.ds(first + 6 + k, TILE), :] for k in range(5)]
+
+        total = render(rows_of(sx), rows_of(dx), (TILE, sx.shape[2]), len(slots) - 2)
         for channel in range(4):
             image[channel, pl.ds(first, TILE), :] = total[channel]
 
 
-def join_kernel(info, mine, other, picture):
+def edge_kernel(*refs):
+    blocks, out = refs[:-1], refs[-1]
+    own, width = blocks[0].shape[1] - 8, blocks[0].shape[2]
+    places = [(block, plane) for block in blocks for plane in range(block.shape[0])]
+    group = LANES // 8
+    lane = lax.broadcasted_iota(jnp.int32, (own + 8, width), 1) // 8
+    for base in range(0, len(places), group):
+        packed = jnp.zeros((own + 8, width), jnp.float32)
+        for at, (block, plane) in enumerate(places[base : base + group]):
+            packed = jnp.where(lane == at, pltpu.roll(block[plane], (8 * at + 4) % width, 1), packed)
+        for part, rows in enumerate((packed[0:own], packed[own:])):
+            missing = LANES - rows.shape[0]
+            if missing:
+                rows = jnp.concatenate([rows, jnp.zeros((missing, width), jnp.float32)], 0)
+            out[part, base : base + group] = jnp.transpose(rows).reshape(group, 8, LANES)
+
+
+def render_edges(size, depth, last, own, info, mine, before, after, sx, dx):
+    slots, empty = plane_slots(size, depth, last, info)
+    count = len(slots)
+    lane = lax.broadcasted_iota(jnp.int32, (count, 8, LANES), 2)
+    line = lax.broadcasted_iota(jnp.int32, (count, 8, 2 * LANES), 1)
+
+    def all_rows(ref):
+        main, around = ref[0, 0:count], ref[1, 0:count]
+        if own < LANES:
+            main = jnp.where(lane < own, main, pltpu.roll(around, own - 2, 2))
+        return jnp.concatenate([main, pltpu.roll(around, LANES - 2, 2)], 2)
+
+    mid = all_rows(mine)
+    left = jnp.where(info[3] == 1, all_rows(before), 0.0)
+    right = jnp.where(info[4] == 1, all_rows(after), 0.0)
+    end = jnp.where(line < 4, mid, right)
+    top = jnp.where(line < 4, left, mid)
+    taps = [jnp.where(line < 2, end, top)]
+    for k in range(1, 5):
+        taps.append(jnp.where(line < 2, pltpu.roll(end, 8 - k, 1), pltpu.roll(top, 8 - k, 1)))
+    a, b, c, d, e = taps
+    smooth = SCALE * gauss_rows(a, b, c, d, e)
+    slope = SCALE * ((e - a) + 2.0 * (d - b))
+    for out, values in ((sx, smooth), (dx, slope)):
+        out[pl.ds(empty, 2)] = jnp.zeros((2,) + out.shape[1:], jnp.float32)
+        for index, slot in enumerate(slots):
+            out[slot] = values[index]
+
+    def rows_of(ref):
+        def five(index):
+            rows = ref[index]
+            return [pltpu.roll(rows, k % (2 * LANES), 1)[:, :LANES] for k in (2, 1, 0, -1, -2)]
+
+        return five
+
+    return render(rows_of(sx), rows_of(dx), (8, LANES), count - 2)
+
+
+def with_edges(state, image):
+    own, width = image.shape[1:]
+    rows = jnp.concatenate(list(state) + [jnp.zeros((LANES - 32, LANES), jnp.float32)], 0)
+    columns = jnp.transpose(rows)[0:own]
+    lane = lax.broadcasted_iota(jnp.int32, columns.shape, 1)
+    inside = (lane >= 2) & (lane < width - 2)
+    return [
+        jnp.where(inside, image[channel], pltpu.roll(columns, width - 2 - 8 * channel, 1)) for channel in range(4)
+    ]
+
+
+def fix_kernel(size, depth, info, mine, before, after, image, out, sx, dx):
+    state = render_edges(size, depth, False, image.shape[1], info, mine, before, after, sx, dx)
+    for channel, values in enumerate(with_edges(state, image)):
+        out[channel] = values
+
+
+def join_kernel(size, depth, info, mine, before, after, own_part, other, picture, sx, dx):
+    state = render_edges(size, depth, True, picture.shape[1], info, mine, before, after, sx, dx)
     is_front = info[2] == 1
-    mine = tuple(mine[channel] for channel in range(4))
+    mine = with_edges(state, own_part)
     other = tuple(other[channel] for channel in range(4))
     ahead = tuple(jnp.where(is_front, m, o) for m, o in zip(mine, other))
     behind = tuple(jnp.where(is_front, o, m) for m, o in zip(mine, other))
@@ -163,23 +211,6 @@
     picture[1] = 0.5 * v_sum + 0.4 * vt_sum
     picture[2] = 0.5 * (v_sum - vt_sum)
     picture[3] = cover
-
-
-def edge_kernel(*refs):
-    blocks, out = refs[:-1], refs[-1]
-    own, width = blocks[0].shape[1] - 8, blocks[0].shape[2]
-    places = [(block, plane) for block in blocks for plane in range(block.shape[0])]
-    group = LANES // 4
-    lane = lax.broadcasted_iota(jnp.int32, (own + 8, width), 1) // 4
-    for base in range(0, len(places), group):
-        packed = jnp.zeros((own + 8, width), jnp.float32)
-        for at, (block, plane) in enumerate(places[base : base + group]):
-            packed = jnp.where(lane == at, pltpu.roll(block[plane], (4 * at + 2) % width, 1), packed)
-        for part, rows in enumerate((packed[0:own], packed[own:])):
-            missing = LANES - rows.shape[0]
-            if missing:
-                rows = jnp.concatenate([rows, jnp.zeros((missing, width), jnp.float32)], 0)
-            out[part, 4 * base : 4 * base + LANES] = jnp.transpose(rows)
 
 
 def rows_around(field, plane, target, own):
@@ -265,11 +296,24 @@
             name="pack_shared" if source is shared else "pack_own",
         )(info, source, *blocks)
 
+    def call(kernel, name, out_shape, *args, **more):
+        return pl.pallas_call(
+            kernel,
+            out_shape=out_shape,
+            in_specs=[SMEM] + [VMEM] * (len(args) - 1),
+            out_specs=jax.tree.map(lambda _: VMEM, out_shape),
+            compiler_params=PARAMS,
+            cost_estimate=cost(1000, 1000),
+            name=name,
+            **more,
+        )(*args)
+
     def columns_near(parts):
         count = sum(part.shape[0] for part in parts)
+        group = LANES // 8
         edges = pl.pallas_call(
             edge_kernel,
-            out_shape=jax.ShapeDtypeStruct((2, -(-count // (LANES // 4)) * LANES, LANES), f32),
+            out_shape=jax.ShapeDtypeStruct((2, -(-count // group) * group, 8, LANES), f32),
             in_specs=[VMEM] * len(parts),
             out_specs=VMEM,
             compiler_params=PARAMS,
@@ -277,24 +321,20 @@
             name="edge_columns",
         )(*parts)
         if columns == 2:
-            return (lax.ppermute(edges, "cols", [(0, 1), (1, 0)]),) * 2
-        return tuple(
+            return (edges,) + (lax.ppermute(edges, "cols", [(0, 1), (1, 0)]),) * 2
+        return (edges,) + tuple(
             lax.ppermute(edges, "cols", [(i, i + shift) for i in range(columns) if 0 <= i + shift < columns])
             for shift in (1, -1)
         )
 
+    def plane_scratch(last, rows, lanes):
+        return [pltpu.VMEM((depth * size + (6 if last else 2), rows, lanes), f32)] * 2
+
     def render_call(last, parts):
-        count = depth * size + (6 if last else 2)
-        return pl.pallas_call(
-            functools.partial(render_kernel, size, last),
-            out_shape=image,
-            in_specs=[SMEM] + [VMEM] * (3 + len(parts)),
-            out_specs=VMEM,
-            scratch_shapes=[pltpu.VMEM((count, own + 16, width), f32)] * 2,
-            compiler_params=PARAMS,
-            cost_estimate=cost(1000, 1000),
-            name="render_last" if last else "render_first",
-        )(info, weights, *columns_near(parts), *parts)
+        kernel = functools.partial(render_kernel, size, last)
+        scratch = plane_scratch(last, own + 16, width)
+        name = "render_last" if last else "render_first"
+        return call(kernel, name, image, info, weights, *parts, scratch_shapes=scratch)
 
     pick = pl.pallas_call(
         functools.partial(pick_kernel, size),
@@ -315,6 +355,11 @@
     theirs = gathered(blocks[:steps])
     boundary = swap(pick(info, *theirs), size)
     first_image = render_call(False, theirs)
+    kernel = functools.partial(fix_kernel, size, 2 * depth)
+    scratch = plane_scratch(False, 8, 2 * LANES)
+    first_image = call(
+        kernel, "first_edges", image, info, *columns_near(theirs), first_image, scratch_shapes=scratch
+    )
     image_part = swap(first_image, size)
     mine = [blocks[steps]]
     for step in range(1, steps):
@@ -322,15 +367,11 @@
         mine.append(swap(held, 2 * step))
     parts, _ = lax.optimization_barrier((mine + [boundary], first_image))
     own_part = render_call(True, parts)
-    return pl.pallas_call(
-        join_kernel,
-        out_shape=image,
-        in_specs=[SMEM, VMEM, VMEM],
-        out_specs=VMEM,
-        compiler_params=PARAMS,
-        cost_estimate=cost(1000, 1000),
-        name="join_halves",
-    )(info, own_part, image_part)
+    kernel = functools.partial(join_kernel, size, 2 * depth)
+    scratch = plane_scratch(True, 8, 2 * LANES)
+    return call(
+        kernel, "join_halves", image, info, *columns_near(parts), own_part, image_part, scratch_shapes=scratch
+    )
 
 
 def solution(mesh):

time: 55.1 us -> 54.2 us (0.984)
  waiting for transfers between devices: 22.5 us -> 20.1 us
  Pallas kernels: 12.5 us -> 14.6 us
    ppermute x2, waiting for transfers between devices: 6.74 us -> 0.97 us  [columns_near(): return (edges,) + (lax.ppermute(edges, 'cols', [(0, 1), (1, 0)]),) * 2]
    ppermute x8, waiting for transfers between devices: 14.1 us -> 17.4 us  [swap(): return lax.ppermute(x, 'depth', [(i, i ^ bits) for i in range(groups)])]
    pallas_call x3 -> x4, Pallas kernels: 9.66 us -> 11.8 us  [call(): pl.pallas_call(kernel, out_shape=out_shape, in_specs=[SMEM] + [VMEM] * (l...]
  transfers between devices with their start and end apart: 11 -> 11, of which waited for: 7 -> 7; matrix products, arithmetic and copies ran while one was open for 0% -> 0% of each run, Pallas kernels for 19% -> 22%
where the time goes in v6:
time: 54.2 us; the launch traced here: 54.1 us
  waiting for transfers between devices  20.1 us (37%)
  starting transfers between devices  17.6 us (32%)
  Pallas kernels  14.6 us (27%)
  local copies, waits for them, and re-layouts  1.68 us (3%)
    ppermute x8, waiting for transfers between devices, swap(): return lax.ppermute(x, 'depth', [(i, i ^ bits) for i in range(groups)])  17.4 us
    ppermute x8, starting transfers between devices, swap(): return lax.ppermute(x, 'depth', [(i, i ^ bits) for i in range(groups)])  13.9 us
    pallas_call x4, Pallas kernels, call(): pl.pallas_call(kernel, out_shape=out_shape, in_specs=[SMEM] + [VMEM] * (l...  11.8 us
    ppermute x2, starting transfers between devices, columns_near(): return (edges,) + (lax.ppermute(edges, 'cols', [(0, 1), (1, 0)]),) * 2  3.26 us
    ppermute x1, waiting for transfers between devices, local(): shared = lax.ppermute(field, 'depth', [(i, i ^ 1) for i in range(groups)])  1.69 us
    unnamed x4, local copies, waits for them, and re-layouts  1.6 us
    pallas_call x2, Pallas kernels, local(): pl.pallas_call(functools.partial(pack_kernel, size, source is shared), ou...  1.26 us
  transfers between devices with their start and end apart: 11, of which 7 were waited for; matrix products, arithmetic and copies ran while one was open for 0% of the time, Pallas kernels for 22%

profile of v6, /device:TPU:0, one launch (start us, length us, event | category | flops | bytes accessed | tf_op | source)
XLA Modules:
  0.0 54.1 jit_solution(15018651591480868825)
XLA Ops:
  0.5 1.6 %copy-done = f32[2,2048,128]{2,1,0:T(8,128)S(1)} copy-done((f32[2,2048,128]{2,1,0:T(8,128)S(1)}, f32[2,2048,128]{2,1,0:T(8,128)}, u32[]{:S(2)}) %copy-start) | copy-done | bytes 2097176
  2.1 0.6 %pack_own.1 = (f32[4,136,128]{2,1,0:T(8,128)S(1)}, f32[4,136,128]{2,1,0:T(8,128)S(1)}, f32[4,136,128]{2,1,0:T(8,128)S(1)}, f32[4,136,128]{2,1,0:T(8,128)S(1)}, f...) custom-call(s32[5]{0:T(128)S(1)} %stack.31.info, ...), custom_call_target="tpu_custom_call" | custom-call | tf_op jit(solution)/shard_map/pack_own/pallas_call | solution.py:289
  2.8 1.7 %collective-permute-done.source = f32[2,2048,128]{2,1,0:T(8,128)S(1)} collective-permute-done((f32[2,2048,128]{2,1,0:T(8,128)}, f32[2,2048,128]{2,1,0:T(8,128)S(1)}, u32[]{:S(2)}, u32[]{:S(2)}) %collective-permute-start) | collective-permute-done | bytes 2097184 | tf_op jit(solution)/shard_map/ppermute | solution.py:286
  4.5 0.6 %pack_shared.1 = (f32[4,136,128]{2,1,0:T(8,128)S(1)}, f32[4,136,128]{2,1,0:T(8,128)S(1)}, f32[4,136,128]{2,1,0:T(8,128)S(1)}, f32[4,136,128]{2,1,0:T(8,128)S(1)}...) custom-call(s32[5]{0:T(128)S(1)} %stack.31.info, ...), custom_call_target="tpu_custom_call", output_to_operand_aliasing={{0}: (2, {}), {1}: (3, {}), {2}: (4, {}), {3}: (5, {}), {4}... | custom-call | tf_op jit(solution)/shard_map/pack_shared/pallas_call | solution.py:289
  5.1 3.0 %collective-permute-start.1 = (f32[4,136,128]{2,1,0:T(8,128)S(1)}, f32[4,136,128]{2,1,0:T(8,128)S(1)}, u32[]{:S(2)}, u32[]{:S(2)}) collective-permute-start(f32[4,136,128]{2,1,0:T(8,128)S(1)} %get-tuple-element.39), channel_id=1, source_target_pairs={{0,4},{2,6},{4,0},{6,2},{8,12},{10,14},{12,8},{14,10},{16,20},{18,... | collective-permute-start | bytes 835592 | tf_op jit(solution)/shard_map/ppermute | solution.py:350
  8.1 1.6 %collective-permute-start.3 = (f32[4,136,128]{2,1,0:T(8,128)S(1)}, f32[4,136,128]{2,1,0:T(8,128)S(1)}, u32[]{:S(2)}, u32[]{:S(2)}) collective-permute-start(f32[4,136,128]{2,1,0:T(8,128)S(1)} %get-tuple-element.42), channel_id=1, source_target_pairs={{0,8},{2,10},{4,12},{6,14},{8,0},{10,2},{12,4},{14,6},{16,24},{18,... | collective-permute-start | bytes 835592 | tf_op jit(solution)/shard_map/ppermute | solution.py:350
  9.6 5.4 %collective-permute-done.1.refs_1_ = f32[4,136,128]{2,1,0:T(8,128)S(1)} collective-permute-done((f32[4,136,128]{2,1,0:T(8,128)S(1)}, f32[4,136,128]{2,1,0:T(8,128)S(1)}, u32[]{:S(2)}, u32[]{:S(2)}) %collective-permute-start.1) | collective-permute-done | bytes 278560 | tf_op jit(solution)/shard_map/ppermute | solution.py:350
  15.0 1.7 %collective-permute-start.2 = (f32[4,136,128]{2,1,0:T(8,128)S(1)}, f32[4,136,128]{2,1,0:T(8,128)S(1)}, u32[]{:S(2)}, u32[]{:S(2)}) collective-permute-start(f32[4,136,128]{2,1,0:T(8,128)S(1)} %get-tuple-element.40), channel_id=1, source_target_pairs={{0,4},{2,6},{4,0},{6,2},{8,12},{10,14},{12,8},{14,10},{16,20},{18,... | collective-permute-start | bytes 835592 | tf_op jit(solution)/shard_map/ppermute | solution.py:350
  16.8 0.8 %collective-permute-done.3.refs_2_ = f32[4,136,128]{2,1,0:T(8,128)S(1)} collective-permute-done((f32[4,136,128]{2,1,0:T(8,128)S(1)}, f32[4,136,128]{2,1,0:T(8,128)S(1)}, u32[]{:S(2)}, u32[]{:S(2)}) %collective-permute-start.3) | collective-permute-done | bytes 278560 | tf_op jit(solution)/shard_map/ppermute | solution.py:350
  17.6 1.6 %collective-permute-start.4 = (f32[4,136,128]{2,1,0:T(8,128)S(1)}, f32[4,136,128]{2,1,0:T(8,128)S(1)}, u32[]{:S(2)}, u32[]{:S(2)}) collective-permute-start(f32[4,136,128]{2,1,0:T(8,128)S(1)} %get-tuple-element.43), channel_id=1, source_target_pairs={{0,8},{2,10},{4,12},{6,14},{8,0},{10,2},{12,4},{14,6},{16,24},{18,... | collective-permute-start | bytes 835592 | tf_op jit(solution)/shard_map/ppermute | solution.py:350
  19.2 3.9 %collective-permute-done.5.refs_3_ = f32[4,136,128]{2,1,0:T(8,128)S(1)} collective-permute-done((f32[4,136,128]{2,1,0:T(8,128)S(1)}, f32[4,136,128]{2,1,0:T(8,128)S(1)}, u32[]{:S(2)}, u32[]{:S(2)}) %collective-permute-start.5) | collective-permute-done | bytes 278560 | tf_op jit(solution)/shard_map/ppermute | solution.py:350
  23.1 0.6 %pick_boundary.1 = f32[4,136,128]{2,1,0:T(8,128)S(1)} custom-call(s32[5]{0:T(128)S(1)} %stack.31.info, f32[4,136,128]{2,1,0:T(8,128)S(1)} %get-tuple-element.47.refs_0_, f32[4,136,128]{2,1,0:T(8,128)S(1)} %collective-permute-done.1.refs_1_, f32[4,136,128]{2,1,0:T(8,128)S(1)} %collective-permute-done.3.refs_2_, f32[4,136,128]{2,1,0:T(8,128)S(1)} %collective-permute-done.5.refs_3_), custom_call_target="tpu_custom_call" | custom-call | flops 1000 | bytes 1000 | tf_op jit(solution)/shard_map/pick_boundary/pallas_call | solution.py:356
  23.7 3.1 %collective-permute-start.7 = (f32[4,136,128]{2,1,0:T(8,128)S(1)}, f32[4,136,128]{2,1,0:T(8,128)S(1)}, u32[]{:S(2)}, u32[]{:S(2)}) collective-permute-start(f32[4,136,128]{2,1,0:T(8,128)S(1)} %pick_boundary.1), channel_id=1, source_target_pairs={{0,16},{2,18},{4,20},{6,22},{8,24},{10,26},{12,28},{14,30},{16,0},... | collective-permute-start | bytes 835592 | tf_op jit(solution)/shard_map/ppermute | solution.py:350
  26.8 2.5 %collective-permute-start.6 = (f32[4,136,128]{2,1,0:T(8,128)S(1)}, f32[4,136,128]{2,1,0:T(8,128)S(1)}, u32[]{:S(2)}, u32[]{:S(2)}) collective-permute-start(f32[4,136,128]{2,1,0:T(8,128)S(1)} %get-tuple-element.46), channel_id=1, source_target_pairs={{0,12},{2,14},{4,8},{6,10},{8,4},{10,6},{12,0},{14,2},{16,28},{18,... | collective-permute-start | bytes 835592 | tf_op jit(solution)/shard_map/ppermute | solution.py:350
  29.8 1.6 %collective-permute-start.8 = (f32[2,16,8,128]{3,2,1,0:T(8,128)S(1)}, f32[2,16,8,128]{3,2,1,0:T(8,128)S(1)}, u32[]{:S(2)}, u32[]{:S(2)}) collective-permute-start(f32[2,16,8,128]{3,2,1,0:T(8,128)S(1)} %edge_columns.2.mine), channel_id=1, source_target_pairs={{0,1},{1,0},{2,3},{3,2},{4,5},{5,4},{6,7},{7,6},{8,9},{9,8},{10,11... | collective-permute-start | bytes 393224 | tf_op jit(solution)/shard_map/ppermute | solution.py:324
  31.3 3.7 %render_first.1.image = f32[4,128,128]{2,1,0:T(8,128)S(1)} custom-call(s32[5]{0:T(128)S(1)} %stack.31.info, bf16[384,256]{1,0:T(8,128)(2,1)S(1)} %copy-done.1, f32[4,136,128]{2,1,0:T(8,128)S(1)} %get-tuple-element.47.refs_0_, f32[4,136,128]{2,1,0:T(8,128)S(1)} %collective-permute-done.1.refs_1_, f32[4,136,128]{2,1,0:T(8,128)S(1)} %collective-permute-done.3.refs_2_, ...), custom_call_target="tpu_custom_call" | custom-call | flops 1000 | bytes 1000 | tf_op jit(solution)/shard_map/render_first/pallas_call | solution.py:300
  35.1 1.4 %first_edges.1 = f32[4,128,128]{2,1,0:T(8,128)S(1)} custom-call(s32[5]{0:T(128)S(1)} %stack.31.info, f32[2,16,8,128]{3,2,1,0:T(8,128)S(1)} %edge_columns.2.mine, f32[2,16,8,128]{3,2,1,0:T(8,128)S(1)} %collective-permute-done.8.before.after, f32[2,16,8,128]{3,2,1,0:T(8,128)S(1)} %collective-permute-done.8.before.after, f32[4,128,128]{2,1,0:T(8,128)S(1)} %render_first.1.image), custom_call_target="tpu_custom_call" | custom-call | flops 1000 | bytes 1000 | tf_op jit(solution)/shard_map/first_edges/pallas_call | solution.py:300
  36.9 1.3 %collective-permute-done.7.refs_4_ = f32[4,136,128]{2,1,0:T(8,128)S(1)} collective-permute-done((f32[4,136,128]{2,1,0:T(8,128)S(1)}, f32[4,136,128]{2,1,0:T(8,128)S(1)}, u32[]{:S(2)}, u32[]{:S(2)}) %collective-permute-start.7) | collective-permute-done | bytes 278560 | tf_op jit(solution)/shard_map/ppermute | solution.py:350
  38.1 6.0 %collective-permute-done.6.refs_3_ = f32[4,136,128]{2,1,0:T(8,128)S(1)} collective-permute-done((f32[4,136,128]{2,1,0:T(8,128)S(1)}, f32[4,136,128]{2,1,0:T(8,128)S(1)}, u32[]{:S(2)}, u32[]{:S(2)}) %collective-permute-start.6) | collective-permute-done | bytes 278560 | tf_op jit(solution)/shard_map/ppermute | solution.py:350
  44.1 0.5 edge_columns.3.mine
  44.7 1.7 %collective-permute-start.9 = (f32[2,32,8,128]{3,2,1,0:T(8,128)S(1)}, f32[2,32,8,128]{3,2,1,0:T(8,128)S(1)}, u32[]{:S(2)}, u32[]{:S(2)}) collective-permute-start(f32[2,32,8,128]{3,2,1,0:T(8,128)S(1)} %edge_columns.3.mine), channel_id=1, source_target_pairs={{0,1},{1,0},{2,3},{3,2},{4,5},{5,4},{6,7},{7,6},{8,9},{9,8},{10,11... | collective-permute-start | bytes 786440 | tf_op jit(solution)/shard_map/ppermute | solution.py:324
  46.4 4.5 %render_last.1.own_part = f32[4,128,128]{2,1,0:T(8,128)S(1)} custom-call(s32[5]{0:T(128)S(1)} %stack.31.info, bf16[384,256]{1,0:T(8,128)(2,1)S(1)} %copy-done.1, f32[4,136,128]{2,1,0:T(8,128)S(1)} %get-tuple-element.48.refs_0_, f32[4,136,128]{2,1,0:T(8,128)S(1)} %collective-permute-done.2.refs_1_, f32[4,136,128]{2,1,0:T(8,128)S(1)} %collective-permute-done.4.refs_2_, ...), custom_call_target="tpu_custom_call" | custom-call | flops 1000 | bytes 1000 | tf_op jit(solution)/shard_map/render_last/pallas_call | solution.py:300
  50.9 1.0 %collective-permute-done.9.before.after = f32[2,32,8,128]{3,2,1,0:T(8,128)S(1)} collective-permute-done((f32[2,32,8,128]{3,2,1,0:T(8,128)S(1)}, f32[2,32,8,128]{3,2,1,0:T(8,128)S(1)}, u32[]{:S(2)}, u32[]{:S(2)}) %collective-permute-start.9) | collective-permute-done | bytes 262176 | tf_op jit(solution)/shard_map/ppermute | solution.py:324
  51.9 2.2 %join_halves.1 = f32[4,128,128]{2,1,0:T(8,128)} custom-call(s32[5]{0:T(128)S(1)} %stack.31.info, f32[2,32,8,128]{3,2,1,0:T(8,128)S(1)} %edge_columns.3.mine, f32[2,32,8,128]{3,2,1,0:T(8,128)S(1)} %collective-permute-done.9.before.after, f32[2,32,8,128]{3,2,1,0:T(8,128)S(1)} %collective-permute-done.9.before.after, f32[4,128,128]{2,1,0:T(8,128)S(1)} %render_last.1.own_part, ...), custom_call_target="tpu_custom_call" | custom-call | flops 1000 | bytes 1000 | tf_op jit(solution)/shard_map/join_halves/pallas_call | solution.py:300
  (12 shorter events, 1.4 us)
Async XLA Ops:
  0.0 4.5 %collective-permute-start = (f32[2,2048,128]{2,1,0:T(8,128)}, f32[2,2048,128]{2,1,0:T(8,128)S(1)}, u32[]{:S(2)}, u32[]{:S(2)}) collective-permute-start(f32[2,2048,128]{2,1,0:T(8,128)} %source.1), channel_id=1, source_target_pairs={{0,2},{2,0},{4,6},{6,4},{8,10},{10,8},{12,14},{14,12},{16,18},{18,... | collective-permute-start | bytes 6291464 | tf_op jit(solution)/shard_map/ppermute | solution.py:286
  0.5 1.6 %copy-start = (f32[2,2048,128]{2,1,0:T(8,128)S(1)}, f32[2,2048,128]{2,1,0:T(8,128)}, u32[]{:S(2)}) copy-start(f32[2,2048,128]{2,1,0:T(8,128)} %source.1) | copy-start | bytes 6291460
  5.1 26.2 %copy-start.1 = (bf16[384,256]{1,0:T(8,128)(2,1)S(1)}, bf16[384,256]{1,0:T(8,128)(2,1)}, u32[]{:S(2)}) copy-start(bf16[384,256]{1,0:T(8,128)(2,1)} %constant.55.clone.weights) | copy-start | bytes 589828
  5.1 9.9 %collective-permute-start.1 = (f32[4,136,128]{2,1,0:T(8,128)S(1)}, f32[4,136,128]{2,1,0:T(8,128)S(1)}, u32[]{:S(2)}, u32[]{:S(2)}) collective-permute-start(f32[4,136,128]{2,1,0:T(8,128)S(1)} %get-tuple-element.39), channel_id=1, source_target_pairs={{0,4},{2,6},{4,0},{6,2},{8,12},{10,14},{12,8},{14,10},{16,20},{18,... | collective-permute-start | bytes 835592 | tf_op jit(solution)/shard_map/ppermute | solution.py:350
  8.1 9.5 %collective-permute-start.3 = (f32[4,136,128]{2,1,0:T(8,128)S(1)}, f32[4,136,128]{2,1,0:T(8,128)S(1)}, u32[]{:S(2)}, u32[]{:S(2)}) collective-permute-start(f32[4,136,128]{2,1,0:T(8,128)S(1)} %get-tuple-element.42), channel_id=1, source_target_pairs={{0,8},{2,10},{4,12},{6,14},{8,0},{10,2},{12,4},{14,6},{16,24},{18,... | collective-permute-start | bytes 835592 | tf_op jit(solution)/shard_map/ppermute | solution.py:350
  9.6 13.4 %collective-permute-start.5 = (f32[4,136,128]{2,1,0:T(8,128)S(1)}, f32[4,136,128]{2,1,0:T(8,128)S(1)}, u32[]{:S(2)}, u32[]{:S(2)}) collective-permute-start(f32[4,136,128]{2,1,0:T(8,128)S(1)} %get-tuple-element.45), channel_id=1, source_target_pairs={{0,12},{2,14},{4,8},{6,10},{8,4},{10,6},{12,0},{14,2},{16,28},{18,... | collective-permute-start | bytes 835592 | tf_op jit(solution)/shard_map/ppermute | solution.py:350
  15.0 21.9 %collective-permute-start.2 = (f32[4,136,128]{2,1,0:T(8,128)S(1)}, f32[4,136,128]{2,1,0:T(8,128)S(1)}, u32[]{:S(2)}, u32[]{:S(2)}) collective-permute-start(f32[4,136,128]{2,1,0:T(8,128)S(1)} %get-tuple-element.40), channel_id=1, source_target_pairs={{0,4},{2,6},{4,0},{6,2},{8,12},{10,14},{12,8},{14,10},{16,20},{18,... | collective-permute-start | bytes 835592 | tf_op jit(solution)/shard_map/ppermute | solution.py:350
  17.6 19.3 %collective-permute-start.4 = (f32[4,136,128]{2,1,0:T(8,128)S(1)}, f32[4,136,128]{2,1,0:T(8,128)S(1)}, u32[]{:S(2)}, u32[]{:S(2)}) collective-permute-start(f32[4,136,128]{2,1,0:T(8,128)S(1)} %get-tuple-element.43), channel_id=1, source_target_pairs={{0,8},{2,10},{4,12},{6,14},{8,0},{10,2},{12,4},{14,6},{16,24},{18,... | collective-permute-start | bytes 835592 | tf_op jit(solution)/shard_map/ppermute | solution.py:350
  23.7 14.5 %collective-permute-start.7 = (f32[4,136,128]{2,1,0:T(8,128)S(1)}, f32[4,136,128]{2,1,0:T(8,128)S(1)}, u32[]{:S(2)}, u32[]{:S(2)}) collective-permute-start(f32[4,136,128]{2,1,0:T(8,128)S(1)} %pick_boundary.1), channel_id=1, source_target_pairs={{0,16},{2,18},{4,20},{6,22},{8,24},{10,26},{12,28},{14,30},{16,0},... | collective-permute-start | bytes 835592 | tf_op jit(solution)/shard_map/ppermute | solution.py:350
  26.8 17.4 %collective-permute-start.6 = (f32[4,136,128]{2,1,0:T(8,128)S(1)}, f32[4,136,128]{2,1,0:T(8,128)S(1)}, u32[]{:S(2)}, u32[]{:S(2)}) collective-permute-start(f32[4,136,128]{2,1,0:T(8,128)S(1)} %get-tuple-element.46), channel_id=1, source_target_pairs={{0,12},{2,14},{4,8},{6,10},{8,4},{10,6},{12,0},{14,2},{16,28},{18,... | collective-permute-start | bytes 835592 | tf_op jit(solution)/shard_map/ppermute | solution.py:350
  29.8 5.3 %collective-permute-start.8 = (f32[2,16,8,128]{3,2,1,0:T(8,128)S(1)}, f32[2,16,8,128]{3,2,1,0:T(8,128)S(1)}, u32[]{:S(2)}, u32[]{:S(2)}) collective-permute-start(f32[2,16,8,128]{3,2,1,0:T(8,128)S(1)} %edge_columns.2.mine), channel_id=1, source_target_pairs={{0,1},{1,0},{2,3},{3,2},{4,5},{5,4},{6,7},{7,6},{8,9},{9,8},{10,11... | collective-permute-start | bytes 393224 | tf_op jit(solution)/shard_map/ppermute | solution.py:324
  36.5 14.4 %collective-permute-start.10 = (f32[4,128,128]{2,1,0:T(8,128)S(1)}, f32[4,128,128]{2,1,0:T(8,128)S(1)}, u32[]{:S(2)}, u32[]{:S(2)}) collective-permute-start(f32[4,128,128]{2,1,0:T(8,128)S(1)} %first_edges.1), channel_id=1, source_target_pairs={{0,16},{2,18},{4,20},{6,22},{8,24},{10,26},{12,28},{14,30},{16,0},... | collective-permute-start | bytes 786440 | tf_op jit(solution)/shard_map/ppermute | solution.py:350
  44.7 7.2 %collective-permute-start.9 = (f32[2,32,8,128]{3,2,1,0:T(8,128)S(1)}, f32[2,32,8,128]{3,2,1,0:T(8,128)S(1)}, u32[]{:S(2)}, u32[]{:S(2)}) collective-permute-start(f32[2,32,8,128]{3,2,1,0:T(8,128)S(1)} %edge_columns.3.mine), channel_id=1, source_target_pairs={{0,1},{1,0},{2,3},{3,2},{4,5},{5,4},{6,7},{7,6},{8,9},{9,8},{10,11... | collective-permute-start | bytes 786440 | tf_op jit(solution)/shard_map/ppermute | solution.py:324

commit v7 on v6

--- a/solution.py
+++ b/solution.py
@@ -15,7 +15,6 @@
 ONE = 49.0 / 256.0
 HALF_LEN = math.sqrt(0.48 * 0.48 + 0.6 * 0.6 + 1.64 * 1.64)
 SPEC = 0.35 / HALF_LEN**8
-LOG2E = 1.0 / math.log(2.0)
 LANES = 128
 TILE = 16
 
@@ -38,14 +37,12 @@
     return hi, mid, lo
 
 
-def filter_columns(block, plane, own, weights, sx, dx, slot):
-    width = block.shape[-1]
-    row = jnp.concatenate(three_parts(block[plane]), 1)
+def filter_columns(planes, index, weights, sx, dx):
+    width = planes.shape[2]
+    row = jnp.concatenate(three_parts(planes[index]), 1)
     both = jnp.dot(row, weights[...], preferred_element_type=jnp.float32)
-    for out, part in ((sx, both[:, :width]), (dx, both[:, width:])):
-        out[slot, 8 : 8 + own] = part[0:own]
-        out[slot, 6:8] = part[own : own + 2]
-        out[slot, 8 + own : 10 + own] = part[own + 2 : own + 4]
+    sx[index] = both[:, :width]
+    dx[index] = both[:, width:]
 
 
 def gauss_rows(a, b, c, d, e):
@@ -54,7 +51,7 @@
 
 def shade(t, gx, gy, gz, state):
     v_sum, vt_sum, vu_sum, cover = state
-    opacity = 0.6 * pl.reciprocal(1.0 + jnp.exp2(jnp.minimum(13.2 * LOG2E - (6.0 * LOG2E) * t, 126.0)))
+    opacity = pl.reciprocal(1.0 / 0.6 + jnp.exp(jnp.minimum((13.2 - math.log(0.6)) - 6.0 * t, 80.0)))
     tanh_t = jnp.tanh(t)
     tanh_u = jnp.tanh(t + 0.25)
     light = 0.48 * gx + 0.6 * gy + 0.64 * gz
@@ -106,29 +103,57 @@
     return slots + [(planes + 2) * front + plane for plane in range(extra)], (1 - front) * (planes + extra)
 
 
-def render_kernel(size, last, info, weights, *refs):
-    blocks, (image, sx, dx) = refs[:-3], refs[-3:]
-    depth, own = blocks[0].shape[0], image.shape[1]
+def render_kernel(size, depth, last, info, weights, *refs):
+    blocks, (image, planes, cubed, sx, dx) = refs[:-5], refs[-5:]
+    own, width = image.shape[1:]
     slots, empty = plane_slots(size, depth, last, info)
-    for out in (sx, dx):
-        out[pl.ds(empty, 2)] = jnp.zeros((2,) + out.shape[1:], jnp.float32)
-    for index, slot in enumerate(slots):
-        filter_columns(blocks[index // depth], index % depth, own, weights, sx, dx, slot)
+    planes[pl.ds(empty, 2)] = jnp.zeros((2,) + planes.shape[1:], jnp.float32)
+    places = [(block, plane) for block in blocks for plane in range(block.shape[0])]
+    for (block, plane), slot in zip(places, slots):
+        planes[slot, 8 : 8 + own] = block[plane, 0:own]
+        planes[slot, 6:8] = block[plane, own : own + 2]
+        planes[slot, 8 + own : 10 + own] = block[plane, own + 2 : own + 4]
+
+    def cube(first, rows):
+        chain = [None] * 3
+        for index in range(planes.shape[0]):
+            a, b, c, d = (planes[index, pl.ds(first + 6 + k, rows), :] for k in range(4))
+            x = (a + d) + 3.0 * (b + c)
+            for level in range(3):
+                before, chain[level] = chain[level], x
+                if before is None:
+                    x = None
+                    break
+                x = x + before
+            if x is not None:
+                cubed[index - 3, pl.ds(first, rows), :] = x
+
+    @pl.loop(0, own // TILE)
+    def _(tile):
+        cube(pl.multiple_of(tile * TILE, TILE), TILE)
+
+    cube(own, 8)
+    for index in range(cubed.shape[0]):
+        filter_columns(cubed, index, weights, sx, dx)
 
     @pl.loop(0, own // TILE)
     def _(tile):
         first = pl.multiple_of(tile * TILE, TILE)
-
-        def rows_of(ref):
-            return lambda index: [ref[index, pl.ds(first + 6 + k, TILE), :] for k in range(5)]
-
-        total = render(rows_of(sx), rows_of(dx), (TILE, sx.shape[2]), len(slots) - 2)
+        zero = jnp.zeros((TILE, width), jnp.float32)
+        state = (zero, zero, zero, zero)
+        for index in range(cubed.shape[0]):
+            a, b, c, d = (ref[index, pl.ds(first + k, TILE), :] for ref in (sx, dx) for k in range(2))
+            now = (a + b, b - a, c + d)
+            if index:
+                t, gy, gx = (x + y for x, y in zip(before, now))
+                state = shade(t, gx, gy, now[0] - before[0], state)
+            before = now
         for channel in range(4):
-            image[channel, pl.ds(first, TILE), :] = total[channel]
+            image[channel, pl.ds(first, TILE), :] = state[channel]
 
 
 def edge_kernel(*refs):
-    blocks, out = refs[:-1], refs[-1]
+    blocks, (out, sent) = refs[:-2], refs[-2:]
     own, width = blocks[0].shape[1] - 8, blocks[0].shape[2]
     places = [(block, plane) for block in blocks for plane in range(block.shape[0])]
     group = LANES // 8
@@ -142,6 +167,30 @@
             if missing:
                 rows = jnp.concatenate([rows, jnp.zeros((missing, width), jnp.float32)], 0)
             out[part, base : base + group] = jnp.transpose(rows).reshape(group, 8, LANES)
+    line = lax.broadcasted_iota(jnp.int32, (8, LANES), 0)
+    pairs = -(-len(places) // 2)
+    for pair in range(pairs):
+        sent[pair] = jnp.where(line < 4, pltpu.roll(out[0, 2 * pair], 6, 0), pltpu.roll(out[0, 2 * pair + 1], 2, 0))
+    lane = lax.broadcasted_iota(jnp.int32, (8, LANES), 1) // 4
+    for base in range(0, len(places), LANES // 4):
+        packed = jnp.zeros((8, LANES), jnp.float32)
+        for at in range(min(LANES // 4, len(places) - base)):
+            packed = jnp.where(lane == at, pltpu.roll(out[1, base + at], 4 * at, 1), packed)
+        sent[pairs + base // (LANES // 4)] = packed
+
+
+def sent_tiles(count):
+    return -(-count // 2) + -(-count // (LANES // 4))
+
+
+def received_edges(sent, count):
+    pairs = -(-count // 2)
+    own = jnp.stack([pltpu.roll(sent[0:pairs], 2, 1), pltpu.roll(sent[0:pairs], 6, 1)], 1)
+    own = own.reshape(2 * pairs, 8, LANES)[0:count]
+    group = LANES // 4
+    turns = [(LANES - 4 * (index % group)) % LANES for index in range(count)]
+    around = [pltpu.roll(sent[pairs + index // group], turn, 1) for index, turn in enumerate(turns)]
+    return own, jnp.stack(around, 0)
 
 
 def render_edges(size, depth, last, own, info, mine, before, after, sx, dx):
@@ -150,15 +199,18 @@
     lane = lax.broadcasted_iota(jnp.int32, (count, 8, LANES), 2)
     line = lax.broadcasted_iota(jnp.int32, (count, 8, 2 * LANES), 1)
 
-    def all_rows(ref):
-        main, around = ref[0, 0:count], ref[1, 0:count]
+    def all_rows(main, around):
         if own < LANES:
             main = jnp.where(lane < own, main, pltpu.roll(around, own - 2, 2))
         return jnp.concatenate([main, pltpu.roll(around, LANES - 2, 2)], 2)
 
-    mid = all_rows(mine)
-    left = jnp.where(info[3] == 1, all_rows(before), 0.0)
-    right = jnp.where(info[4] == 1, all_rows(after), 0.0)
+    mid = all_rows(mine[0, 0:count], mine[1, 0:count])
+    if before is after:
+        left = right = all_rows(*received_edges(before, count))
+    else:
+        left, right = all_rows(*received_edges(before, count)), all_rows(*received_edges(after, count))
+    left = jnp.where(info[3] == 1, left, 0.0)
+    right = jnp.where(info[4] == 1, right, 0.0)
     end = jnp.where(line < 4, mid, right)
     top = jnp.where(line < 4, left, mid)
     taps = [jnp.where(line < 2, end, top)]
@@ -193,16 +245,18 @@
     ]
 
 
-def fix_kernel(size, depth, info, mine, before, after, image, out, sx, dx):
+def fix_kernel(size, depth, info, image, mine, *refs):
+    before, after, (out, sx, dx) = refs[0], refs[-4], refs[-3:]
     state = render_edges(size, depth, False, image.shape[1], info, mine, before, after, sx, dx)
     for channel, values in enumerate(with_edges(state, image)):
         out[channel] = values
 
 
-def join_kernel(size, depth, info, mine, before, after, own_part, other, picture, sx, dx):
-    state = render_edges(size, depth, True, picture.shape[1], info, mine, before, after, sx, dx)
+def join_kernel(size, depth, info, image, other, mine, *refs):
+    before, after, (picture, sx, dx) = refs[0], refs[-4], refs[-3:]
+    state = render_edges(size, depth, True, image.shape[1], info, mine, before, after, sx, dx)
+    mine = with_edges(state, image)
     is_front = info[2] == 1
-    mine = with_edges(state, own_part)
     other = tuple(other[channel] for channel in range(4))
     ahead = tuple(jnp.where(is_front, m, o) for m, o in zip(mine, other))
     behind = tuple(jnp.where(is_front, o, m) for m, o in zip(mine, other))
@@ -311,30 +365,34 @@
     def columns_near(parts):
         count = sum(part.shape[0] for part in parts)
         group = LANES // 8
-        edges = pl.pallas_call(
+        edges, sent = pl.pallas_call(
             edge_kernel,
-            out_shape=jax.ShapeDtypeStruct((2, -(-count // group) * group, 8, LANES), f32),
+            out_shape=(
+                jax.ShapeDtypeStruct((2, -(-count // group) * group, 8, LANES), f32),
+                jax.ShapeDtypeStruct((sent_tiles(count), 8, LANES), f32),
+            ),
             in_specs=[VMEM] * len(parts),
-            out_specs=VMEM,
+            out_specs=(VMEM, VMEM),
             compiler_params=PARAMS,
             cost_estimate=cost(1000, 1000),
             name="edge_columns",
         )(*parts)
         if columns == 2:
-            return (edges,) + (lax.ppermute(edges, "cols", [(0, 1), (1, 0)]),) * 2
+            return edges, lax.ppermute(sent, "cols", [(0, 1), (1, 0)])
         return (edges,) + tuple(
-            lax.ppermute(edges, "cols", [(i, i + shift) for i in range(columns) if 0 <= i + shift < columns])
+            lax.ppermute(sent, "cols", [(i, i + shift) for i in range(columns) if 0 <= i + shift < columns])
             for shift in (1, -1)
         )
 
-    def plane_scratch(last, rows, lanes):
-        return [pltpu.VMEM((depth * size + (6 if last else 2), rows, lanes), f32)] * 2
-
     def render_call(last, parts):
-        kernel = functools.partial(render_kernel, size, last)
-        scratch = plane_scratch(last, own + 16, width)
+        count = depth * size + (6 if last else 2)
+        scratch = [pltpu.VMEM((count, own + 24, width), f32)] + [pltpu.VMEM((count - 3, own + 8, width), f32)] * 3
+        kernel = functools.partial(render_kernel, size, 2 * depth, last)
         name = "render_last" if last else "render_first"
         return call(kernel, name, image, info, weights, *parts, scratch_shapes=scratch)
+
+    def edge_scratch(last):
+        return [pltpu.VMEM((depth * size + (6 if last else 2), 8, 2 * LANES), f32)] * 2
 
     pick = pl.pallas_call(
         functools.partial(pick_kernel, size),
@@ -356,10 +414,8 @@
     boundary = swap(pick(info, *theirs), size)
     first_image = render_call(False, theirs)
     kernel = functools.partial(fix_kernel, size, 2 * depth)
-    scratch = plane_scratch(False, 8, 2 * LANES)
-    first_image = call(
-        kernel, "first_edges", image, info, *columns_near(theirs), first_image, scratch_shapes=scratch
-    )
+    near = columns_near(theirs)
+    first_image = call(kernel, "first_edges", image, info, first_image, *near, scratch_shapes=edge_scratch(False))
     image_part = swap(first_image, size)
     mine = [blocks[steps]]
     for step in range(1, steps):
@@ -368,10 +424,8 @@
     parts, _ = lax.optimization_barrier((mine + [boundary], first_image))
     own_part = render_call(True, parts)
     kernel = functools.partial(join_kernel, size, 2 * depth)
-    scratch = plane_scratch(True, 8, 2 * LANES)
-    return call(
-        kernel, "join_halves", image, info, *columns_near(parts), own_part, image_part, scratch_shapes=scratch
-    )
+    near = columns_near(parts)
+    return call(kernel, "join_halves", image, info, own_part, image_part, *near, scratch_shapes=edge_scratch(True))
 
 
 def solution(mesh):

time: 54.2 us -> 52.8 us (0.974)
  Pallas kernels: 14.6 us -> 13.7 us
  waiting for transfers between devices: 20.1 us -> 19.5 us
    pallas_call x4, Pallas kernels: 11.8 us -> 10.9 us  [call(): pl.pallas_call(kernel, out_shape=out_shape, in_specs=[SMEM] + [VMEM] * (l...]
    ppermute x2, waiting for transfers between devices: 0.97 us -> 0.01 us  [columns_near(): return (edges, lax.ppermute(sent, 'cols', [(0, 1), (1, 0)]))]
  transfers between devices with their start and end apart: 11 -> 11, of which waited for: 7 -> 6; matrix products, arithmetic and copies ran while one was open for 0% -> 0% of each run, Pallas kernels for 22% -> 21%
where the time goes in v7:
time: 52.8 us; the launch traced here: 52.6 us
  waiting for transfers between devices  19.5 us (37%)
  starting transfers between devices  17.6 us (33%)
  Pallas kernels  13.7 us (26%)
  local copies, waits for them, and re-layouts  1.68 us (3%)
    ppermute x8, waiting for transfers between devices, swap(): return lax.ppermute(x, 'depth', [(i, i ^ bits) for i in range(groups)])  17.8 us
    ppermute x8, starting transfers between devices, swap(): return lax.ppermute(x, 'depth', [(i, i ^ bits) for i in range(groups)])  13.9 us
    pallas_call x4, Pallas kernels, call(): pl.pallas_call(kernel, out_shape=out_shape, in_specs=[SMEM] + [VMEM] * (l...  10.9 us
    ppermute x2, starting transfers between devices, columns_near(): return (edges, lax.ppermute(sent, 'cols', [(0, 1), (1, 0)]))  3.26 us
    ppermute x1, waiting for transfers between devices, local(): shared = lax.ppermute(field, 'depth', [(i, i ^ 1) for i in range(groups)])  1.69 us
    unnamed x4, local copies, waits for them, and re-layouts  1.6 us
    pallas_call x2, Pallas kernels, local(): pl.pallas_call(functools.partial(pack_kernel, size, source is shared), ou...  1.26 us
  transfers between devices with their start and end apart: 11, of which 6 were waited for; matrix products, arithmetic and copies ran while one was open for 0% of the time, Pallas kernels for 21%

profile of v7, /device:TPU:0, one launch (start us, length us, event | category | flops | bytes accessed | tf_op | source)
XLA Modules:
  0.0 52.6 jit_solution(6678393441030111863)
XLA Ops:
  0.5 1.6 %copy-done = f32[2,2048,128]{2,1,0:T(8,128)S(1)} copy-done((f32[2,2048,128]{2,1,0:T(8,128)S(1)}, f32[2,2048,128]{2,1,0:T(8,128)}, u32[]{:S(2)}) %copy-start) | copy-done | bytes 2097176
  2.1 0.6 %pack_own.1 = (f32[4,136,128]{2,1,0:T(8,128)S(1)}, f32[4,136,128]{2,1,0:T(8,128)S(1)}, f32[4,136,128]{2,1,0:T(8,128)S(1)}, f32[4,136,128]{2,1,0:T(8,128)S(1)}, f...) custom-call(s32[5]{0:T(128)S(1)} %stack.31.info, ...), custom_call_target="tpu_custom_call" | custom-call | tf_op jit(solution)/shard_map/pack_own/pallas_call | solution.py:343
  2.8 1.7 %collective-permute-done.source = f32[2,2048,128]{2,1,0:T(8,128)S(1)} collective-permute-done((f32[2,2048,128]{2,1,0:T(8,128)}, f32[2,2048,128]{2,1,0:T(8,128)S(1)}, u32[]{:S(2)}, u32[]{:S(2)}) %collective-permute-start) | collective-permute-done | bytes 2097184 | tf_op jit(solution)/shard_map/ppermute | solution.py:340
  4.5 0.6 %pack_shared.1 = (f32[4,136,128]{2,1,0:T(8,128)S(1)}, f32[4,136,128]{2,1,0:T(8,128)S(1)}, f32[4,136,128]{2,1,0:T(8,128)S(1)}, f32[4,136,128]{2,1,0:T(8,128)S(1)}...) custom-call(s32[5]{0:T(128)S(1)} %stack.31.info, ...), custom_call_target="tpu_custom_call", output_to_operand_aliasing={{0}: (2, {}), {1}: (3, {}), {2}: (4, {}), {3}: (5, {}), {4}... | custom-call | tf_op jit(solution)/shard_map/pack_shared/pallas_call | solution.py:343
  5.1 3.0 %collective-permute-start.1 = (f32[4,136,128]{2,1,0:T(8,128)S(1)}, f32[4,136,128]{2,1,0:T(8,128)S(1)}, u32[]{:S(2)}, u32[]{:S(2)}) collective-permute-start(f32[4,136,128]{2,1,0:T(8,128)S(1)} %get-tuple-element.43), channel_id=1, source_target_pairs={{0,4},{2,6},{4,0},{6,2},{8,12},{10,14},{12,8},{14,10},{16,20},{18,... | collective-permute-start | bytes 835592 | tf_op jit(solution)/shard_map/ppermute | solution.py:408
  8.1 1.6 %collective-permute-start.3 = (f32[4,136,128]{2,1,0:T(8,128)S(1)}, f32[4,136,128]{2,1,0:T(8,128)S(1)}, u32[]{:S(2)}, u32[]{:S(2)}) collective-permute-start(f32[4,136,128]{2,1,0:T(8,128)S(1)} %get-tuple-element.46), channel_id=1, source_target_pairs={{0,8},{2,10},{4,12},{6,14},{8,0},{10,2},{12,4},{14,6},{16,24},{18,... | collective-permute-start | bytes 835592 | tf_op jit(solution)/shard_map/ppermute | solution.py:408
  9.6 5.4 %collective-permute-done.1.refs_1_ = f32[4,136,128]{2,1,0:T(8,128)S(1)} collective-permute-done((f32[4,136,128]{2,1,0:T(8,128)S(1)}, f32[4,136,128]{2,1,0:T(8,128)S(1)}, u32[]{:S(2)}, u32[]{:S(2)}) %collective-permute-start.1) | collective-permute-done | bytes 278560 | tf_op jit(solution)/shard_map/ppermute | solution.py:408
  15.0 1.7 %collective-permute-start.2 = (f32[4,136,128]{2,1,0:T(8,128)S(1)}, f32[4,136,128]{2,1,0:T(8,128)S(1)}, u32[]{:S(2)}, u32[]{:S(2)}) collective-permute-start(f32[4,136,128]{2,1,0:T(8,128)S(1)} %get-tuple-element.44), channel_id=1, source_target_pairs={{0,4},{2,6},{4,0},{6,2},{8,12},{10,14},{12,8},{14,10},{16,20},{18,... | collective-permute-start | bytes 835592 | tf_op jit(solution)/shard_map/ppermute | solution.py:408
  16.8 0.8 %collective-permute-done.3.refs_2_ = f32[4,136,128]{2,1,0:T(8,128)S(1)} collective-permute-done((f32[4,136,128]{2,1,0:T(8,128)S(1)}, f32[4,136,128]{2,1,0:T(8,128)S(1)}, u32[]{:S(2)}, u32[]{:S(2)}) %collective-permute-start.3) | collective-permute-done | bytes 278560 | tf_op jit(solution)/shard_map/ppermute | solution.py:408
  17.6 1.6 %collective-permute-start.4 = (f32[4,136,128]{2,1,0:T(8,128)S(1)}, f32[4,136,128]{2,1,0:T(8,128)S(1)}, u32[]{:S(2)}, u32[]{:S(2)}) collective-permute-start(f32[4,136,128]{2,1,0:T(8,128)S(1)} %get-tuple-element.47), channel_id=1, source_target_pairs={{0,8},{2,10},{4,12},{6,14},{8,0},{10,2},{12,4},{14,6},{16,24},{18,... | collective-permute-start | bytes 835592 | tf_op jit(solution)/shard_map/ppermute | solution.py:408
  19.2 3.9 %collective-permute-done.5.refs_3_ = f32[4,136,128]{2,1,0:T(8,128)S(1)} collective-permute-done((f32[4,136,128]{2,1,0:T(8,128)S(1)}, f32[4,136,128]{2,1,0:T(8,128)S(1)}, u32[]{:S(2)}, u32[]{:S(2)}) %collective-permute-start.5) | collective-permute-done | bytes 278560 | tf_op jit(solution)/shard_map/ppermute | solution.py:408
  23.1 0.6 %pick_boundary.1 = f32[4,136,128]{2,1,0:T(8,128)S(1)} custom-call(s32[5]{0:T(128)S(1)} %stack.31.info, f32[4,136,128]{2,1,0:T(8,128)S(1)} %get-tuple-element.51.refs_0_, f32[4,136,128]{2,1,0:T(8,128)S(1)} %collective-permute-done.1.refs_1_, f32[4,136,128]{2,1,0:T(8,128)S(1)} %collective-permute-done.3.refs_2_, f32[4,136,128]{2,1,0:T(8,128)S(1)} %collective-permute-done.5.refs_3_), custom_call_target="tpu_custom_call" | custom-call | flops 1000 | bytes 1000 | tf_op jit(solution)/shard_map/pick_boundary/pallas_call | solution.py:414
  23.7 3.1 %collective-permute-start.7 = (f32[4,136,128]{2,1,0:T(8,128)S(1)}, f32[4,136,128]{2,1,0:T(8,128)S(1)}, u32[]{:S(2)}, u32[]{:S(2)}) collective-permute-start(f32[4,136,128]{2,1,0:T(8,128)S(1)} %pick_boundary.1), channel_id=1, source_target_pairs={{0,16},{2,18},{4,20},{6,22},{8,24},{10,26},{12,28},{14,30},{16,0},... | collective-permute-start | bytes 835592 | tf_op jit(solution)/shard_map/ppermute | solution.py:408
  26.8 2.5 %collective-permute-start.6 = (f32[4,136,128]{2,1,0:T(8,128)S(1)}, f32[4,136,128]{2,1,0:T(8,128)S(1)}, u32[]{:S(2)}, u32[]{:S(2)}) collective-permute-start(f32[4,136,128]{2,1,0:T(8,128)S(1)} %get-tuple-element.50), channel_id=1, source_target_pairs={{0,12},{2,14},{4,8},{6,10},{8,4},{10,6},{12,0},{14,2},{16,28},{18,... | collective-permute-start | bytes 835592 | tf_op jit(solution)/shard_map/ppermute | solution.py:408
  29.3 0.5 edge_columns.2
  29.8 1.6 %collective-permute-start.8 = (f32[9,8,128]{2,1,0:T(8,128)S(1)}, f32[9,8,128]{2,1,0:T(8,128)S(1)}, u32[]{:S(2)}, u32[]{:S(2)}) collective-permute-start(f32[9,8,128]{2,1,0:T(8,128)S(1)} %get-tuple-element.53), channel_id=1, source_target_pairs={{0,1},{1,0},{2,3},{3,2},{4,5},{5,4},{6,7},{7,6},{8,9},{9,8},{10,11... | collective-permute-start | bytes 110600 | tf_op jit(solution)/shard_map/ppermute | solution.py:381
  31.4 3.3 %render_first.1.image = f32[4,128,128]{2,1,0:T(8,128)S(1)} custom-call(s32[5]{0:T(128)S(1)} %stack.31.info, bf16[384,256]{1,0:T(8,128)(2,1)S(1)} %copy-done.1, f32[4,136,128]{2,1,0:T(8,128)S(1)} %get-tuple-element.51.refs_0_, f32[4,136,128]{2,1,0:T(8,128)S(1)} %collective-permute-done.1.refs_1_, f32[4,136,128]{2,1,0:T(8,128)S(1)} %collective-permute-done.3.refs_2_, ...), custom_call_target="tpu_custom_call" | custom-call | flops 1000 | bytes 1000 | tf_op jit(solution)/shard_map/render_first/pallas_call | solution.py:354
  34.6 1.4 %first_edges.1 = f32[4,128,128]{2,1,0:T(8,128)S(1)} custom-call(s32[5]{0:T(128)S(1)} %stack.31.info, f32[4,128,128]{2,1,0:T(8,128)S(1)} %render_first.1.image, f32[2,16,8,128]{3,2,1,0:T(8,128)S(1)} %get-tuple-element.52.mine, f32[9,8,128]{2,1,0:T(8,128)S(1)} %collective-permute-done.8.refs_0_), custom_call_target="tpu_custom_call" | custom-call | flops 1000 | bytes 1000 | tf_op jit(solution)/shard_map/first_edges/pallas_call | solution.py:354
  36.5 1.9 %collective-permute-done.7.refs_4_ = f32[4,136,128]{2,1,0:T(8,128)S(1)} collective-permute-done((f32[4,136,128]{2,1,0:T(8,128)S(1)}, f32[4,136,128]{2,1,0:T(8,128)S(1)}, u32[]{:S(2)}, u32[]{:S(2)}) %collective-permute-start.7) | collective-permute-done | bytes 278560 | tf_op jit(solution)/shard_map/ppermute | solution.py:408
  38.3 5.8 %collective-permute-done.6.refs_3_ = f32[4,136,128]{2,1,0:T(8,128)S(1)} collective-permute-done((f32[4,136,128]{2,1,0:T(8,128)S(1)}, f32[4,136,128]{2,1,0:T(8,128)S(1)}, u32[]{:S(2)}, u32[]{:S(2)}) %collective-permute-start.6) | collective-permute-done | bytes 278560 | tf_op jit(solution)/shard_map/ppermute | solution.py:408
  44.1 0.6 %edge_columns.3 = (f32[2,32,8,128]{3,2,1,0:T(8,128)S(1)}, f32[11,8,128]{2,1,0:T(8,128)S(1)}) custom-call(f32[4,136,128]{2,1,0:T(8,128)S(1)} %get-tuple-element.54.refs_0_, f32[4,136,128]{2,1,0:T(8,128)S(1)} %collective-permute-done.2.refs_1_, f32[4,136,128]{2,1,0:T(8,128)S(1)} %collective-permute-done.4.refs_2_, ...), custom_call_target="tpu_custom_call" | custom-call | flops 1000 | bytes 1000 | tf_op jit(solution)/shard_map/edge_columns/pallas_call | solution.py:368
  44.7 1.7 %collective-permute-start.10 = (f32[11,8,128]{2,1,0:T(8,128)S(1)}, f32[11,8,128]{2,1,0:T(8,128)S(1)}, u32[]{:S(2)}, u32[]{:S(2)}) collective-permute-start(f32[11,8,128]{2,1,0:T(8,128)S(1)} %get-tuple-element.60), channel_id=1, source_target_pairs={{0,1},{1,0},{2,3},{3,2},{4,5},{5,4},{6,7},{7,6},{8,9},{9,8},{10,11... | collective-permute-start | bytes 135176 | tf_op jit(solution)/shard_map/ppermute | solution.py:381
  46.4 3.9 %render_last.1.image = f32[4,128,128]{2,1,0:T(8,128)S(1)} custom-call(s32[5]{0:T(128)S(1)} %stack.31.info, bf16[384,256]{1,0:T(8,128)(2,1)S(1)} %copy-done.1, f32[4,136,128]{2,1,0:T(8,128)S(1)} %get-tuple-element.54.refs_0_, f32[4,136,128]{2,1,0:T(8,128)S(1)} %collective-permute-done.2.refs_1_, f32[4,136,128]{2,1,0:T(8,128)S(1)} %collective-permute-done.4.refs_2_, ...), custom_call_target="tpu_custom_call" | custom-call | flops 1000 | bytes 1000 | tf_op jit(solution)/shard_map/render_last/pallas_call | solution.py:354
  50.4 2.3 %join_halves.1 = f32[4,128,128]{2,1,0:T(8,128)} custom-call(s32[5]{0:T(128)S(1)} %stack.31.info, f32[4,128,128]{2,1,0:T(8,128)S(1)} %render_last.1.image, f32[4,128,128]{2,1,0:T(8,128)S(1)} %collective-permute-done.9.other, f32[2,32,8,128]{3,2,1,0:T(8,128)S(1)} %get-tuple-element.59.mine, f32[11,8,128]{2,1,0:T(8,128)S(1)} %collective-permute-done.10.refs_0_), custom_call_target="tpu_custom_call" | custom-call | flops 1000 | bytes 1000 | tf_op jit(solution)/shard_map/join_halves/pallas_call | solution.py:354
  (12 shorter events, 1.0 us)
Async XLA Ops:
  0.0 4.5 %collective-permute-start = (f32[2,2048,128]{2,1,0:T(8,128)}, f32[2,2048,128]{2,1,0:T(8,128)S(1)}, u32[]{:S(2)}, u32[]{:S(2)}) collective-permute-start(f32[2,2048,128]{2,1,0:T(8,128)} %source.1), channel_id=1, source_target_pairs={{0,2},{2,0},{4,6},{6,4},{8,10},{10,8},{12,14},{14,12},{16,18},{18,... | collective-permute-start | bytes 6291464 | tf_op jit(solution)/shard_map/ppermute | solution.py:340
  0.5 1.6 %copy-start = (f32[2,2048,128]{2,1,0:T(8,128)S(1)}, f32[2,2048,128]{2,1,0:T(8,128)}, u32[]{:S(2)}) copy-start(f32[2,2048,128]{2,1,0:T(8,128)} %source.1) | copy-start | bytes 6291460
  5.1 26.3 %copy-start.1 = (bf16[384,256]{1,0:T(8,128)(2,1)S(1)}, bf16[384,256]{1,0:T(8,128)(2,1)}, u32[]{:S(2)}) copy-start(bf16[384,256]{1,0:T(8,128)(2,1)} %constant.55.clone.weights) | copy-start | bytes 589828
  5.1 9.9 %collective-permute-start.1 = (f32[4,136,128]{2,1,0:T(8,128)S(1)}, f32[4,136,128]{2,1,0:T(8,128)S(1)}, u32[]{:S(2)}, u32[]{:S(2)}) collective-permute-start(f32[4,136,128]{2,1,0:T(8,128)S(1)} %get-tuple-element.43), channel_id=1, source_target_pairs={{0,4},{2,6},{4,0},{6,2},{8,12},{10,14},{12,8},{14,10},{16,20},{18,... | collective-permute-start | bytes 835592 | tf_op jit(solution)/shard_map/ppermute | solution.py:408
  8.1 9.5 %collective-permute-start.3 = (f32[4,136,128]{2,1,0:T(8,128)S(1)}, f32[4,136,128]{2,1,0:T(8,128)S(1)}, u32[]{:S(2)}, u32[]{:S(2)}) collective-permute-start(f32[4,136,128]{2,1,0:T(8,128)S(1)} %get-tuple-element.46), channel_id=1, source_target_pairs={{0,8},{2,10},{4,12},{6,14},{8,0},{10,2},{12,4},{14,6},{16,24},{18,... | collective-permute-start | bytes 835592 | tf_op jit(solution)/shard_map/ppermute | solution.py:408
  9.6 13.4 %collective-permute-start.5 = (f32[4,136,128]{2,1,0:T(8,128)S(1)}, f32[4,136,128]{2,1,0:T(8,128)S(1)}, u32[]{:S(2)}, u32[]{:S(2)}) collective-permute-start(f32[4,136,128]{2,1,0:T(8,128)S(1)} %get-tuple-element.49), channel_id=1, source_target_pairs={{0,12},{2,14},{4,8},{6,10},{8,4},{10,6},{12,0},{14,2},{16,28},{18,... | collective-permute-start | bytes 835592 | tf_op jit(solution)/shard_map/ppermute | solution.py:408
  15.0 21.4 %collective-permute-start.2 = (f32[4,136,128]{2,1,0:T(8,128)S(1)}, f32[4,136,128]{2,1,0:T(8,128)S(1)}, u32[]{:S(2)}, u32[]{:S(2)}) collective-permute-start(f32[4,136,128]{2,1,0:T(8,128)S(1)} %get-tuple-element.44), channel_id=1, source_target_pairs={{0,4},{2,6},{4,0},{6,2},{8,12},{10,14},{12,8},{14,10},{16,20},{18,... | collective-permute-start | bytes 835592 | tf_op jit(solution)/shard_map/ppermute | solution.py:408
  17.6 18.9 %collective-permute-start.4 = (f32[4,136,128]{2,1,0:T(8,128)S(1)}, f32[4,136,128]{2,1,0:T(8,128)S(1)}, u32[]{:S(2)}, u32[]{:S(2)}) collective-permute-start(f32[4,136,128]{2,1,0:T(8,128)S(1)} %get-tuple-element.47), channel_id=1, source_target_pairs={{0,8},{2,10},{4,12},{6,14},{8,0},{10,2},{12,4},{14,6},{16,24},{18,... | collective-permute-start | bytes 835592 | tf_op jit(solution)/shard_map/ppermute | solution.py:408
  23.7 14.7 %collective-permute-start.7 = (f32[4,136,128]{2,1,0:T(8,128)S(1)}, f32[4,136,128]{2,1,0:T(8,128)S(1)}, u32[]{:S(2)}, u32[]{:S(2)}) collective-permute-start(f32[4,136,128]{2,1,0:T(8,128)S(1)} %pick_boundary.1), channel_id=1, source_target_pairs={{0,16},{2,18},{4,20},{6,22},{8,24},{10,26},{12,28},{14,30},{16,0},... | collective-permute-start | bytes 835592 | tf_op jit(solution)/shard_map/ppermute | solution.py:408
  26.8 17.4 %collective-permute-start.6 = (f32[4,136,128]{2,1,0:T(8,128)S(1)}, f32[4,136,128]{2,1,0:T(8,128)S(1)}, u32[]{:S(2)}, u32[]{:S(2)}) collective-permute-start(f32[4,136,128]{2,1,0:T(8,128)S(1)} %get-tuple-element.50), channel_id=1, source_target_pairs={{0,12},{2,14},{4,8},{6,10},{8,4},{10,6},{12,0},{14,2},{16,28},{18,... | collective-permute-start | bytes 835592 | tf_op jit(solution)/shard_map/ppermute | solution.py:408
  29.8 4.8 %collective-permute-start.8 = (f32[9,8,128]{2,1,0:T(8,128)S(1)}, f32[9,8,128]{2,1,0:T(8,128)S(1)}, u32[]{:S(2)}, u32[]{:S(2)}) collective-permute-start(f32[9,8,128]{2,1,0:T(8,128)S(1)} %get-tuple-element.53), channel_id=1, source_target_pairs={{0,1},{1,0},{2,3},{3,2},{4,5},{5,4},{6,7},{7,6},{8,9},{9,8},{10,11... | collective-permute-start | bytes 110600 | tf_op jit(solution)/shard_map/ppermute | solution.py:381
  36.0 14.3 %collective-permute-start.9 = (f32[4,128,128]{2,1,0:T(8,128)S(1)}, f32[4,128,128]{2,1,0:T(8,128)S(1)}, u32[]{:S(2)}, u32[]{:S(2)}) collective-permute-start(f32[4,128,128]{2,1,0:T(8,128)S(1)} %first_edges.1), channel_id=1, source_target_pairs={{0,16},{2,18},{4,20},{6,22},{8,24},{10,26},{12,28},{14,30},{16,0},... | collective-permute-start | bytes 786440 | tf_op jit(solution)/shard_map/ppermute | solution.py:408
  44.7 5.7 %collective-permute-start.10 = (f32[11,8,128]{2,1,0:T(8,128)S(1)}, f32[11,8,128]{2,1,0:T(8,128)S(1)}, u32[]{:S(2)}, u32[]{:S(2)}) collective-permute-start(f32[11,8,128]{2,1,0:T(8,128)S(1)} %get-tuple-element.60), channel_id=1, source_target_pairs={{0,1},{1,0},{2,3},{3,2},{4,5},{5,4},{6,7},{7,6},{8,9},{9,8},{10,11... | collective-permute-start | bytes 135176 | tf_op jit(solution)/shard_map/ppermute | solution.py:381

commit v8 on v7

--- a/solution.py
+++ b/solution.py
@@ -108,11 +108,12 @@
     own, width = image.shape[1:]
     slots, empty = plane_slots(size, depth, last, info)
     planes[pl.ds(empty, 2)] = jnp.zeros((2,) + planes.shape[1:], jnp.float32)
-    places = [(block, plane) for block in blocks for plane in range(block.shape[0])]
+    places = [(block, plane) for block in blocks for plane in range(depth)]
     for (block, plane), slot in zip(places, slots):
-        planes[slot, 8 : 8 + own] = block[plane, 0:own]
-        planes[slot, 6:8] = block[plane, own : own + 2]
-        planes[slot, 8 + own : 10 + own] = block[plane, own + 2 : own + 4]
+        around = depth * own + 4 * plane
+        planes[slot, 8 : 8 + own] = block[plane * own : (plane + 1) * own]
+        planes[slot, 6:8] = block[around : around + 2]
+        planes[slot, 8 + own : 10 + own] = block[around + 2 : around + 4]
 
     def cube(first, rows):
         chain = [None] * 3
@@ -152,49 +153,79 @@
             image[channel, pl.ds(first, TILE), :] = state[channel]
 
 
-def edge_kernel(*refs):
+def edge_columns(blocks, depth, own, out):
+    width = blocks[0].shape[1]
+    places = [(block, plane) for block in blocks for plane in range(depth)]
+    group = LANES // 8
+    for base in range(0, len(places), group):
+        for part, count in enumerate((own, 4)):
+            lane = lax.broadcasted_iota(jnp.int32, (count, width), 1) // 8
+            packed = jnp.zeros((count, width), jnp.float32)
+            for at, (block, plane) in enumerate(places[base : base + group]):
+                first = part * depth * own + plane * count
+                turned = pltpu.roll(block[first : first + count], (8 * at + 4) % width, 1)
+                packed = jnp.where(lane == at, turned, packed)
+            if count < LANES:
+                packed = jnp.concatenate([packed, jnp.zeros((LANES - count, width), jnp.float32)], 0)
+            out[part, base : base + group] = jnp.transpose(packed).reshape(group, 8, LANES)
+
+
+def sent_tiles(count):
+    return -(-count // 2) + -(-count // (LANES // 4))
+
+
+def edge_kernel(depth, own, *refs):
     blocks, (out, sent) = refs[:-2], refs[-2:]
-    own, width = blocks[0].shape[1] - 8, blocks[0].shape[2]
-    places = [(block, plane) for block in blocks for plane in range(block.shape[0])]
-    group = LANES // 8
-    lane = lax.broadcasted_iota(jnp.int32, (own + 8, width), 1) // 8
-    for base in range(0, len(places), group):
-        packed = jnp.zeros((own + 8, width), jnp.float32)
-        for at, (block, plane) in enumerate(places[base : base + group]):
-            packed = jnp.where(lane == at, pltpu.roll(block[plane], (8 * at + 4) % width, 1), packed)
-        for part, rows in enumerate((packed[0:own], packed[own:])):
-            missing = LANES - rows.shape[0]
-            if missing:
-                rows = jnp.concatenate([rows, jnp.zeros((missing, width), jnp.float32)], 0)
-            out[part, base : base + group] = jnp.transpose(rows).reshape(group, 8, LANES)
+    edge_columns(blocks, depth, own, out)
+    count = depth * len(blocks)
     line = lax.broadcasted_iota(jnp.int32, (8, LANES), 0)
-    pairs = -(-len(places) // 2)
+    pairs = -(-count // 2)
     for pair in range(pairs):
         sent[pair] = jnp.where(line < 4, pltpu.roll(out[0, 2 * pair], 6, 0), pltpu.roll(out[0, 2 * pair + 1], 2, 0))
     lane = lax.broadcasted_iota(jnp.int32, (8, LANES), 1) // 4
-    for base in range(0, len(places), LANES // 4):
+    for base in range(0, count, LANES // 4):
         packed = jnp.zeros((8, LANES), jnp.float32)
-        for at in range(min(LANES // 4, len(places) - base)):
+        for at in range(min(LANES // 4, count - base)):
             packed = jnp.where(lane == at, pltpu.roll(out[1, base + at], 4 * at, 1), packed)
         sent[pairs + base // (LANES // 4)] = packed
 
 
-def sent_tiles(count):
-    return -(-count // 2) + -(-count // (LANES // 4))
-
-
-def received_edges(sent, count):
+def near_tiles(info, count, before, after, near):
     pairs = -(-count // 2)
-    own = jnp.stack([pltpu.roll(sent[0:pairs], 2, 1), pltpu.roll(sent[0:pairs], 6, 1)], 1)
-    own = own.reshape(2 * pairs, 8, LANES)[0:count]
-    group = LANES // 4
-    turns = [(LANES - 4 * (index % group)) % LANES for index in range(count)]
-    around = [pltpu.roll(sent[pairs + index // group], turn, 1) for index, turn in enumerate(turns)]
-    return own, jnp.stack(around, 0)
-
-
-def render_edges(size, depth, last, own, info, mine, before, after, sx, dx):
-    slots, empty = plane_slots(size, depth, last, info)
+    left = jnp.where(info[3] == 1, before[...], 0.0)
+    right = jnp.where(info[4] == 1, after[...], 0.0)
+    line = lax.broadcasted_iota(jnp.int32, left.shape, 1)
+    near[0:pairs] = jnp.where(line % 4 < 2, left, right)[0:pairs]
+    near[pairs:] = jnp.where(line < 4, left, right)[pairs:]
+
+
+def block_near(near, depth, blocks, block):
+    pairs, group = depth // 2, LANES // (4 * depth)
+    turn = LANES - block % group * (4 * depth)
+    around = pltpu.roll(near[blocks * pairs + block // group], turn % LANES, 1)
+    return [near[block * pairs + pair] for pair in range(pairs)] + [around]
+
+
+def near_kernel(depth, info, before, after, *refs):
+    blocks, near = refs[(len(refs) - 1) // 2 : -1], refs[-1]
+    near_tiles(info, depth * len(blocks), before, after, near)
+    for index, out in enumerate(blocks):
+        tiles = block_near(near, depth, len(blocks), index)
+        first = out.shape[0] - 8 * len(tiles)
+        for at, tile in enumerate(tiles):
+            out[first + 8 * at : first + 8 * at + 8] = tile
+
+
+def neighbour_columns(depth, tiles):
+    own, around = [], []
+    for block in tiles:
+        for plane in range(depth):
+            own.append(pltpu.roll(block[plane // 2], 6 if plane % 2 else 2, 0))
+            around.append(pltpu.roll(block[-1], (LANES - 4 * plane) % LANES, 1))
+    return jnp.stack(own, 0), jnp.stack(around, 0)
+
+
+def filter_edges(own, mine, tiles, depth, slots, sx, dx):
     count = len(slots)
     lane = lax.broadcasted_iota(jnp.int32, (count, 8, LANES), 2)
     line = lax.broadcasted_iota(jnp.int32, (count, 8, 2 * LANES), 1)
@@ -205,25 +236,26 @@
         return jnp.concatenate([main, pltpu.roll(around, LANES - 2, 2)], 2)
 
     mid = all_rows(mine[0, 0:count], mine[1, 0:count])
-    if before is after:
-        left = right = all_rows(*received_edges(before, count))
-    else:
-        left, right = all_rows(*received_edges(before, count)), all_rows(*received_edges(after, count))
-    left = jnp.where(info[3] == 1, left, 0.0)
-    right = jnp.where(info[4] == 1, right, 0.0)
-    end = jnp.where(line < 4, mid, right)
-    top = jnp.where(line < 4, left, mid)
+    beside = all_rows(*neighbour_columns(depth, tiles))
+    end = jnp.where(line < 4, mid, beside)
+    top = jnp.where(line < 4, beside, mid)
     taps = [jnp.where(line < 2, end, top)]
     for k in range(1, 5):
         taps.append(jnp.where(line < 2, pltpu.roll(end, 8 - k, 1), pltpu.roll(top, 8 - k, 1)))
     a, b, c, d, e = taps
     smooth = SCALE * gauss_rows(a, b, c, d, e)
     slope = SCALE * ((e - a) + 2.0 * (d - b))
-    for out, values in ((sx, smooth), (dx, slope)):
+    for index, slot in enumerate(slots):
+        sx[slot] = smooth[index]
+        dx[slot] = slope[index]
+
+
+def clear_planes(empty, *planes):
+    for out in planes:
         out[pl.ds(empty, 2)] = jnp.zeros((2,) + out.shape[1:], jnp.float32)
-        for index, slot in enumerate(slots):
-            out[slot] = values[index]
-
+
+
+def render_edges(sx, dx):
     def rows_of(ref):
         def five(index):
             rows = ref[index]
@@ -231,7 +263,7 @@
 
         return five
 
-    return render(rows_of(sx), rows_of(dx), (8, LANES), count - 2)
+    return render(rows_of(sx), rows_of(dx), (8, LANES), sx.shape[0] - 4)
 
 
 def with_edges(state, image):
@@ -245,19 +277,46 @@
     ]
 
 
-def fix_kernel(size, depth, info, image, mine, *refs):
-    before, after, (out, sx, dx) = refs[0], refs[-4], refs[-3:]
-    state = render_edges(size, depth, False, image.shape[1], info, mine, before, after, sx, dx)
+def fix_kernel(size, depth, info, image, mine, before, after, out, sx, dx, near):
+    steps, own = size // 2, image.shape[1]
+    near_tiles(info, depth * steps, before, after, near)
+    tiles = [block_near(near, depth, steps, step) for step in range(steps)]
+    slots, empty = plane_slots(size, depth, False, info)
+    clear_planes(empty, sx, dx)
+    filter_edges(own, mine, tiles, depth, slots, sx, dx)
+    state = render_edges(sx, dx)
     for channel, values in enumerate(with_edges(state, image)):
-        out[channel] = values
-
-
-def join_kernel(size, depth, info, image, other, mine, *refs):
-    before, after, (picture, sx, dx) = refs[0], refs[-4], refs[-3:]
-    state = render_edges(size, depth, True, image.shape[1], info, mine, before, after, sx, dx)
-    mine = with_edges(state, image)
+        out[channel * own : (channel + 1) * own] = values
+    wanted = info[0] ^ (info[2] * (steps - 1))
+    for step in range(steps):
+
+        @pl.when(wanted == step)
+        def _():
+            for at, tile in enumerate(tiles[step]):
+                out[4 * own + 8 * at : 4 * own + 8 * at + 8] = tile
+
+
+def block_tiles(source, depth):
+    first = source.shape[0] - 8 * (depth // 2 + 1)
+    return [source[first + 8 * at : first + 8 * at + 8] for at in range(depth // 2 + 1)]
+
+
+def own_edges_kernel(size, depth, own, info, *refs):
+    blocks, (sx, dx, mine) = refs[:-3], refs[-3:]
+    edge_columns(blocks, depth, own, mine)
+    slots, empty = plane_slots(size, depth, True, info)
+    clear_planes(empty, sx, dx)
+    tiles = [block_tiles(block, depth) for block in blocks]
+    filter_edges(own, mine, tiles, depth, slots[:-4], sx, dx)
+
+
+def join_kernel(size, depth, info, image, other, boundary, sx_own, dx_own, picture, sx, dx, mine):
+    own = image.shape[1]
+    edge_columns([boundary], depth, own, mine)
+    filter_edges(own, mine, [block_tiles(other, depth)], depth, plane_slots(size, depth, True, info)[0][-4:], sx, dx)
+    mine = with_edges(render_edges(sx, dx), image)
     is_front = info[2] == 1
-    other = tuple(other[channel] for channel in range(4))
+    other = tuple(other[channel * own : (channel + 1) * own] for channel in range(4))
     ahead = tuple(jnp.where(is_front, m, o) for m, o in zip(mine, other))
     behind = tuple(jnp.where(is_front, o, m) for m, o in zip(mine, other))
     v_sum, vt_sum, vu_sum, cover = over(ahead, behind)
@@ -286,30 +345,30 @@
             yield chunk * (size // 2) + step, base + 2 * (chip ^ step), core
 
 
-def pack_kernel(size, shared, info, source, *refs):
+def pack_kernel(size, own, shared, info, source, *refs):
     outs = refs[-size:]
-    depth, own = source.shape[0], outs[0].shape[1] - 8
+    depth, width = source.shape[0], source.shape[2]
+    line = lax.broadcasted_iota(jnp.int32, (8, width), 0)
     for index, target, core in targets(size, info):
-        target = target + core
+        out, target, place = outs[index], target + core, 1 - core if shared else core
         start = pl.multiple_of(target * own, 8)
         for plane in range(depth):
-            slot = (1 - core if shared else core) * depth + plane
-            outs[index][slot, 0:own, :] = source[plane, pl.ds(start, own), :]
-            outs[index][slot, own : own + 8, :] = rows_around(source, plane, target, own)
+            to = pl.multiple_of((place * depth + plane) * own, 8)
+            out[pl.ds(to, own), :] = source[plane, pl.ds(start, own), :]
+        for plane in range(0, depth, 2):
+            first, second = (rows_around(source, plane + k, target, own) for k in range(2))
+            to = pl.multiple_of(2 * depth * own + 4 * (place * depth + plane), 8)
+            out[pl.ds(to, 8), :] = jnp.where(line < 4, first, pltpu.roll(second, 4, 0))
 
 
 def pick_kernel(size, info, *refs):
     blocks, out = refs[:-1], refs[-1]
-    depth = blocks[0].shape[0]
-    chip, front = info[0], info[2]
-    count = 4 // depth
-    for part in range(count):
-        wanted = chip ^ (front * (size // 2 - count) + part)
-        for step in range(size // 2):
-
-            @pl.when(wanted == step)
-            def _():
-                out[part * depth : (part + 1) * depth] = blocks[step][...]
+    wanted = info[0] ^ (info[2] * (size // 2 - 1))
+    for step, block in enumerate(blocks):
+
+        @pl.when(wanted == step)
+        def _():
+            out[...] = block[...]
 
 
 SMEM = pl.BlockSpec(memory_space=pltpu.SMEM)
@@ -334,15 +393,17 @@
     weights = jnp.asarray(column_weights(width))
     f32 = jnp.float32
     steps = size // 2
-    block = jax.ShapeDtypeStruct((2 * depth, own + 8, width), f32)
+    chip_depth = 2 * depth
+    near_rows = 8 * (chip_depth // 2 + 1)
+    block = wide_block = jax.ShapeDtypeStruct((chip_depth * (own + 4) + near_rows, width), f32)
     image = jax.ShapeDtypeStruct((4, own, width), f32)
 
     shared = lax.ppermute(field, "depth", [(i, i ^ 1) for i in range(groups)])
     blocks = ()
     for source in (field, shared):
         blocks = pl.pallas_call(
-            functools.partial(pack_kernel, size, source is shared),
-            out_shape=(block,) * size,
+            functools.partial(pack_kernel, size, own, source is shared),
+            out_shape=(block,) * steps + (wide_block,) * steps,
             in_specs=[SMEM, VMEM] + [VMEM] * len(blocks),
             out_specs=(VMEM,) * size,
             input_output_aliases={2 + i: i for i in range(len(blocks))},
@@ -357,20 +418,22 @@
             in_specs=[SMEM] + [VMEM] * (len(args) - 1),
             out_specs=jax.tree.map(lambda _: VMEM, out_shape),
             compiler_params=PARAMS,
-            cost_estimate=cost(1000, 1000),
+            cost_estimate=cost(1000000000 if name == 'render_last' else 1000, 1000),
             name=name,
             **more,
         )(*args)
 
-    def columns_near(parts):
-        count = sum(part.shape[0] for part in parts)
+    def edges_of(parts):
+        count = chip_depth * len(parts)
         group = LANES // 8
+        shapes = (
+            jax.ShapeDtypeStruct((2, -(-count // group) * group, 8, LANES), f32),
+            jax.ShapeDtypeStruct((sent_tiles(count), 8, LANES), f32),
+        )
+        kernel = functools.partial(edge_kernel, chip_depth, own)
         edges, sent = pl.pallas_call(
-            edge_kernel,
-            out_shape=(
-                jax.ShapeDtypeStruct((2, -(-count // group) * group, 8, LANES), f32),
-                jax.ShapeDtypeStruct((sent_tiles(count), 8, LANES), f32),
-            ),
+            kernel,
+            out_shape=shapes,
             in_specs=[VMEM] * len(parts),
             out_specs=(VMEM, VMEM),
             compiler_params=PARAMS,
@@ -378,7 +441,7 @@
             name="edge_columns",
         )(*parts)
         if columns == 2:
-            return edges, lax.ppermute(sent, "cols", [(0, 1), (1, 0)])
+            return (edges,) + (lax.ppermute(sent, "cols", [(0, 1), (1, 0)]),) * 2
         return (edges,) + tuple(
             lax.ppermute(sent, "cols", [(i, i + shift) for i in range(columns) if 0 <= i + shift < columns])
             for shift in (1, -1)
@@ -387,45 +450,69 @@
     def render_call(last, parts):
         count = depth * size + (6 if last else 2)
         scratch = [pltpu.VMEM((count, own + 24, width), f32)] + [pltpu.VMEM((count - 3, own + 8, width), f32)] * 3
-        kernel = functools.partial(render_kernel, size, 2 * depth, last)
+        kernel = functools.partial(render_kernel, size, chip_depth, last)
         name = "render_last" if last else "render_first"
         return call(kernel, name, image, info, weights, *parts, scratch_shapes=scratch)
 
     def edge_scratch(last):
         return [pltpu.VMEM((depth * size + (6 if last else 2), 8, 2 * LANES), f32)] * 2
 
-    pick = pl.pallas_call(
-        functools.partial(pick_kernel, size),
-        out_shape=jax.ShapeDtypeStruct((4,) + block.shape[1:], f32),
-        in_specs=[SMEM] + [VMEM] * (size // 2),
-        out_specs=VMEM,
-        compiler_params=PARAMS,
-        cost_estimate=cost(1000, 1000),
-        name="pick_boundary",
-    )
-
     def swap(x, bits):
         return lax.ppermute(x, "depth", [(i, i ^ bits) for i in range(groups)])
 
     def gathered(parts):
         return [parts[0]] + [swap(parts[step], 2 * step) for step in range(1, steps)]
 
+    near = pltpu.VMEM((sent_tiles(chip_depth * steps), 8, LANES), f32)
+    _, before, after = edges_of(blocks[steps:])
+    ours = call(
+        functools.partial(near_kernel, chip_depth),
+        "lay_columns",
+        (wide_block,) * steps,
+        info,
+        before,
+        after,
+        *blocks[steps:],
+        scratch_shapes=[near],
+        input_output_aliases={3 + i: i for i in range(steps)},
+    )
     theirs = gathered(blocks[:steps])
-    boundary = swap(pick(info, *theirs), size)
-    first_image = render_call(False, theirs)
-    kernel = functools.partial(fix_kernel, size, 2 * depth)
-    near = columns_near(theirs)
-    first_image = call(kernel, "first_edges", image, info, first_image, *near, scratch_shapes=edge_scratch(False))
+    loose = theirs
+    theirs, _ = lax.optimization_barrier((theirs, ours))
+    boundary = swap(call(functools.partial(pick_kernel, size), "pick_boundary", block, info, *theirs), size)
+    drawn = render_call(False, theirs)
+    first_image = call(
+        functools.partial(fix_kernel, size, chip_depth),
+        "first_edges",
+        jax.ShapeDtypeStruct((4 * own + near_rows, width), f32),
+        info,
+        drawn,
+        *edges_of(theirs),
+        scratch_shapes=edge_scratch(False) + [near],
+    )
     image_part = swap(first_image, size)
-    mine = [blocks[steps]]
+    mine = [ours[0]]
     for step in range(1, steps):
-        held, _ = lax.optimization_barrier((blocks[steps + step], theirs[step]))
+        held, _ = lax.optimization_barrier((ours[step], loose[step]))
         mine.append(swap(held, 2 * step))
     parts, _ = lax.optimization_barrier((mine + [boundary], first_image))
     own_part = render_call(True, parts)
-    kernel = functools.partial(join_kernel, size, 2 * depth)
-    near = columns_near(parts)
-    return call(kernel, "join_halves", image, info, own_part, image_part, *near, scratch_shapes=edge_scratch(True))
+    planes = jax.ShapeDtypeStruct((depth * size + 6, 8, 2 * LANES), f32)
+    mine_edges = [pltpu.VMEM((2, -(-chip_depth * steps // (LANES // 8)) * (LANES // 8), 8, LANES), f32)]
+    kernel = functools.partial(own_edges_kernel, size, chip_depth, own)
+    filtered = call(kernel, "own_edges", (planes, planes), info, *parts[:-1], scratch_shapes=mine_edges)
+    return call(
+        functools.partial(join_kernel, size, chip_depth),
+        "join_halves",
+        (image, planes, planes),
+        info,
+        own_part,
+        image_part,
+        parts[-1],
+        *filtered,
+        scratch_shapes=[pltpu.VMEM((2, LANES // 8, 8, LANES), f32)],
+        input_output_aliases={4: 1, 5: 2},
+    )[0]
 
 
 def solution(mesh):

time: 52.8 us -> 52.3 us (level)
  waiting for transfers between devices: 19.5 us -> 16.3 us
  Pallas kernels: 13.7 us -> 16.1 us
    ppermute x8, waiting for transfers between devices: 17.8 us -> 12.6 us  [swap(): return lax.ppermute(x, 'depth', [(i, i ^ bits) for i in range(groups)])]
    pallas_call x4 -> x7, Pallas kernels: 10.9 us -> 13.3 us  [call(): pl.pallas_call(kernel, out_shape=out_shape, in_specs=[SMEM] + [VMEM] * (l...]
    ppermute x2, waiting for transfers between devices: 0.01 us -> 2.08 us  [edges_of(): return (edges,) + (lax.ppermute(sent, 'cols', [(0, 1), (1, 0)]),) * 2]
    pallas_call x5 -> x4, Pallas kernels: 2.87 us -> 2.86 us  [the longest x2 1.61 us: edges_of(): pl.pallas_call(kernel, out_shape=shapes, in_specs=[VMEM] * len(parts), ou...]
  transfers between devices with their start and end apart: 11 -> 11, of which waited for: 6 -> 7; matrix products, arithmetic and copies ran while one was open for 0% -> 0% of each run, Pallas kernels for 21% -> 25%
where the time goes in v8:
time: 52.3 us; the launch traced here: 52.2 us
  starting transfers between devices  18 us (34%)
  waiting for transfers between devices  16.3 us (31%)
  Pallas kernels  16.1 us (31%)
  local copies, waits for them, and re-layouts  1.68 us (3%)
    ppermute x8, starting transfers between devices, swap(): return lax.ppermute(x, 'depth', [(i, i ^ bits) for i in range(groups)])  14.1 us
    pallas_call x7, Pallas kernels, call(): pl.pallas_call(kernel, out_shape=out_shape, in_specs=[SMEM] + [VMEM] * (l...  13.3 us
    ppermute x8, waiting for transfers between devices, swap(): return lax.ppermute(x, 'depth', [(i, i ^ bits) for i in range(groups)])  12.6 us
    ppermute x2, starting transfers between devices, edges_of(): return (edges,) + (lax.ppermute(sent, 'cols', [(0, 1), (1, 0)]),) * 2  3.44 us
    ppermute x2, waiting for transfers between devices, edges_of(): return (edges,) + (lax.ppermute(sent, 'cols', [(0, 1), (1, 0)]),) * 2  2.08 us
    ppermute x1, waiting for transfers between devices, local(): shared = lax.ppermute(field, 'depth', [(i, i ^ 1) for i in range(groups)])  1.69 us
    pallas_call x2, Pallas kernels, edges_of(): pl.pallas_call(kernel, out_shape=shapes, in_specs=[VMEM] * len(parts), ou...  1.61 us
    unnamed x4, local copies, waits for them, and re-layouts  1.59 us
  transfers between devices with their start and end apart: 11, of which 7 were waited for; matrix products, arithmetic and copies ran while one was open for 0% of the time, Pallas kernels for 25%

profile of v8, /device:TPU:0, one launch (start us, length us, event | category | flops | bytes accessed | tf_op | source)
XLA Modules:
  0.0 52.2 jit_solution(17808356697194659712)
XLA Ops:
  0.5 1.6 %copy-done = f32[2,2048,128]{2,1,0:T(8,128)S(1)} copy-done((f32[2,2048,128]{2,1,0:T(8,128)S(1)}, f32[2,2048,128]{2,1,0:T(8,128)}, u32[]{:S(2)}) %copy-start) | copy-done | bytes 2097176
  2.1 0.6 %pack_own.1 = (f32[552,128]{1,0:T(8,128)S(1)}, f32[552,128]{1,0:T(8,128)S(1)}, f32[552,128]{1,0:T(8,128)S(1)}, f32[552,128]{1,0:T(8,128)S(1)}, f32[552,128]{1,0:...) custom-call(s32[5]{0:T(128)S(1)} %stack.31.info, f32[2,2048,128]{2,1,0:T(8,128)S(1)} %copy-done), custom_call_target="tpu_custom_call" | custom-call | tf_op jit(solution)/shard_map/pack_own/pallas_call | solution.py:404
  2.8 1.7 %collective-permute-done.source = f32[2,2048,128]{2,1,0:T(8,128)S(1)} collective-permute-done((f32[2,2048,128]{2,1,0:T(8,128)}, f32[2,2048,128]{2,1,0:T(8,128)S(1)}, u32[]{:S(2)}, u32[]{:S(2)}) %collective-permute-start) | collective-permute-done | bytes 2097184 | tf_op jit(solution)/shard_map/ppermute | solution.py:401
  4.5 0.6 %pack_shared.1 = (f32[552,128]{1,0:T(8,128)S(1)}, f32[552,128]{1,0:T(8,128)S(1)}, f32[552,128]{1,0:T(8,128)S(1)}, f32[552,128]{1,0:T(8,128)S(1)}, f32[552,128]{1...) custom-call(s32[5]{0:T(128)S(1)} %stack.31.info, ...), custom_call_target="tpu_custom_call", output_to_operand_aliasing={{0}: (2, {}), {1}: (3, {}), {2}: (4, {}), {3}: (5, {}), {4}... | custom-call | tf_op jit(solution)/shard_map/pack_shared/pallas_call | solution.py:404
  5.1 3.0 %collective-permute-start.2 = (f32[552,128]{1,0:T(8,128)S(1)}, f32[552,128]{1,0:T(8,128)S(1)}, u32[]{:S(2)}, u32[]{:S(2)}) collective-permute-start(f32[552,128]{1,0:T(8,128)S(1)} %get-tuple-element.58), channel_id=1, source_target_pairs={{0,4},{2,6},{4,0},{6,2},{8,12},{10,14},{12,8},{14,10},{16,20},{18,... | collective-permute-start | bytes 847880 | tf_op jit(solution)/shard_map/ppermute | solution.py:461
  8.0 1.6 %collective-permute-start.4 = (f32[552,128]{1,0:T(8,128)S(1)}, f32[552,128]{1,0:T(8,128)S(1)}, u32[]{:S(2)}, u32[]{:S(2)}) collective-permute-start(f32[552,128]{1,0:T(8,128)S(1)} %get-tuple-element.61), channel_id=1, source_target_pairs={{0,8},{2,10},{4,12},{6,14},{8,0},{10,2},{12,4},{14,6},{16,24},{18,... | collective-permute-start | bytes 847880 | tf_op jit(solution)/shard_map/ppermute | solution.py:461
  9.6 1.1 %edge_columns.2 = (f32[2,16,8,128]{3,2,1,0:T(8,128)}, f32[9,8,128]{2,1,0:T(8,128)S(1)}) custom-call(f32[552,128]{1,0:T(8,128)S(1)} %get-tuple-element.51.refs_0_, f32[552,128]{1,0:T(8,128)S(1)} %get-tuple-element.52.refs_1_, f32[552,128]{1,0:T(8,128)S(1)} %get-tuple-element.53.refs_2_, f32[552,128]{1,0:T(8,128)S(1)} %get-tuple-element.54.refs_3_), custom_call_target="tpu_custom_call" | custom-call | flops 1000 | bytes 1000 | tf_op jit(solution)/shard_map/edge_columns/pallas_call | solution.py:434
  10.7 1.9 %collective-permute-start.1 = (f32[9,8,128]{2,1,0:T(8,128)S(1)}, f32[9,8,128]{2,1,0:T(8,128)S(1)}, u32[]{:S(2)}, u32[]{:S(2)}) collective-permute-start(f32[9,8,128]{2,1,0:T(8,128)S(1)} %get-tuple-element.55), channel_id=1, source_target_pairs={{0,1},{1,0},{2,3},{3,2},{4,5},{5,4},{6,7},{7,6},{8,9},{9,8},{10,11... | collective-permute-start | bytes 110600 | tf_op jit(solution)/shard_map/ppermute | solution.py:444
  12.6 2.1 %collective-permute-done.1.before.after = f32[9,8,128]{2,1,0:T(8,128)S(1)} collective-permute-done((f32[9,8,128]{2,1,0:T(8,128)S(1)}, f32[9,8,128]{2,1,0:T(8,128)S(1)}, u32[]{:S(2)}, u32[]{:S(2)}) %collective-permute-start.1) | collective-permute-done | bytes 36896 | tf_op jit(solution)/shard_map/ppermute | solution.py:444
  14.7 0.6 %lay_columns.1 = (f32[552,128]{1,0:T(8,128)S(1)}, f32[552,128]{1,0:T(8,128)S(1)}, f32[552,128]{1,0:T(8,128)S(1)}, f32[552,128]{1,0:T(8,128)S(1)}) custom-call(s32[5]{0:T(128)S(1)} %stack.31.info, f32[9,8,128]{2,1,0:T(8,128)S(1)} %collective-permute-done.1.before.after, ...), custom_call_target="tpu_custom_call", output_to_operand_aliasing={{0}: (3, {}), {1}: (4, {}), {2}: (5, {}), {3}: (6, {})} | custom-call | flops 1000 | bytes 1000 | tf_op jit(solution)/shard_map/lay_columns/pallas_call | solution.py:415
  15.3 1.9 %collective-permute-start.3 = (f32[552,128]{1,0:T(8,128)S(1)}, f32[552,128]{1,0:T(8,128)S(1)}, u32[]{:S(2)}, u32[]{:S(2)}) collective-permute-start(f32[552,128]{1,0:T(8,128)S(1)} %get-tuple-element.59), channel_id=1, source_target_pairs={{0,4},{2,6},{4,0},{6,2},{8,12},{10,14},{12,8},{14,10},{16,20},{18,... | collective-permute-start | bytes 847880 | tf_op jit(solution)/shard_map/ppermute | solution.py:461
  17.7 1.6 %collective-permute-start.5 = (f32[552,128]{1,0:T(8,128)S(1)}, f32[552,128]{1,0:T(8,128)S(1)}, u32[]{:S(2)}, u32[]{:S(2)}) collective-permute-start(f32[552,128]{1,0:T(8,128)S(1)} %get-tuple-element.62), channel_id=1, source_target_pairs={{0,8},{2,10},{4,12},{6,14},{8,0},{10,2},{12,4},{14,6},{16,24},{18,... | collective-permute-start | bytes 847880 | tf_op jit(solution)/shard_map/ppermute | solution.py:461
  19.2 4.0 %collective-permute-done.6.refs_3_ = f32[552,128]{1,0:T(8,128)S(1)} collective-permute-done((f32[552,128]{1,0:T(8,128)S(1)}, f32[552,128]{1,0:T(8,128)S(1)}, u32[]{:S(2)}, u32[]{:S(2)}) %collective-permute-start.6) | collective-permute-done | bytes 282656 | tf_op jit(solution)/shard_map/ppermute | solution.py:461
  23.2 0.6 %pick_boundary.1 = f32[552,128]{1,0:T(8,128)S(1)} custom-call(s32[5]{0:T(128)S(1)} %stack.31.info, f32[552,128]{1,0:T(8,128)S(1)} %get-tuple-element.67.refs_0_, f32[552,128]{1,0:T(8,128)S(1)} %collective-permute-done.2.refs_1_, f32[552,128]{1,0:T(8,128)S(1)} %collective-permute-done.4.refs_2_, f32[552,128]{1,0:T(8,128)S(1)} %collective-permute-done.6.refs_3_), custom_call_target="tpu_custom_call" | custom-call | flops 1000 | bytes 1000 | tf_op jit(solution)/shard_map/pick_boundary/pallas_call | solution.py:415
  23.8 3.1 %collective-permute-start.8 = (f32[552,128]{1,0:T(8,128)S(1)}, f32[552,128]{1,0:T(8,128)S(1)}, u32[]{:S(2)}, u32[]{:S(2)}) collective-permute-start(f32[552,128]{1,0:T(8,128)S(1)} %pick_boundary.1), channel_id=1, source_target_pairs={{0,16},{2,18},{4,20},{6,22},{8,24},{10,26},{12,28},{14,30},{16,0},... | collective-permute-start | bytes 847880 | tf_op jit(solution)/shard_map/ppermute | solution.py:461
  26.9 2.5 %collective-permute-start.7 = (f32[552,128]{1,0:T(8,128)S(1)}, f32[552,128]{1,0:T(8,128)S(1)}, u32[]{:S(2)}, u32[]{:S(2)}) collective-permute-start(f32[552,128]{1,0:T(8,128)S(1)} %get-tuple-element.65), channel_id=1, source_target_pairs={{0,12},{2,14},{4,8},{6,10},{8,4},{10,6},{12,0},{14,2},{16,28},{18,... | collective-permute-start | bytes 847880 | tf_op jit(solution)/shard_map/ppermute | solution.py:461
  30.0 1.6 %collective-permute-start.9 = (f32[9,8,128]{2,1,0:T(8,128)S(1)}, f32[9,8,128]{2,1,0:T(8,128)S(1)}, u32[]{:S(2)}, u32[]{:S(2)}) collective-permute-start(f32[9,8,128]{2,1,0:T(8,128)S(1)} %get-tuple-element.72), channel_id=1, source_target_pairs={{0,1},{1,0},{2,3},{3,2},{4,5},{5,4},{6,7},{7,6},{8,9},{9,8},{10,11... | collective-permute-start | bytes 110600 | tf_op jit(solution)/shard_map/ppermute | solution.py:444
  31.6 3.3 %render_first.1.image = f32[4,128,128]{2,1,0:T(8,128)S(1)} custom-call(s32[5]{0:T(128)S(1)} %stack.31.info, bf16[384,256]{1,0:T(8,128)(2,1)S(1)} %copy-done.1, f32[552,128]{1,0:T(8,128)S(1)} %get-tuple-element.67.refs_0_, f32[552,128]{1,0:T(8,128)S(1)} %collective-permute-done.2.refs_1_, f32[552,128]{1,0:T(8,128)S(1)} %collective-permute-done.4.refs_2_, ...), custom_call_target="tpu_custom_call" | custom-call | flops 1000 | bytes 1000 | tf_op jit(solution)/shard_map/render_first/pallas_call | solution.py:415
  34.8 1.4 %first_edges.1 = f32[536,128]{1,0:T(8,128)S(1)} custom-call(s32[5]{0:T(128)S(1)} %stack.31.info, f32[4,128,128]{2,1,0:T(8,128)S(1)} %render_first.1.image, f32[2,16,8,128]{3,2,1,0:T(8,128)S(1)} %get-tuple-element.71.mine, f32[9,8,128]{2,1,0:T(8,128)S(1)} %collective-permute-done.9.before.after, f32[9,8,128]{2,1,0:T(8,128)S(1)} %collective-permute-done.9.before.after), custom_call_target="tpu_custom_call" | custom-call | flops 1000 | bytes 1000 | tf_op jit(solution)/shard_map/first_edges/pallas_call | solution.py:415
  36.7 2.1 %collective-permute-done.8.refs_4_.boundary = f32[552,128]{1,0:T(8,128)S(1)} collective-permute-done((f32[552,128]{1,0:T(8,128)S(1)}, f32[552,128]{1,0:T(8,128)S(1)}, u32[]{:S(2)}, u32[]{:S(2)}) %collective-permute-start.8) | collective-permute-done | bytes 282656 | tf_op jit(solution)/shard_map/ppermute | solution.py:461
  38.7 5.9 %collective-permute-done.7.refs_3_ = f32[552,128]{1,0:T(8,128)S(1)} collective-permute-done((f32[552,128]{1,0:T(8,128)S(1)}, f32[552,128]{1,0:T(8,128)S(1)}, u32[]{:S(2)}, u32[]{:S(2)}) %collective-permute-start.7) | collective-permute-done | bytes 282656 | tf_op jit(solution)/shard_map/ppermute | solution.py:461
  44.7 1.1 %own_edges.1 = (f32[22,8,256]{2,1,0:T(8,128)S(1)}, f32[22,8,256]{2,1,0:T(8,128)S(1)}) custom-call(s32[5]{0:T(128)S(1)} %stack.31.info, f32[552,128]{1,0:T(8,128)S(1)} %get-tuple-element.73.refs_0_, f32[552,128]{1,0:T(8,128)S(1)} %collective-permute-done.3.refs_1_, f32[552,128]{1,0:T(8,128)S(1)} %collective-permute-done.5.refs_2_, ...), custom_call_target="tpu_custom_call" | custom-call | flops 1000 | bytes 1000 | tf_op jit(solution)/shard_map/own_edges/pallas_call | solution.py:415
  45.8 3.9 %render_last.1.image = f32[4,128,128]{2,1,0:T(8,128)S(1)} custom-call(s32[5]{0:T(128)S(1)} %stack.31.info, bf16[384,256]{1,0:T(8,128)(2,1)S(1)} %copy-done.1, f32[552,128]{1,0:T(8,128)S(1)} %get-tuple-element.73.refs_0_, f32[552,128]{1,0:T(8,128)S(1)} %collective-permute-done.3.refs_1_, f32[552,128]{1,0:T(8,128)S(1)} %collective-permute-done.5.refs_2_, ...), custom_call_target="tpu_custom_call" | custom-call | flops 1000000000 | bytes 1000 | tf_op jit(solution)/shard_map/render_last/pallas_call | solution.py:415
  49.9 2.3 %join_halves.1 = (f32[4,128,128]{2,1,0:T(8,128)}, f32[22,8,256]{2,1,0:T(8,128)S(1)}, f32[22,8,256]{2,1,0:T(8,128)S(1)}) custom-call(s32[5]{0:T(128)S(1)} %stack.31.info, f32[4,128,128]{2,1,0:T(8,128)S(1)} %render_last.1.image, f32[536,128]{1,0:T(8,128)S(1)} %collective-permute-done.10.other, ...), custom_call_target="tpu_custom_call", output_to_operand_aliasing={{1}: (4, {}), {2}: (5, {})} | custom-call | flops 1000 | bytes 1000 | tf_op jit(solution)/shard_map/join_halves/pallas_call | solution.py:415
  (14 shorter events, 2.0 us)
Async XLA Ops:
  0.0 4.5 %collective-permute-start = (f32[2,2048,128]{2,1,0:T(8,128)}, f32[2,2048,128]{2,1,0:T(8,128)S(1)}, u32[]{:S(2)}, u32[]{:S(2)}) collective-permute-start(f32[2,2048,128]{2,1,0:T(8,128)} %source.1), channel_id=1, source_target_pairs={{0,2},{2,0},{4,6},{6,4},{8,10},{10,8},{12,14},{14,12},{16,18},{18,... | collective-permute-start | bytes 6291464 | tf_op jit(solution)/shard_map/ppermute | solution.py:401
  0.5 1.6 %copy-start = (f32[2,2048,128]{2,1,0:T(8,128)S(1)}, f32[2,2048,128]{2,1,0:T(8,128)}, u32[]{:S(2)}) copy-start(f32[2,2048,128]{2,1,0:T(8,128)} %source.1) | copy-start | bytes 6291460
  5.1 10.2 %collective-permute-start.2 = (f32[552,128]{1,0:T(8,128)S(1)}, f32[552,128]{1,0:T(8,128)S(1)}, u32[]{:S(2)}, u32[]{:S(2)}) collective-permute-start(f32[552,128]{1,0:T(8,128)S(1)} %get-tuple-element.58), channel_id=1, source_target_pairs={{0,4},{2,6},{4,0},{6,2},{8,12},{10,14},{12,8},{14,10},{16,20},{18,... | collective-permute-start | bytes 847880 | tf_op jit(solution)/shard_map/ppermute | solution.py:461
  8.0 9.6 %collective-permute-start.4 = (f32[552,128]{1,0:T(8,128)S(1)}, f32[552,128]{1,0:T(8,128)S(1)}, u32[]{:S(2)}, u32[]{:S(2)}) collective-permute-start(f32[552,128]{1,0:T(8,128)S(1)} %get-tuple-element.61), channel_id=1, source_target_pairs={{0,8},{2,10},{4,12},{6,14},{8,0},{10,2},{12,4},{14,6},{16,24},{18,... | collective-permute-start | bytes 847880 | tf_op jit(solution)/shard_map/ppermute | solution.py:461
  9.6 13.6 %collective-permute-start.6 = (f32[552,128]{1,0:T(8,128)S(1)}, f32[552,128]{1,0:T(8,128)S(1)}, u32[]{:S(2)}, u32[]{:S(2)}) collective-permute-start(f32[552,128]{1,0:T(8,128)S(1)} %get-tuple-element.64), channel_id=1, source_target_pairs={{0,12},{2,14},{4,8},{6,10},{8,4},{10,6},{12,0},{14,2},{16,28},{18,... | collective-permute-start | bytes 847880 | tf_op jit(solution)/shard_map/ppermute | solution.py:461
  10.7 20.8 %copy-start.1 = (bf16[384,256]{1,0:T(8,128)(2,1)S(1)}, bf16[384,256]{1,0:T(8,128)(2,1)}, u32[]{:S(2)}) copy-start(bf16[384,256]{1,0:T(8,128)(2,1)} %constant.55.clone.weights) | copy-start | bytes 589828
  10.7 4.0 %collective-permute-start.1 = (f32[9,8,128]{2,1,0:T(8,128)S(1)}, f32[9,8,128]{2,1,0:T(8,128)S(1)}, u32[]{:S(2)}, u32[]{:S(2)}) collective-permute-start(f32[9,8,128]{2,1,0:T(8,128)S(1)} %get-tuple-element.55), channel_id=1, source_target_pairs={{0,1},{1,0},{2,3},{3,2},{4,5},{5,4},{6,7},{7,6},{8,9},{9,8},{10,11... | collective-permute-start | bytes 110600 | tf_op jit(solution)/shard_map/ppermute | solution.py:444
  15.3 21.4 %collective-permute-start.3 = (f32[552,128]{1,0:T(8,128)S(1)}, f32[552,128]{1,0:T(8,128)S(1)}, u32[]{:S(2)}, u32[]{:S(2)}) collective-permute-start(f32[552,128]{1,0:T(8,128)S(1)} %get-tuple-element.59), channel_id=1, source_target_pairs={{0,4},{2,6},{4,0},{6,2},{8,12},{10,14},{12,8},{14,10},{16,20},{18,... | collective-permute-start | bytes 847880 | tf_op jit(solution)/shard_map/ppermute | solution.py:461
  17.7 19.0 %collective-permute-start.5 = (f32[552,128]{1,0:T(8,128)S(1)}, f32[552,128]{1,0:T(8,128)S(1)}, u32[]{:S(2)}, u32[]{:S(2)}) collective-permute-start(f32[552,128]{1,0:T(8,128)S(1)} %get-tuple-element.62), channel_id=1, source_target_pairs={{0,8},{2,10},{4,12},{6,14},{8,0},{10,2},{12,4},{14,6},{16,24},{18,... | collective-permute-start | bytes 847880 | tf_op jit(solution)/shard_map/ppermute | solution.py:461
  23.8 14.9 %collective-permute-start.8 = (f32[552,128]{1,0:T(8,128)S(1)}, f32[552,128]{1,0:T(8,128)S(1)}, u32[]{:S(2)}, u32[]{:S(2)}) collective-permute-start(f32[552,128]{1,0:T(8,128)S(1)} %pick_boundary.1), channel_id=1, source_target_pairs={{0,16},{2,18},{4,20},{6,22},{8,24},{10,26},{12,28},{14,30},{16,0},... | collective-permute-start | bytes 847880 | tf_op jit(solution)/shard_map/ppermute | solution.py:461
  26.9 17.7 %collective-permute-start.7 = (f32[552,128]{1,0:T(8,128)S(1)}, f32[552,128]{1,0:T(8,128)S(1)}, u32[]{:S(2)}, u32[]{:S(2)}) collective-permute-start(f32[552,128]{1,0:T(8,128)S(1)} %get-tuple-element.65), channel_id=1, source_target_pairs={{0,12},{2,14},{4,8},{6,10},{8,4},{10,6},{12,0},{14,2},{16,28},{18,... | collective-permute-start | bytes 847880 | tf_op jit(solution)/shard_map/ppermute | solution.py:461
  30.0 4.8 %collective-permute-start.9 = (f32[9,8,128]{2,1,0:T(8,128)S(1)}, f32[9,8,128]{2,1,0:T(8,128)S(1)}, u32[]{:S(2)}, u32[]{:S(2)}) collective-permute-start(f32[9,8,128]{2,1,0:T(8,128)S(1)} %get-tuple-element.72), channel_id=1, source_target_pairs={{0,1},{1,0},{2,3},{3,2},{4,5},{5,4},{6,7},{7,6},{8,9},{9,8},{10,11... | collective-permute-start | bytes 110600 | tf_op jit(solution)/shard_map/ppermute | solution.py:444
  36.3 13.6 %collective-permute-start.10 = (f32[536,128]{1,0:T(8,128)S(1)}, f32[536,128]{1,0:T(8,128)S(1)}, u32[]{:S(2)}, u32[]{:S(2)}) collective-permute-start(f32[536,128]{1,0:T(8,128)S(1)} %first_edges.1), channel_id=1, source_target_pairs={{0,16},{2,18},{4,20},{6,22},{8,24},{10,26},{12,28},{14,30},{16,0},... | collective-permute-start | bytes 823304 | tf_op jit(solution)/shard_map/ppermute | solution.py:461

commit v9 on v8

--- a/solution.py
+++ b/solution.py
@@ -16,7 +16,7 @@
 HALF_LEN = math.sqrt(0.48 * 0.48 + 0.6 * 0.6 + 1.64 * 1.64)
 SPEC = 0.35 / HALF_LEN**8
 LANES = 128
-TILE = 16
+TILE = 32
 
 
 def column_weights(width):
@@ -37,12 +37,12 @@
     return hi, mid, lo
 
 
-def filter_columns(planes, index, weights, sx, dx):
-    width = planes.shape[2]
-    row = jnp.concatenate(three_parts(planes[index]), 1)
-    both = jnp.dot(row, weights[...], preferred_element_type=jnp.float32)
-    sx[index] = both[:, :width]
-    dx[index] = both[:, width:]
+def filter_columns(planes, first, count, weights, sx, dx):
+    rows, width = planes.shape[1:]
+    flat = planes[first : first + count].reshape(count * rows, width)
+    both = jnp.dot(jnp.concatenate(three_parts(flat), 1), weights[...], preferred_element_type=jnp.float32)
+    sx[first : first + count] = both[:, :width].reshape(count, rows, width)
+    dx[first : first + count] = both[:, width:].reshape(count, rows, width)
 
 
 def gauss_rows(a, b, c, d, e):
@@ -134,8 +134,9 @@
         cube(pl.multiple_of(tile * TILE, TILE), TILE)
 
     cube(own, 8)
-    for index in range(cubed.shape[0]):
-        filter_columns(cubed, index, weights, sx, dx)
+    group = 8
+    for index in range(0, cubed.shape[0], group):
+        filter_columns(cubed, index, min(group, cubed.shape[0] - index), weights, sx, dx)
 
     @pl.loop(0, own // TILE)
     def _(tile):
@@ -359,6 +360,9 @@
             first, second = (rows_around(source, plane + k, target, own) for k in range(2))
             to = pl.multiple_of(2 * depth * own + 4 * (place * depth + plane), 8)
             out[pl.ds(to, 8), :] = jnp.where(line < 4, first, pltpu.roll(second, 4, 0))
+        if not shared:
+            used = 2 * depth * (own + 4)
+            out[used:] = jnp.zeros((out.shape[0] - used, width), jnp.float32)
 
 
 def pick_kernel(size, info, *refs):
@@ -418,7 +422,7 @@
             in_specs=[SMEM] + [VMEM] * (len(args) - 1),
             out_specs=jax.tree.map(lambda _: VMEM, out_shape),
             compiler_params=PARAMS,
-            cost_estimate=cost(1000000000 if name == 'render_last' else 1000, 1000),
+            cost_estimate=cost(1_000_000_000 if name == "render_last" else 1000, 1000),
             name=name,
             **more,
         )(*args)

time: 52.3 us -> 52.3 us (level)
  no operation moved by 1% of the time
where the time goes in v9:
time: 52.3 us; the launch traced here: 52.2 us
  starting transfers between devices  18 us (34%)
  waiting for transfers between devices  16.5 us (32%)
  Pallas kernels  15.9 us (30%)
  local copies, waits for them, and re-layouts  1.68 us (3%)
    ppermute x8, starting transfers between devices, swap(): return lax.ppermute(x, 'depth', [(i, i ^ bits) for i in range(groups)])  14.1 us
    pallas_call x7, Pallas kernels, call(): pl.pallas_call(kernel, out_shape=out_shape, in_specs=[SMEM] + [VMEM] * (l...  13.1 us
    ppermute x8, waiting for transfers between devices, swap(): return lax.ppermute(x, 'depth', [(i, i ^ bits) for i in range(groups)])  12.8 us
    ppermute x2, starting transfers between devices, edges_of(): return (edges,) + (lax.ppermute(sent, 'cols', [(0, 1), (1, 0)]),) * 2  3.44 us
    ppermute x2, waiting for transfers between devices, edges_of(): return (edges,) + (lax.ppermute(sent, 'cols', [(0, 1), (1, 0)]),) * 2  2.08 us
    ppermute x1, waiting for transfers between devices, local(): shared = lax.ppermute(field, 'depth', [(i, i ^ 1) for i in range(groups)])  1.68 us
    pallas_call x2, Pallas kernels, edges_of(): pl.pallas_call(kernel, out_shape=shapes, in_specs=[VMEM] * len(parts), ou...  1.61 us
    unnamed x4, local copies, waits for them, and re-layouts  1.59 us
  transfers between devices with their start and end apart: 11, of which 7 were waited for; matrix products, arithmetic and copies ran while one was open for 0% of the time, Pallas kernels for 25%

profile of v9, /device:TPU:0, one launch (start us, length us, event | category | flops | bytes accessed | tf_op | source)
XLA Modules:
  0.0 52.2 jit_solution(3464944118453359495)
XLA Ops:
  0.5 1.6 %copy-done = f32[2,2048,128]{2,1,0:T(8,128)S(1)} copy-done((f32[2,2048,128]{2,1,0:T(8,128)S(1)}, f32[2,2048,128]{2,1,0:T(8,128)}, u32[]{:S(2)}) %copy-start) | copy-done | bytes 2097176
  2.1 0.6 %pack_own.1 = (f32[552,128]{1,0:T(8,128)S(1)}, f32[552,128]{1,0:T(8,128)S(1)}, f32[552,128]{1,0:T(8,128)S(1)}, f32[552,128]{1,0:T(8,128)S(1)}, f32[552,128]{1,0:...) custom-call(s32[5]{0:T(128)S(1)} %stack.31.info, f32[2,2048,128]{2,1,0:T(8,128)S(1)} %copy-done), custom_call_target="tpu_custom_call" | custom-call | tf_op jit(solution)/shard_map/pack_own/pallas_call | solution.py:408
  2.8 1.7 %collective-permute-done.source = f32[2,2048,128]{2,1,0:T(8,128)S(1)} collective-permute-done((f32[2,2048,128]{2,1,0:T(8,128)}, f32[2,2048,128]{2,1,0:T(8,128)S(1)}, u32[]{:S(2)}, u32[]{:S(2)}) %collective-permute-start) | collective-permute-done | bytes 2097184 | tf_op jit(solution)/shard_map/ppermute | solution.py:405
  4.5 0.6 %pack_shared.1 = (f32[552,128]{1,0:T(8,128)S(1)}, f32[552,128]{1,0:T(8,128)S(1)}, f32[552,128]{1,0:T(8,128)S(1)}, f32[552,128]{1,0:T(8,128)S(1)}, f32[552,128]{1...) custom-call(s32[5]{0:T(128)S(1)} %stack.31.info, ...), custom_call_target="tpu_custom_call", output_to_operand_aliasing={{0}: (2, {}), {1}: (3, {}), {2}: (4, {}), {3}: (5, {}), {4}... | custom-call | tf_op jit(solution)/shard_map/pack_shared/pallas_call | solution.py:408
  5.1 3.0 %collective-permute-start.2 = (f32[552,128]{1,0:T(8,128)S(1)}, f32[552,128]{1,0:T(8,128)S(1)}, u32[]{:S(2)}, u32[]{:S(2)}) collective-permute-start(f32[552,128]{1,0:T(8,128)S(1)} %get-tuple-element.58), channel_id=1, source_target_pairs={{0,4},{2,6},{4,0},{6,2},{8,12},{10,14},{12,8},{14,10},{16,20},{18,... | collective-permute-start | bytes 847880 | tf_op jit(solution)/shard_map/ppermute | solution.py:465
  8.0 1.6 %collective-permute-start.4 = (f32[552,128]{1,0:T(8,128)S(1)}, f32[552,128]{1,0:T(8,128)S(1)}, u32[]{:S(2)}, u32[]{:S(2)}) collective-permute-start(f32[552,128]{1,0:T(8,128)S(1)} %get-tuple-element.61), channel_id=1, source_target_pairs={{0,8},{2,10},{4,12},{6,14},{8,0},{10,2},{12,4},{14,6},{16,24},{18,... | collective-permute-start | bytes 847880 | tf_op jit(solution)/shard_map/ppermute | solution.py:465
  9.6 1.1 %edge_columns.2 = (f32[2,16,8,128]{3,2,1,0:T(8,128)}, f32[9,8,128]{2,1,0:T(8,128)S(1)}) custom-call(f32[552,128]{1,0:T(8,128)S(1)} %get-tuple-element.51.refs_0_, f32[552,128]{1,0:T(8,128)S(1)} %get-tuple-element.52.refs_1_, f32[552,128]{1,0:T(8,128)S(1)} %get-tuple-element.53.refs_2_, f32[552,128]{1,0:T(8,128)S(1)} %get-tuple-element.54.refs_3_), custom_call_target="tpu_custom_call" | custom-call | flops 1000 | bytes 1000 | tf_op jit(solution)/shard_map/edge_columns/pallas_call | solution.py:438
  10.7 1.9 %collective-permute-start.1 = (f32[9,8,128]{2,1,0:T(8,128)S(1)}, f32[9,8,128]{2,1,0:T(8,128)S(1)}, u32[]{:S(2)}, u32[]{:S(2)}) collective-permute-start(f32[9,8,128]{2,1,0:T(8,128)S(1)} %get-tuple-element.55), channel_id=1, source_target_pairs={{0,1},{1,0},{2,3},{3,2},{4,5},{5,4},{6,7},{7,6},{8,9},{9,8},{10,11... | collective-permute-start | bytes 110600 | tf_op jit(solution)/shard_map/ppermute | solution.py:448
  12.6 2.1 %collective-permute-done.1.before.after = f32[9,8,128]{2,1,0:T(8,128)S(1)} collective-permute-done((f32[9,8,128]{2,1,0:T(8,128)S(1)}, f32[9,8,128]{2,1,0:T(8,128)S(1)}, u32[]{:S(2)}, u32[]{:S(2)}) %collective-permute-start.1) | collective-permute-done | bytes 36896 | tf_op jit(solution)/shard_map/ppermute | solution.py:448
  14.7 0.6 %lay_columns.1 = (f32[552,128]{1,0:T(8,128)S(1)}, f32[552,128]{1,0:T(8,128)S(1)}, f32[552,128]{1,0:T(8,128)S(1)}, f32[552,128]{1,0:T(8,128)S(1)}) custom-call(s32[5]{0:T(128)S(1)} %stack.31.info, f32[9,8,128]{2,1,0:T(8,128)S(1)} %collective-permute-done.1.before.after, ...), custom_call_target="tpu_custom_call", output_to_operand_aliasing={{0}: (3, {}), {1}: (4, {}), {2}: (5, {}), {3}: (6, {})} | custom-call | flops 1000 | bytes 1000 | tf_op jit(solution)/shard_map/lay_columns/pallas_call | solution.py:419
  15.3 1.9 %collective-permute-start.3 = (f32[552,128]{1,0:T(8,128)S(1)}, f32[552,128]{1,0:T(8,128)S(1)}, u32[]{:S(2)}, u32[]{:S(2)}) collective-permute-start(f32[552,128]{1,0:T(8,128)S(1)} %get-tuple-element.59), channel_id=1, source_target_pairs={{0,4},{2,6},{4,0},{6,2},{8,12},{10,14},{12,8},{14,10},{16,20},{18,... | collective-permute-start | bytes 847880 | tf_op jit(solution)/shard_map/ppermute | solution.py:465
  17.7 1.6 %collective-permute-start.5 = (f32[552,128]{1,0:T(8,128)S(1)}, f32[552,128]{1,0:T(8,128)S(1)}, u32[]{:S(2)}, u32[]{:S(2)}) collective-permute-start(f32[552,128]{1,0:T(8,128)S(1)} %get-tuple-element.62), channel_id=1, source_target_pairs={{0,8},{2,10},{4,12},{6,14},{8,0},{10,2},{12,4},{14,6},{16,24},{18,... | collective-permute-start | bytes 847880 | tf_op jit(solution)/shard_map/ppermute | solution.py:465
  19.2 4.0 %collective-permute-done.6.refs_3_ = f32[552,128]{1,0:T(8,128)S(1)} collective-permute-done((f32[552,128]{1,0:T(8,128)S(1)}, f32[552,128]{1,0:T(8,128)S(1)}, u32[]{:S(2)}, u32[]{:S(2)}) %collective-permute-start.6) | collective-permute-done | bytes 282656 | tf_op jit(solution)/shard_map/ppermute | solution.py:465
  23.2 0.6 %pick_boundary.1 = f32[552,128]{1,0:T(8,128)S(1)} custom-call(s32[5]{0:T(128)S(1)} %stack.31.info, f32[552,128]{1,0:T(8,128)S(1)} %get-tuple-element.67.refs_0_, f32[552,128]{1,0:T(8,128)S(1)} %collective-permute-done.2.refs_1_, f32[552,128]{1,0:T(8,128)S(1)} %collective-permute-done.4.refs_2_, f32[552,128]{1,0:T(8,128)S(1)} %collective-permute-done.6.refs_3_), custom_call_target="tpu_custom_call" | custom-call | flops 1000 | bytes 1000 | tf_op jit(solution)/shard_map/pick_boundary/pallas_call | solution.py:419
  23.8 3.1 %collective-permute-start.8 = (f32[552,128]{1,0:T(8,128)S(1)}, f32[552,128]{1,0:T(8,128)S(1)}, u32[]{:S(2)}, u32[]{:S(2)}) collective-permute-start(f32[552,128]{1,0:T(8,128)S(1)} %pick_boundary.1), channel_id=1, source_target_pairs={{0,16},{2,18},{4,20},{6,22},{8,24},{10,26},{12,28},{14,30},{16,0},... | collective-permute-start | bytes 847880 | tf_op jit(solution)/shard_map/ppermute | solution.py:465
  26.9 2.5 %collective-permute-start.7 = (f32[552,128]{1,0:T(8,128)S(1)}, f32[552,128]{1,0:T(8,128)S(1)}, u32[]{:S(2)}, u32[]{:S(2)}) collective-permute-start(f32[552,128]{1,0:T(8,128)S(1)} %get-tuple-element.65), channel_id=1, source_target_pairs={{0,12},{2,14},{4,8},{6,10},{8,4},{10,6},{12,0},{14,2},{16,28},{18,... | collective-permute-start | bytes 847880 | tf_op jit(solution)/shard_map/ppermute | solution.py:465
  30.0 1.6 %collective-permute-start.9 = (f32[9,8,128]{2,1,0:T(8,128)S(1)}, f32[9,8,128]{2,1,0:T(8,128)S(1)}, u32[]{:S(2)}, u32[]{:S(2)}) collective-permute-start(f32[9,8,128]{2,1,0:T(8,128)S(1)} %get-tuple-element.72), channel_id=1, source_target_pairs={{0,1},{1,0},{2,3},{3,2},{4,5},{5,4},{6,7},{7,6},{8,9},{9,8},{10,11... | collective-permute-start | bytes 110600 | tf_op jit(solution)/shard_map/ppermute | solution.py:448
  31.6 3.2 %render_first.1.image = f32[4,128,128]{2,1,0:T(8,128)S(1)} custom-call(s32[5]{0:T(128)S(1)} %stack.31.info, bf16[384,256]{1,0:T(8,128)(2,1)S(1)} %copy-done.1, f32[552,128]{1,0:T(8,128)S(1)} %get-tuple-element.67.refs_0_, f32[552,128]{1,0:T(8,128)S(1)} %collective-permute-done.2.refs_1_, f32[552,128]{1,0:T(8,128)S(1)} %collective-permute-done.4.refs_2_, ...), custom_call_target="tpu_custom_call" | custom-call | flops 1000 | bytes 1000 | tf_op jit(solution)/shard_map/render_first/pallas_call | solution.py:419
  34.7 1.4 %first_edges.1 = f32[536,128]{1,0:T(8,128)S(1)} custom-call(s32[5]{0:T(128)S(1)} %stack.31.info, f32[4,128,128]{2,1,0:T(8,128)S(1)} %render_first.1.image, f32[2,16,8,128]{3,2,1,0:T(8,128)S(1)} %get-tuple-element.71.mine, f32[9,8,128]{2,1,0:T(8,128)S(1)} %collective-permute-done.9.before.after, f32[9,8,128]{2,1,0:T(8,128)S(1)} %collective-permute-done.9.before.after), custom_call_target="tpu_custom_call" | custom-call | flops 1000 | bytes 1000 | tf_op jit(solution)/shard_map/first_edges/pallas_call | solution.py:419
  36.6 2.2 %collective-permute-done.8.refs_4_.boundary = f32[552,128]{1,0:T(8,128)S(1)} collective-permute-done((f32[552,128]{1,0:T(8,128)S(1)}, f32[552,128]{1,0:T(8,128)S(1)}, u32[]{:S(2)}, u32[]{:S(2)}) %collective-permute-start.8) | collective-permute-done | bytes 282656 | tf_op jit(solution)/shard_map/ppermute | solution.py:465
  38.8 5.9 %collective-permute-done.7.refs_3_ = f32[552,128]{1,0:T(8,128)S(1)} collective-permute-done((f32[552,128]{1,0:T(8,128)S(1)}, f32[552,128]{1,0:T(8,128)S(1)}, u32[]{:S(2)}, u32[]{:S(2)}) %collective-permute-start.7) | collective-permute-done | bytes 282656 | tf_op jit(solution)/shard_map/ppermute | solution.py:465
  44.7 1.1 %own_edges.1 = (f32[22,8,256]{2,1,0:T(8,128)S(1)}, f32[22,8,256]{2,1,0:T(8,128)S(1)}) custom-call(s32[5]{0:T(128)S(1)} %stack.31.info, f32[552,128]{1,0:T(8,128)S(1)} %get-tuple-element.73.refs_0_, f32[552,128]{1,0:T(8,128)S(1)} %collective-permute-done.3.refs_1_, f32[552,128]{1,0:T(8,128)S(1)} %collective-permute-done.5.refs_2_, ...), custom_call_target="tpu_custom_call" | custom-call | flops 1000 | bytes 1000 | tf_op jit(solution)/shard_map/own_edges/pallas_call | solution.py:419
  45.8 3.8 %render_last.1.image = f32[4,128,128]{2,1,0:T(8,128)S(1)} custom-call(s32[5]{0:T(128)S(1)} %stack.31.info, bf16[384,256]{1,0:T(8,128)(2,1)S(1)} %copy-done.1, f32[552,128]{1,0:T(8,128)S(1)} %get-tuple-element.73.refs_0_, f32[552,128]{1,0:T(8,128)S(1)} %collective-permute-done.3.refs_1_, f32[552,128]{1,0:T(8,128)S(1)} %collective-permute-done.5.refs_2_, ...), custom_call_target="tpu_custom_call" | custom-call | flops 1000000000 | bytes 1000 | tf_op jit(solution)/shard_map/render_last/pallas_call | solution.py:419
  49.9 2.3 %join_halves.1 = (f32[4,128,128]{2,1,0:T(8,128)}, f32[22,8,256]{2,1,0:T(8,128)S(1)}, f32[22,8,256]{2,1,0:T(8,128)S(1)}) custom-call(s32[5]{0:T(128)S(1)} %stack.31.info, f32[4,128,128]{2,1,0:T(8,128)S(1)} %render_last.1.image, f32[536,128]{1,0:T(8,128)S(1)} %collective-permute-done.10.other, ...), custom_call_target="tpu_custom_call", output_to_operand_aliasing={{1}: (4, {}), {2}: (5, {})} | custom-call | flops 1000 | bytes 1000 | tf_op jit(solution)/shard_map/join_halves/pallas_call | solution.py:419
  (14 shorter events, 2.2 us)
Async XLA Ops:
  0.0 4.5 %collective-permute-start = (f32[2,2048,128]{2,1,0:T(8,128)}, f32[2,2048,128]{2,1,0:T(8,128)S(1)}, u32[]{:S(2)}, u32[]{:S(2)}) collective-permute-start(f32[2,2048,128]{2,1,0:T(8,128)} %source.1), channel_id=1, source_target_pairs={{0,2},{2,0},{4,6},{6,4},{8,10},{10,8},{12,14},{14,12},{16,18},{18,... | collective-permute-start | bytes 6291464 | tf_op jit(solution)/shard_map/ppermute | solution.py:405
  0.5 1.6 %copy-start = (f32[2,2048,128]{2,1,0:T(8,128)S(1)}, f32[2,2048,128]{2,1,0:T(8,128)}, u32[]{:S(2)}) copy-start(f32[2,2048,128]{2,1,0:T(8,128)} %source.1) | copy-start | bytes 6291460
  5.1 10.2 %collective-permute-start.2 = (f32[552,128]{1,0:T(8,128)S(1)}, f32[552,128]{1,0:T(8,128)S(1)}, u32[]{:S(2)}, u32[]{:S(2)}) collective-permute-start(f32[552,128]{1,0:T(8,128)S(1)} %get-tuple-element.58), channel_id=1, source_target_pairs={{0,4},{2,6},{4,0},{6,2},{8,12},{10,14},{12,8},{14,10},{16,20},{18,... | collective-permute-start | bytes 847880 | tf_op jit(solution)/shard_map/ppermute | solution.py:465
  8.0 9.6 %collective-permute-start.4 = (f32[552,128]{1,0:T(8,128)S(1)}, f32[552,128]{1,0:T(8,128)S(1)}, u32[]{:S(2)}, u32[]{:S(2)}) collective-permute-start(f32[552,128]{1,0:T(8,128)S(1)} %get-tuple-element.61), channel_id=1, source_target_pairs={{0,8},{2,10},{4,12},{6,14},{8,0},{10,2},{12,4},{14,6},{16,24},{18,... | collective-permute-start | bytes 847880 | tf_op jit(solution)/shard_map/ppermute | solution.py:465
  9.6 13.6 %collective-permute-start.6 = (f32[552,128]{1,0:T(8,128)S(1)}, f32[552,128]{1,0:T(8,128)S(1)}, u32[]{:S(2)}, u32[]{:S(2)}) collective-permute-start(f32[552,128]{1,0:T(8,128)S(1)} %get-tuple-element.64), channel_id=1, source_target_pairs={{0,12},{2,14},{4,8},{6,10},{8,4},{10,6},{12,0},{14,2},{16,28},{18,... | collective-permute-start | bytes 847880 | tf_op jit(solution)/shard_map/ppermute | solution.py:465
  10.7 20.8 %copy-start.1 = (bf16[384,256]{1,0:T(8,128)(2,1)S(1)}, bf16[384,256]{1,0:T(8,128)(2,1)}, u32[]{:S(2)}) copy-start(bf16[384,256]{1,0:T(8,128)(2,1)} %constant.55.clone.weights) | copy-start | bytes 589828
  10.7 4.0 %collective-permute-start.1 = (f32[9,8,128]{2,1,0:T(8,128)S(1)}, f32[9,8,128]{2,1,0:T(8,128)S(1)}, u32[]{:S(2)}, u32[]{:S(2)}) collective-permute-start(f32[9,8,128]{2,1,0:T(8,128)S(1)} %get-tuple-element.55), channel_id=1, source_target_pairs={{0,1},{1,0},{2,3},{3,2},{4,5},{5,4},{6,7},{7,6},{8,9},{9,8},{10,11... | collective-permute-start | bytes 110600 | tf_op jit(solution)/shard_map/ppermute | solution.py:448
  15.3 21.3 %collective-permute-start.3 = (f32[552,128]{1,0:T(8,128)S(1)}, f32[552,128]{1,0:T(8,128)S(1)}, u32[]{:S(2)}, u32[]{:S(2)}) collective-permute-start(f32[552,128]{1,0:T(8,128)S(1)} %get-tuple-element.59), channel_id=1, source_target_pairs={{0,4},{2,6},{4,0},{6,2},{8,12},{10,14},{12,8},{14,10},{16,20},{18,... | collective-permute-start | bytes 847880 | tf_op jit(solution)/shard_map/ppermute | solution.py:465
  17.7 18.9 %collective-permute-start.5 = (f32[552,128]{1,0:T(8,128)S(1)}, f32[552,128]{1,0:T(8,128)S(1)}, u32[]{:S(2)}, u32[]{:S(2)}) collective-permute-start(f32[552,128]{1,0:T(8,128)S(1)} %get-tuple-element.62), channel_id=1, source_target_pairs={{0,8},{2,10},{4,12},{6,14},{8,0},{10,2},{12,4},{14,6},{16,24},{18,... | collective-permute-start | bytes 847880 | tf_op jit(solution)/shard_map/ppermute | solution.py:465
  23.8 15.0 %collective-permute-start.8 = (f32[552,128]{1,0:T(8,128)S(1)}, f32[552,128]{1,0:T(8,128)S(1)}, u32[]{:S(2)}, u32[]{:S(2)}) collective-permute-start(f32[552,128]{1,0:T(8,128)S(1)} %pick_boundary.1), channel_id=1, source_target_pairs={{0,16},{2,18},{4,20},{6,22},{8,24},{10,26},{12,28},{14,30},{16,0},... | collective-permute-start | bytes 847880 | tf_op jit(solution)/shard_map/ppermute | solution.py:465
  26.9 17.7 %collective-permute-start.7 = (f32[552,128]{1,0:T(8,128)S(1)}, f32[552,128]{1,0:T(8,128)S(1)}, u32[]{:S(2)}, u32[]{:S(2)}) collective-permute-start(f32[552,128]{1,0:T(8,128)S(1)} %get-tuple-element.65), channel_id=1, source_target_pairs={{0,12},{2,14},{4,8},{6,10},{8,4},{10,6},{12,0},{14,2},{16,28},{18,... | collective-permute-start | bytes 847880 | tf_op jit(solution)/shard_map/ppermute | solution.py:465
  30.0 4.7 %collective-permute-start.9 = (f32[9,8,128]{2,1,0:T(8,128)S(1)}, f32[9,8,128]{2,1,0:T(8,128)S(1)}, u32[]{:S(2)}, u32[]{:S(2)}) collective-permute-start(f32[9,8,128]{2,1,0:T(8,128)S(1)} %get-tuple-element.72), channel_id=1, source_target_pairs={{0,1},{1,0},{2,3},{3,2},{4,5},{5,4},{6,7},{7,6},{8,9},{9,8},{10,11... | collective-permute-start | bytes 110600 | tf_op jit(solution)/shard_map/ppermute | solution.py:448
  36.2 13.7 %collective-permute-start.10 = (f32[536,128]{1,0:T(8,128)S(1)}, f32[536,128]{1,0:T(8,128)S(1)}, u32[]{:S(2)}, u32[]{:S(2)}) collective-permute-start(f32[536,128]{1,0:T(8,128)S(1)} %first_edges.1), channel_id=1, source_target_pairs={{0,16},{2,18},{4,20},{6,22},{8,24},{10,26},{12,28},{14,30},{16,0},... | collective-permute-start | bytes 823304 | tf_op jit(solution)/shard_map/ppermute | solution.py:465

commit v10 on v9

--- a/solution.py
+++ b/solution.py
@@ -311,7 +311,7 @@
     filter_edges(own, mine, tiles, depth, slots[:-4], sx, dx)
 
 
-def join_kernel(size, depth, info, image, other, boundary, sx_own, dx_own, picture, sx, dx, mine):
+def join_kernel(size, depth, info, image, other, boundary, sx_own, dx_own, picture, sx, dx, mine, drawn, sems):
     own = image.shape[1]
     edge_columns([boundary], depth, own, mine)
     filter_edges(own, mine, [block_tiles(other, depth)], depth, plane_slots(size, depth, True, info)[0][-4:], sx, dx)
@@ -321,10 +321,14 @@
     ahead = tuple(jnp.where(is_front, m, o) for m, o in zip(mine, other))
     behind = tuple(jnp.where(is_front, o, m) for m, o in zip(mine, other))
     v_sum, vt_sum, vu_sum, cover = over(ahead, behind)
-    picture[0] = 0.5 * (v_sum + vu_sum)
-    picture[1] = 0.5 * v_sum + 0.4 * vt_sum
-    picture[2] = 0.5 * (v_sum - vt_sum)
-    picture[3] = cover
+    colours = (0.5 * (v_sum + vu_sum), 0.5 * v_sum + 0.4 * vt_sum, 0.5 * (v_sum - vt_sum), cover)
+    copies = []
+    for channel, values in enumerate(colours):
+        drawn[channel] = values
+        copies.append(pltpu.make_async_copy(drawn.at[channel], picture.at[channel], sems.at[channel]))
+        copies[-1].start()
+    for copy in copies:
+        copy.wait()
 
 
 def rows_around(field, plane, target, own):
@@ -415,12 +419,12 @@
             name="pack_shared" if source is shared else "pack_own",
         )(info, source, *blocks)
 
-    def call(kernel, name, out_shape, *args, **more):
+    def call(kernel, name, out_shape, *args, specs=None, **more):
         return pl.pallas_call(
             kernel,
             out_shape=out_shape,
             in_specs=[SMEM] + [VMEM] * (len(args) - 1),
-            out_specs=jax.tree.map(lambda _: VMEM, out_shape),
+            out_specs=specs or jax.tree.map(lambda _: VMEM, out_shape),
             compiler_params=PARAMS,
             cost_estimate=cost(1_000_000_000 if name == "render_last" else 1000, 1000),
             name=name,
@@ -514,7 +518,12 @@
         image_part,
         parts[-1],
         *filtered,
-        scratch_shapes=[pltpu.VMEM((2, LANES // 8, 8, LANES), f32)],
+        specs=(pl.BlockSpec(memory_space=pl.ANY), VMEM, VMEM),
+        scratch_shapes=[
+            pltpu.VMEM((2, LANES // 8, 8, LANES), f32),
+            pltpu.VMEM(image.shape, f32),
+            pltpu.SemaphoreType.DMA((4,)),
+        ],
         input_output_aliases={4: 1, 5: 2},
     )[0]
 

time: 52.3 us -> 52.3 us (level)
  no operation moved by 1% of the time
where the time goes in v10:
time: 52.3 us; the launch traced here: 52.2 us
  starting transfers between devices  18 us (34%)
  waiting for transfers between devices  16.5 us (32%)
  Pallas kernels  15.9 us (30%)
  local copies, waits for them, and re-layouts  1.68 us (3%)
    ppermute x8, starting transfers between devices, swap(): return lax.ppermute(x, 'depth', [(i, i ^ bits) for i in range(groups)])  14.1 us
    pallas_call x7, Pallas kernels, call(): pl.pallas_call(kernel, out_shape=out_shape, in_specs=[SMEM] + [VMEM] * (l...  13.1 us
    ppermute x8, waiting for transfers between devices, swap(): return lax.ppermute(x, 'depth', [(i, i ^ bits) for i in range(groups)])  12.8 us
    ppermute x2, starting transfers between devices, edges_of(): return (edges,) + (lax.ppermute(sent, 'cols', [(0, 1), (1, 0)]),) * 2  3.44 us
    ppermute x2, waiting for transfers between devices, edges_of(): return (edges,) + (lax.ppermute(sent, 'cols', [(0, 1), (1, 0)]),) * 2  2.08 us
    ppermute x1, waiting for transfers between devices, local(): shared = lax.ppermute(field, 'depth', [(i, i ^ 1) for i in range(groups)])  1.68 us
    pallas_call x2, Pallas kernels, edges_of(): pl.pallas_call(kernel, out_shape=shapes, in_specs=[VMEM] * len(parts), ou...  1.61 us
    unnamed x4, local copies, waits for them, and re-layouts  1.59 us
  transfers between devices with their start and end apart: 11, of which 7 were waited for; matrix products, arithmetic and copies ran while one was open for 0% of the time, Pallas kernels for 25%

profile of v10, /device:TPU:0, one launch (start us, length us, event | category | flops | bytes accessed | tf_op | source)
XLA Modules:
  0.0 52.2 jit_solution(17485371628903735853)
XLA Ops:
  0.5 1.6 %copy-done = f32[2,2048,128]{2,1,0:T(8,128)S(1)} copy-done((f32[2,2048,128]{2,1,0:T(8,128)S(1)}, f32[2,2048,128]{2,1,0:T(8,128)}, u32[]{:S(2)}) %copy-start) | copy-done | bytes 2097176
  2.1 0.6 %pack_own.1 = (f32[552,128]{1,0:T(8,128)S(1)}, f32[552,128]{1,0:T(8,128)S(1)}, f32[552,128]{1,0:T(8,128)S(1)}, f32[552,128]{1,0:T(8,128)S(1)}, f32[552,128]{1,0:...) custom-call(s32[5]{0:T(128)S(1)} %stack.31.info, f32[2,2048,128]{2,1,0:T(8,128)S(1)} %copy-done), custom_call_target="tpu_custom_call" | custom-call | tf_op jit(solution)/shard_map/pack_own/pallas_call | solution.py:412
  2.8 1.7 %collective-permute-done.source = f32[2,2048,128]{2,1,0:T(8,128)S(1)} collective-permute-done((f32[2,2048,128]{2,1,0:T(8,128)}, f32[2,2048,128]{2,1,0:T(8,128)S(1)}, u32[]{:S(2)}, u32[]{:S(2)}) %collective-permute-start) | collective-permute-done | bytes 2097184 | tf_op jit(solution)/shard_map/ppermute | solution.py:409
  4.5 0.6 %pack_shared.1 = (f32[552,128]{1,0:T(8,128)S(1)}, f32[552,128]{1,0:T(8,128)S(1)}, f32[552,128]{1,0:T(8,128)S(1)}, f32[552,128]{1,0:T(8,128)S(1)}, f32[552,128]{1...) custom-call(s32[5]{0:T(128)S(1)} %stack.31.info, ...), custom_call_target="tpu_custom_call", output_to_operand_aliasing={{0}: (2, {}), {1}: (3, {}), {2}: (4, {}), {3}: (5, {}), {4}... | custom-call | tf_op jit(solution)/shard_map/pack_shared/pallas_call | solution.py:412
  5.1 3.0 %collective-permute-start.2 = (f32[552,128]{1,0:T(8,128)S(1)}, f32[552,128]{1,0:T(8,128)S(1)}, u32[]{:S(2)}, u32[]{:S(2)}) collective-permute-start(f32[552,128]{1,0:T(8,128)S(1)} %get-tuple-element.58), channel_id=1, source_target_pairs={{0,4},{2,6},{4,0},{6,2},{8,12},{10,14},{12,8},{14,10},{16,20},{18,... | collective-permute-start | bytes 847880 | tf_op jit(solution)/shard_map/ppermute | solution.py:469
  8.0 1.6 %collective-permute-start.4 = (f32[552,128]{1,0:T(8,128)S(1)}, f32[552,128]{1,0:T(8,128)S(1)}, u32[]{:S(2)}, u32[]{:S(2)}) collective-permute-start(f32[552,128]{1,0:T(8,128)S(1)} %get-tuple-element.61), channel_id=1, source_target_pairs={{0,8},{2,10},{4,12},{6,14},{8,0},{10,2},{12,4},{14,6},{16,24},{18,... | collective-permute-start | bytes 847880 | tf_op jit(solution)/shard_map/ppermute | solution.py:469
  9.6 1.1 %edge_columns.2 = (f32[2,16,8,128]{3,2,1,0:T(8,128)}, f32[9,8,128]{2,1,0:T(8,128)S(1)}) custom-call(f32[552,128]{1,0:T(8,128)S(1)} %get-tuple-element.51.refs_0_, f32[552,128]{1,0:T(8,128)S(1)} %get-tuple-element.52.refs_1_, f32[552,128]{1,0:T(8,128)S(1)} %get-tuple-element.53.refs_2_, f32[552,128]{1,0:T(8,128)S(1)} %get-tuple-element.54.refs_3_), custom_call_target="tpu_custom_call" | custom-call | flops 1000 | bytes 1000 | tf_op jit(solution)/shard_map/edge_columns/pallas_call | solution.py:442
  10.7 1.9 %collective-permute-start.1 = (f32[9,8,128]{2,1,0:T(8,128)S(1)}, f32[9,8,128]{2,1,0:T(8,128)S(1)}, u32[]{:S(2)}, u32[]{:S(2)}) collective-permute-start(f32[9,8,128]{2,1,0:T(8,128)S(1)} %get-tuple-element.55), channel_id=1, source_target_pairs={{0,1},{1,0},{2,3},{3,2},{4,5},{5,4},{6,7},{7,6},{8,9},{9,8},{10,11... | collective-permute-start | bytes 110600 | tf_op jit(solution)/shard_map/ppermute | solution.py:452
  12.6 2.1 %collective-permute-done.1.before.after = f32[9,8,128]{2,1,0:T(8,128)S(1)} collective-permute-done((f32[9,8,128]{2,1,0:T(8,128)S(1)}, f32[9,8,128]{2,1,0:T(8,128)S(1)}, u32[]{:S(2)}, u32[]{:S(2)}) %collective-permute-start.1) | collective-permute-done | bytes 36896 | tf_op jit(solution)/shard_map/ppermute | solution.py:452
  14.7 0.6 %lay_columns.1 = (f32[552,128]{1,0:T(8,128)S(1)}, f32[552,128]{1,0:T(8,128)S(1)}, f32[552,128]{1,0:T(8,128)S(1)}, f32[552,128]{1,0:T(8,128)S(1)}) custom-call(s32[5]{0:T(128)S(1)} %stack.31.info, f32[9,8,128]{2,1,0:T(8,128)S(1)} %collective-permute-done.1.before.after, ...), custom_call_target="tpu_custom_call", output_to_operand_aliasing={{0}: (3, {}), {1}: (4, {}), {2}: (5, {}), {3}: (6, {})} | custom-call | flops 1000 | bytes 1000 | tf_op jit(solution)/shard_map/lay_columns/pallas_call | solution.py:423
  15.3 1.9 %collective-permute-start.3 = (f32[552,128]{1,0:T(8,128)S(1)}, f32[552,128]{1,0:T(8,128)S(1)}, u32[]{:S(2)}, u32[]{:S(2)}) collective-permute-start(f32[552,128]{1,0:T(8,128)S(1)} %get-tuple-element.59), channel_id=1, source_target_pairs={{0,4},{2,6},{4,0},{6,2},{8,12},{10,14},{12,8},{14,10},{16,20},{18,... | collective-permute-start | bytes 847880 | tf_op jit(solution)/shard_map/ppermute | solution.py:469
  17.7 1.6 %collective-permute-start.5 = (f32[552,128]{1,0:T(8,128)S(1)}, f32[552,128]{1,0:T(8,128)S(1)}, u32[]{:S(2)}, u32[]{:S(2)}) collective-permute-start(f32[552,128]{1,0:T(8,128)S(1)} %get-tuple-element.62), channel_id=1, source_target_pairs={{0,8},{2,10},{4,12},{6,14},{8,0},{10,2},{12,4},{14,6},{16,24},{18,... | collective-permute-start | bytes 847880 | tf_op jit(solution)/shard_map/ppermute | solution.py:469
  19.2 4.0 %collective-permute-done.6.refs_3_ = f32[552,128]{1,0:T(8,128)S(1)} collective-permute-done((f32[552,128]{1,0:T(8,128)S(1)}, f32[552,128]{1,0:T(8,128)S(1)}, u32[]{:S(2)}, u32[]{:S(2)}) %collective-permute-start.6) | collective-permute-done | bytes 282656 | tf_op jit(solution)/shard_map/ppermute | solution.py:469
  23.2 0.6 %pick_boundary.1 = f32[552,128]{1,0:T(8,128)S(1)} custom-call(s32[5]{0:T(128)S(1)} %stack.31.info, f32[552,128]{1,0:T(8,128)S(1)} %get-tuple-element.67.refs_0_, f32[552,128]{1,0:T(8,128)S(1)} %collective-permute-done.2.refs_1_, f32[552,128]{1,0:T(8,128)S(1)} %collective-permute-done.4.refs_2_, f32[552,128]{1,0:T(8,128)S(1)} %collective-permute-done.6.refs_3_), custom_call_target="tpu_custom_call" | custom-call | flops 1000 | bytes 1000 | tf_op jit(solution)/shard_map/pick_boundary/pallas_call | solution.py:423
  23.8 3.1 %collective-permute-start.8 = (f32[552,128]{1,0:T(8,128)S(1)}, f32[552,128]{1,0:T(8,128)S(1)}, u32[]{:S(2)}, u32[]{:S(2)}) collective-permute-start(f32[552,128]{1,0:T(8,128)S(1)} %pick_boundary.1), channel_id=1, source_target_pairs={{0,16},{2,18},{4,20},{6,22},{8,24},{10,26},{12,28},{14,30},{16,0},... | collective-permute-start | bytes 847880 | tf_op jit(solution)/shard_map/ppermute | solution.py:469
  26.9 2.5 %collective-permute-start.7 = (f32[552,128]{1,0:T(8,128)S(1)}, f32[552,128]{1,0:T(8,128)S(1)}, u32[]{:S(2)}, u32[]{:S(2)}) collective-permute-start(f32[552,128]{1,0:T(8,128)S(1)} %get-tuple-element.65), channel_id=1, source_target_pairs={{0,12},{2,14},{4,8},{6,10},{8,4},{10,6},{12,0},{14,2},{16,28},{18,... | collective-permute-start | bytes 847880 | tf_op jit(solution)/shard_map/ppermute | solution.py:469
  30.0 1.6 %collective-permute-start.9 = (f32[9,8,128]{2,1,0:T(8,128)S(1)}, f32[9,8,128]{2,1,0:T(8,128)S(1)}, u32[]{:S(2)}, u32[]{:S(2)}) collective-permute-start(f32[9,8,128]{2,1,0:T(8,128)S(1)} %get-tuple-element.72), channel_id=1, source_target_pairs={{0,1},{1,0},{2,3},{3,2},{4,5},{5,4},{6,7},{7,6},{8,9},{9,8},{10,11... | collective-permute-start | bytes 110600 | tf_op jit(solution)/shard_map/ppermute | solution.py:452
  31.6 3.2 %render_first.1.image = f32[4,128,128]{2,1,0:T(8,128)S(1)} custom-call(s32[5]{0:T(128)S(1)} %stack.31.info, bf16[384,256]{1,0:T(8,128)(2,1)S(1)} %copy-done.1, f32[552,128]{1,0:T(8,128)S(1)} %get-tuple-element.67.refs_0_, f32[552,128]{1,0:T(8,128)S(1)} %collective-permute-done.2.refs_1_, f32[552,128]{1,0:T(8,128)S(1)} %collective-permute-done.4.refs_2_, ...), custom_call_target="tpu_custom_call" | custom-call | flops 1000 | bytes 1000 | tf_op jit(solution)/shard_map/render_first/pallas_call | solution.py:423
  34.7 1.4 %first_edges.1 = f32[536,128]{1,0:T(8,128)S(1)} custom-call(s32[5]{0:T(128)S(1)} %stack.31.info, f32[4,128,128]{2,1,0:T(8,128)S(1)} %render_first.1.image, f32[2,16,8,128]{3,2,1,0:T(8,128)S(1)} %get-tuple-element.71.mine, f32[9,8,128]{2,1,0:T(8,128)S(1)} %collective-permute-done.9.before.after, f32[9,8,128]{2,1,0:T(8,128)S(1)} %collective-permute-done.9.before.after), custom_call_target="tpu_custom_call" | custom-call | flops 1000 | bytes 1000 | tf_op jit(solution)/shard_map/first_edges/pallas_call | solution.py:423
  36.6 2.2 %collective-permute-done.8.refs_4_.boundary = f32[552,128]{1,0:T(8,128)S(1)} collective-permute-done((f32[552,128]{1,0:T(8,128)S(1)}, f32[552,128]{1,0:T(8,128)S(1)}, u32[]{:S(2)}, u32[]{:S(2)}) %collective-permute-start.8) | collective-permute-done | bytes 282656 | tf_op jit(solution)/shard_map/ppermute | solution.py:469
  38.8 5.9 %collective-permute-done.7.refs_3_ = f32[552,128]{1,0:T(8,128)S(1)} collective-permute-done((f32[552,128]{1,0:T(8,128)S(1)}, f32[552,128]{1,0:T(8,128)S(1)}, u32[]{:S(2)}, u32[]{:S(2)}) %collective-permute-start.7) | collective-permute-done | bytes 282656 | tf_op jit(solution)/shard_map/ppermute | solution.py:469
  44.7 1.1 %own_edges.1 = (f32[22,8,256]{2,1,0:T(8,128)S(1)}, f32[22,8,256]{2,1,0:T(8,128)S(1)}) custom-call(s32[5]{0:T(128)S(1)} %stack.31.info, f32[552,128]{1,0:T(8,128)S(1)} %get-tuple-element.73.refs_0_, f32[552,128]{1,0:T(8,128)S(1)} %collective-permute-done.3.refs_1_, f32[552,128]{1,0:T(8,128)S(1)} %collective-permute-done.5.refs_2_, ...), custom_call_target="tpu_custom_call" | custom-call | flops 1000 | bytes 1000 | tf_op jit(solution)/shard_map/own_edges/pallas_call | solution.py:423
  45.8 3.8 %render_last.1.image = f32[4,128,128]{2,1,0:T(8,128)S(1)} custom-call(s32[5]{0:T(128)S(1)} %stack.31.info, bf16[384,256]{1,0:T(8,128)(2,1)S(1)} %copy-done.1, f32[552,128]{1,0:T(8,128)S(1)} %get-tuple-element.73.refs_0_, f32[552,128]{1,0:T(8,128)S(1)} %collective-permute-done.3.refs_1_, f32[552,128]{1,0:T(8,128)S(1)} %collective-permute-done.5.refs_2_, ...), custom_call_target="tpu_custom_call" | custom-call | flops 1000000000 | bytes 1000 | tf_op jit(solution)/shard_map/render_last/pallas_call | solution.py:423
  49.9 2.3 %join_halves.1 = (f32[4,128,128]{2,1,0:T(8,128)}, f32[22,8,256]{2,1,0:T(8,128)S(1)}, f32[22,8,256]{2,1,0:T(8,128)S(1)}) custom-call(s32[5]{0:T(128)S(1)} %stack.31.info, f32[4,128,128]{2,1,0:T(8,128)S(1)} %render_last.1.image, f32[536,128]{1,0:T(8,128)S(1)} %collective-permute-done.10.other, ...), custom_call_target="tpu_custom_call", output_to_operand_aliasing={{1}: (4, {}), {2}: (5, {})} | custom-call | flops 1000 | bytes 1000 | tf_op jit(solution)/shard_map/join_halves/pallas_call | solution.py:423
  (14 shorter events, 2.2 us)
Async XLA Ops:
  0.0 4.5 %collective-permute-start = (f32[2,2048,128]{2,1,0:T(8,128)}, f32[2,2048,128]{2,1,0:T(8,128)S(1)}, u32[]{:S(2)}, u32[]{:S(2)}) collective-permute-start(f32[2,2048,128]{2,1,0:T(8,128)} %source.1), channel_id=1, source_target_pairs={{0,2},{2,0},{4,6},{6,4},{8,10},{10,8},{12,14},{14,12},{16,18},{18,... | collective-permute-start | bytes 6291464 | tf_op jit(solution)/shard_map/ppermute | solution.py:409
  0.5 1.6 %copy-start = (f32[2,2048,128]{2,1,0:T(8,128)S(1)}, f32[2,2048,128]{2,1,0:T(8,128)}, u32[]{:S(2)}) copy-start(f32[2,2048,128]{2,1,0:T(8,128)} %source.1) | copy-start | bytes 6291460
  5.1 10.2 %collective-permute-start.2 = (f32[552,128]{1,0:T(8,128)S(1)}, f32[552,128]{1,0:T(8,128)S(1)}, u32[]{:S(2)}, u32[]{:S(2)}) collective-permute-start(f32[552,128]{1,0:T(8,128)S(1)} %get-tuple-element.58), channel_id=1, source_target_pairs={{0,4},{2,6},{4,0},{6,2},{8,12},{10,14},{12,8},{14,10},{16,20},{18,... | collective-permute-start | bytes 847880 | tf_op jit(solution)/shard_map/ppermute | solution.py:469
  8.0 9.6 %collective-permute-start.4 = (f32[552,128]{1,0:T(8,128)S(1)}, f32[552,128]{1,0:T(8,128)S(1)}, u32[]{:S(2)}, u32[]{:S(2)}) collective-permute-start(f32[552,128]{1,0:T(8,128)S(1)} %get-tuple-element.61), channel_id=1, source_target_pairs={{0,8},{2,10},{4,12},{6,14},{8,0},{10,2},{12,4},{14,6},{16,24},{18,... | collective-permute-start | bytes 847880 | tf_op jit(solution)/shard_map/ppermute | solution.py:469
  9.6 13.6 %collective-permute-start.6 = (f32[552,128]{1,0:T(8,128)S(1)}, f32[552,128]{1,0:T(8,128)S(1)}, u32[]{:S(2)}, u32[]{:S(2)}) collective-permute-start(f32[552,128]{1,0:T(8,128)S(1)} %get-tuple-element.64), channel_id=1, source_target_pairs={{0,12},{2,14},{4,8},{6,10},{8,4},{10,6},{12,0},{14,2},{16,28},{18,... | collective-permute-start | bytes 847880 | tf_op jit(solution)/shard_map/ppermute | solution.py:469
  10.7 20.8 %copy-start.1 = (bf16[384,256]{1,0:T(8,128)(2,1)S(1)}, bf16[384,256]{1,0:T(8,128)(2,1)}, u32[]{:S(2)}) copy-start(bf16[384,256]{1,0:T(8,128)(2,1)} %constant.55.clone.weights) | copy-start | bytes 589828
  10.7 4.0 %collective-permute-start.1 = (f32[9,8,128]{2,1,0:T(8,128)S(1)}, f32[9,8,128]{2,1,0:T(8,128)S(1)}, u32[]{:S(2)}, u32[]{:S(2)}) collective-permute-start(f32[9,8,128]{2,1,0:T(8,128)S(1)} %get-tuple-element.55), channel_id=1, source_target_pairs={{0,1},{1,0},{2,3},{3,2},{4,5},{5,4},{6,7},{7,6},{8,9},{9,8},{10,11... | collective-permute-start | bytes 110600 | tf_op jit(solution)/shard_map/ppermute | solution.py:452
  15.3 21.3 %collective-permute-start.3 = (f32[552,128]{1,0:T(8,128)S(1)}, f32[552,128]{1,0:T(8,128)S(1)}, u32[]{:S(2)}, u32[]{:S(2)}) collective-permute-start(f32[552,128]{1,0:T(8,128)S(1)} %get-tuple-element.59), channel_id=1, source_target_pairs={{0,4},{2,6},{4,0},{6,2},{8,12},{10,14},{12,8},{14,10},{16,20},{18,... | collective-permute-start | bytes 847880 | tf_op jit(solution)/shard_map/ppermute | solution.py:469
  17.7 18.9 %collective-permute-start.5 = (f32[552,128]{1,0:T(8,128)S(1)}, f32[552,128]{1,0:T(8,128)S(1)}, u32[]{:S(2)}, u32[]{:S(2)}) collective-permute-start(f32[552,128]{1,0:T(8,128)S(1)} %get-tuple-element.62), channel_id=1, source_target_pairs={{0,8},{2,10},{4,12},{6,14},{8,0},{10,2},{12,4},{14,6},{16,24},{18,... | collective-permute-start | bytes 847880 | tf_op jit(solution)/shard_map/ppermute | solution.py:469
  23.8 15.0 %collective-permute-start.8 = (f32[552,128]{1,0:T(8,128)S(1)}, f32[552,128]{1,0:T(8,128)S(1)}, u32[]{:S(2)}, u32[]{:S(2)}) collective-permute-start(f32[552,128]{1,0:T(8,128)S(1)} %pick_boundary.1), channel_id=1, source_target_pairs={{0,16},{2,18},{4,20},{6,22},{8,24},{10,26},{12,28},{14,30},{16,0},... | collective-permute-start | bytes 847880 | tf_op jit(solution)/shard_map/ppermute | solution.py:469
  26.9 17.7 %collective-permute-start.7 = (f32[552,128]{1,0:T(8,128)S(1)}, f32[552,128]{1,0:T(8,128)S(1)}, u32[]{:S(2)}, u32[]{:S(2)}) collective-permute-start(f32[552,128]{1,0:T(8,128)S(1)} %get-tuple-element.65), channel_id=1, source_target_pairs={{0,12},{2,14},{4,8},{6,10},{8,4},{10,6},{12,0},{14,2},{16,28},{18,... | collective-permute-start | bytes 847880 | tf_op jit(solution)/shard_map/ppermute | solution.py:469
  30.0 4.7 %collective-permute-start.9 = (f32[9,8,128]{2,1,0:T(8,128)S(1)}, f32[9,8,128]{2,1,0:T(8,128)S(1)}, u32[]{:S(2)}, u32[]{:S(2)}) collective-permute-start(f32[9,8,128]{2,1,0:T(8,128)S(1)} %get-tuple-element.72), channel_id=1, source_target_pairs={{0,1},{1,0},{2,3},{3,2},{4,5},{5,4},{6,7},{7,6},{8,9},{9,8},{10,11... | collective-permute-start | bytes 110600 | tf_op jit(solution)/shard_map/ppermute | solution.py:452
  36.2 13.7 %collective-permute-start.10 = (f32[536,128]{1,0:T(8,128)S(1)}, f32[536,128]{1,0:T(8,128)S(1)}, u32[]{:S(2)}, u32[]{:S(2)}) collective-permute-start(f32[536,128]{1,0:T(8,128)S(1)} %first_edges.1), channel_id=1, source_target_pairs={{0,16},{2,18},{4,20},{6,22},{8,24},{10,26},{12,28},{14,30},{16,0},... | collective-permute-start | bytes 823304 | tf_op jit(solution)/shard_map/ppermute | solution.py:469
